TPU v7x, 32 devices: a whole 2x2x4 slice. The times are simulated.
32 devices in a mesh: ctx: 8 (over z, x), fsdp: 4 (over y, core).
Axes of the slice: x: 2, y: 2, z: 4, core: 2. Of those that a mesh axis runs over, the one named last changes fastest.
Arguments:
- tokens: bfloat16 [4096, 640], P(('ctx', 'fsdp')), may hold values from -6 to 6
- cotangent: bfloat16 [4096, 640], P(('ctx', 'fsdp')), may hold values from -6 to 6
- block_order: int32 [16], replicated, may hold values from 0 to 15, as said below
- query_weight: bfloat16 [640, 1024], P('fsdp'), may hold values from -0.25 to 0.25
- key_weight: bfloat16 [640, 256], P('fsdp'), may hold values from -0.25 to 0.25
- value_weight: bfloat16 [640, 256], P('fsdp'), may hold values from -0.25 to 0.25
- out_weight: bfloat16 [1024, 640], P('fsdp'), may hold values from -0.1875 to 0.1875
- gate_weight: bfloat16 [640, 2048], P(None, 'fsdp'), may hold values from -0.25 to 0.25
- up_weight: bfloat16 [640, 2048], P(None, 'fsdp'), may hold values from -0.25 to 0.25
- down_weight: bfloat16 [2048, 640], P('fsdp'), may hold values from -0.125 to 0.125
- norm_gains: bfloat16 [4, 640], P(None, 'fsdp'), may hold values from 0.5 to 1.5
- head_gains: bfloat16 [2, 256], P(None, 'fsdp'), may hold values from 0.5 to 1.5
Outputs:
- output: bfloat16 [4096, 640], P(('ctx', 'fsdp'))
- input_grad: float32 [4096, 640], P(('ctx', 'fsdp'))
- grad_query_weight: float32 [640, 1024], P('fsdp')
- grad_key_weight: float32 [640, 256], P('fsdp')
- grad_value_weight: float32 [640, 256], P('fsdp')
- grad_out_weight: float32 [1024, 640], P('fsdp')
- grad_gate_weight: float32 [640, 2048], P(None, 'fsdp')
- grad_up_weight: float32 [640, 2048], P(None, 'fsdp')
- grad_down_weight: float32 [2048, 640], P('fsdp')
- grad_norm_gains: float32 [4, 640], P(None, 'fsdp')
- grad_head_gains: float32 [2, 256], P(None, 'fsdp')
Inputs may be any that keep to these rules, and one draw needn't show every extreme that they name: block_order is a permutation in which entries 2c and 2c + 1 sum to 15 for every c.
All inputs are finite; a program needn't handle non-finite values.
Results may differ from a plain program's by a relative error of at most 0.019.
Values may be sent and summed in bfloat16 or wider, within the bound.
No kernel may reach another device: no remote copies, remote signals or barrier semaphores. Data moves between devices by JAX's collectives and lax.ppermute only.
A program may use at most 128 MiB of HBM per device.

v0:
```python
import math

import jax
import jax.numpy as jnp
from jax import lax
from jax.sharding import PartitionSpec as P

HEADS = 4
HEAD_DIM = 256


NORM_EPS = 1e-06
ROPE_BASE = 1000000.0


def norm_scale(values, scales):
    return values * lax.rsqrt(jnp.mean(values * values, axis=-1, keepdims=True) + NORM_EPS) * scales


def rotate(values, cosine, sine_table):
    half_size = values.shape[-1] // 2
    first_half = values[..., :half_size]
    second_half = values[..., half_size:]
    return jnp.concatenate(
        [
            first_half * cosine - second_half * sine_table,
            second_half * cosine + first_half * sine_table,
        ],
        axis=-1,
    )


def rope_tables(positions, head_size):
    freq_index = jnp.arange(head_size // 2, dtype=jnp.float32)
    inv_freq = ROPE_BASE ** (-2.0 * freq_index / head_size)
    angles = positions.astype(jnp.float32)[:, None] * inv_freq[None, :]
    return (jnp.cos(angles), jnp.sin(angles))


def row_positions(block_order, start_row, piece_rows, block_len):
    rows = start_row + jnp.arange(piece_rows, dtype=jnp.int32)
    return jnp.take(block_order, rows // block_len) * block_len + rows % block_len


def keep_state(current):
    return current


def shards(
    tokens,
    cotangent,
    block_order,
    query_weight,
    key_weight,
    value_weight,
    out_weight,
    gate_weight,
    up_weight,
    down_weight,
    norm_gains,
    head_gains,
):
    tok_rows = tokens.shape[0]
    block_len = tok_rows // 2
    head_count = HEADS
    head_size = HEAD_DIM
    proj_width = head_count * head_size
    score_scale = 1.0 / math.sqrt(head_size)
    my_index = lax.axis_index("ctx")
    positions = row_positions(block_order, my_index * tok_rows, tok_rows, block_len)
    cosine, sine_table = rope_tables(positions, head_size)

    def to_parts(head_rows):
        return jnp.transpose(
            head_rows.reshape(head_count, 2, block_len, head_size), (1, 0, 2, 3)
        ).reshape(2, head_count * block_len, head_size)

    def from_parts(part_rows):
        return jnp.transpose(
            part_rows.reshape(2, head_count, block_len, head_size), (1, 0, 2, 3)
        ).reshape(head_count, tok_rows, head_size)

    full_query, full_key, full_value, full_out, gains_low, head_low = (
        lax.all_gather(query_weight, "fsdp", axis=0, tiled=True),
        lax.all_gather(key_weight, "fsdp", axis=0, tiled=True),
        lax.all_gather(value_weight, "fsdp", axis=0, tiled=True),
        lax.all_gather(out_weight, "fsdp", axis=0, tiled=True),
        lax.all_gather(norm_gains, "fsdp", axis=1, tiled=True),
        lax.all_gather(head_gains, "fsdp", axis=1, tiled=True),
    )
    gains = gains_low.astype(jnp.float32)
    head_gain = head_low.astype(jnp.float32)
    score_bound = (
        math.sqrt(head_size) * jnp.max(jnp.abs(head_gain[0])) * jnp.max(jnp.abs(head_gain[1]))
    )
    source = tokens.astype(jnp.float32)
    normed, pull_input = jax.vjp(norm_scale, source, gains[0])
    normed_low = normed.astype(jnp.bfloat16)
    joined = jnp.concatenate([full_query, full_key, full_value], axis=1)
    projected = jnp.dot(normed_low, joined, preferred_element_type=jnp.float32)
    query_raw = projected[:, :proj_width]
    key_raw = projected[:, proj_width : proj_width + head_size]
    value_low = projected[:, proj_width + head_size :].astype(jnp.bfloat16)

    def query_key(query_in, key_in, gain_pair):
        query_norm = norm_scale(query_in.reshape(tok_rows, head_count, head_size), gain_pair[0])
        key_norm = norm_scale(key_in, gain_pair[1])
        return (
            rotate(query_norm, cosine[:, None, :], sine_table[:, None, :]),
            rotate(key_norm, cosine, sine_table),
        )

    (query_rot, key_rot), pull_heads = jax.vjp(query_key, query_raw, key_raw, head_gain)
    query_parts = to_parts(jnp.transpose(query_rot.astype(jnp.bfloat16), (1, 0, 2)))
    key_low = key_rot.astype(jnp.bfloat16)
    part_pos = [
        jnp.tile(positions[j * block_len : (j + 1) * block_len], head_count) for j in range(2)
    ]
    part_top = [jnp.max(positions[j * block_len : (j + 1) * block_len]) for j in range(2)]

    def exponent(query_part, query_pos, piece_key, key_pos):
        raw_score = jnp.einsum(
            "qd,kd->qk", query_part, piece_key, preferred_element_type=jnp.float32
        )
        allowed = key_pos[None, :] <= query_pos[:, None]
        return jnp.where(allowed, jnp.exp(raw_score * score_scale - score_bound), 0.0)

    def split_piece(pieces, start_row):
        piece_key, piece_value = pieces
        piece_rows = piece_key.shape[0]
        sub_rows = min(block_len, piece_rows)
        count = piece_rows // sub_rows
        key_pos = row_positions(block_order, start_row, piece_rows, block_len)
        return (
            (
                piece_key.reshape(count, sub_rows, head_size),
                piece_value.reshape(count, sub_rows, head_size),
                key_pos.reshape(count, sub_rows),
            ),
            piece_rows,
            sub_rows,
        )

    initial = (
        jnp.zeros((2, head_count * block_len, head_size), jnp.float32),
        jnp.zeros((2, head_count * block_len), jnp.float32),
    )
    items, piece_rows, sub_rows = split_piece(
        (
            lax.all_gather(key_low, "ctx", axis=0, tiled=True),
            lax.all_gather(value_low, "ctx", axis=0, tiled=True),
        ),
        jnp.int32(0),
    )

    def forward_step(carry, item):
        numerators, totals = carry
        key_block, value_block, pos_block = item
        new_num = []
        new_tot = []
        for j in range(2):

            def forward_accumulate(current, j=j):
                numerator, row_total = current
                exp_terms = exponent(query_parts[j], part_pos[j], key_block, pos_block)
                numerator = numerator + jnp.dot(
                    exp_terms.astype(jnp.bfloat16), value_block, preferred_element_type=jnp.float32
                )
                return (numerator, row_total + jnp.sum(exp_terms, axis=1))

            num_j, tot_j = lax.cond(
                jnp.min(pos_block) <= part_top[j],
                forward_accumulate,
                keep_state,
                (numerators[j], totals[j]),
            )
            new_num.append(num_j)
            new_tot.append(tot_j)
        return ((jnp.stack(new_num), jnp.stack(new_tot)), None)

    result_state, unused = lax.scan(forward_step, initial, items)
    numerator, row_total = result_state
    attended = numerator / row_total[..., None]
    attended_low = (
        jnp.transpose(from_parts(attended), (1, 0, 2))
        .reshape(tok_rows, proj_width)
        .astype(jnp.bfloat16)
    )
    branch = jnp.dot(attended_low, full_out, preferred_element_type=jnp.float32)

    def post_attention(branch_in, source_in, gain_post, gain_pre):
        middle_out = source_in + norm_scale(branch_in, gain_post)
        return (middle_out, norm_scale(middle_out, gain_pre))

    (middle, ff_normed), pull_post = jax.vjp(post_attention, branch, source, gains[1], gains[2])
    ff_in = ff_normed.astype(jnp.bfloat16)
    gate_matrix, up_matrix, down_matrix = (
        lax.all_gather(gate_weight, "fsdp", axis=1, tiled=True),
        lax.all_gather(up_weight, "fsdp", axis=1, tiled=True),
        lax.all_gather(down_weight, "fsdp", axis=0, tiled=True),
    )
    gate_out = jnp.dot(ff_in, gate_matrix, preferred_element_type=jnp.float32)
    up_out = jnp.dot(ff_in, up_matrix, preferred_element_type=jnp.float32)

    def activate(gate_in, up_in):
        return jax.nn.gelu(gate_in, approximate=True) * up_in

    hidden_full, pull_act = jax.vjp(activate, gate_out, up_out)
    hidden = hidden_full.astype(jnp.bfloat16)
    mixed_term = jnp.dot(hidden, down_matrix, preferred_element_type=jnp.float32)

    def finish(mixed_in, middle_in, gain_last):
        return middle_in + norm_scale(mixed_in, gain_last)

    result, pull_finish = jax.vjp(finish, mixed_term, middle, gains[3])
    upstream = cotangent.astype(jnp.float32)
    grad_mixed, grad_middle, grad_gain_last = pull_finish(upstream)
    grad_mixed_low = grad_mixed.astype(jnp.bfloat16)
    grad_hidden = jnp.einsum(
        "rd,fd->rf", grad_mixed_low, down_matrix, preferred_element_type=jnp.float32
    )
    grad_down = jnp.einsum("rf,rd->fd", hidden, grad_mixed_low, preferred_element_type=jnp.float32)
    grad_gate, grad_up = pull_act(grad_hidden)
    grad_gate_low = grad_gate.astype(jnp.bfloat16)
    grad_up_low = grad_up.astype(jnp.bfloat16)
    grad_gate_w = jnp.einsum("rd,rf->df", ff_in, grad_gate_low, preferred_element_type=jnp.float32)
    grad_up_w = jnp.einsum("rd,rf->df", ff_in, grad_up_low, preferred_element_type=jnp.float32)
    grad_ff_term = jnp.einsum(
        "rf,df->rd", grad_gate_low, gate_matrix, preferred_element_type=jnp.float32
    ) + jnp.einsum("rf,df->rd", grad_up_low, up_matrix, preferred_element_type=jnp.float32)
    share_gate, share_up, share_down = (
        lax.psum_scatter(
            grad_gate_w.astype(jnp.bfloat16), "fsdp", scatter_dimension=1, tiled=True
        ).astype(jnp.float32),
        lax.psum_scatter(
            grad_up_w.astype(jnp.bfloat16), "fsdp", scatter_dimension=1, tiled=True
        ).astype(jnp.float32),
        lax.psum_scatter(
            grad_down.astype(jnp.bfloat16), "fsdp", scatter_dimension=0, tiled=True
        ).astype(jnp.float32),
    )
    grad_branch, grad_source_post, grad_gain_post, grad_gain_pre = pull_post(
        (grad_middle, grad_ff_term)
    )
    grad_branch_low = grad_branch.astype(jnp.bfloat16)
    grad_out_w = jnp.einsum(
        "rh,rd->hd", attended_low, grad_branch_low, preferred_element_type=jnp.float32
    )
    grad_attended = jnp.einsum(
        "rd,hd->rh", grad_branch_low, full_out, preferred_element_type=jnp.float32
    )
    grad_att_parts = to_parts(
        jnp.transpose(grad_attended.reshape(tok_rows, head_count, head_size), (1, 0, 2))
    )
    scaled_grad = (grad_att_parts / row_total[..., None]).astype(jnp.bfloat16)
    total_grad = -jnp.sum(grad_att_parts * attended, axis=2) / row_total
    grad_query_acc = jnp.zeros((2, head_count * block_len, head_size), jnp.float32)
    items, piece_rows, sub_rows = split_piece(
        (
            lax.all_gather(key_low, "ctx", axis=0, tiled=True),
            lax.all_gather(value_low, "ctx", axis=0, tiled=True),
        ),
        jnp.int32(0),
    )

    def backward_step(carry, item):
        key_block, value_block, pos_block = item
        key_sum = jnp.zeros((sub_rows, head_size), jnp.float32)
        value_sum = jnp.zeros((sub_rows, head_size), jnp.float32)
        new_query = []
        for j in range(2):

            def backward_accumulate(current, j=j):
                query_acc, key_acc, value_acc = current
                exp_terms = exponent(query_parts[j], part_pos[j], key_block, pos_block)
                grad_prob = jnp.einsum(
                    "qd,kd->qk", scaled_grad[j], value_block, preferred_element_type=jnp.float32
                )
                score_grad = (
                    exp_terms * (grad_prob + total_grad[j][:, None]) * score_scale
                ).astype(jnp.bfloat16)
                query_acc = query_acc + jnp.dot(
                    score_grad, key_block, preferred_element_type=jnp.float32
                )
                key_acc = key_acc + jnp.einsum(
                    "qk,qd->kd", score_grad, query_parts[j], preferred_element_type=jnp.float32
                )
                value_acc = value_acc + jnp.einsum(
                    "qk,qd->kd",
                    exp_terms.astype(jnp.bfloat16),
                    scaled_grad[j],
                    preferred_element_type=jnp.float32,
                )
                return (query_acc, key_acc, value_acc)

            query_j, key_sum, value_sum = lax.cond(
                jnp.min(pos_block) <= part_top[j],
                backward_accumulate,
                keep_state,
                (carry[j], key_sum, value_sum),
            )
            new_query.append(query_j)
        return (jnp.stack(new_query), (key_sum, value_sum))

    grad_query_acc, (key_blocks, value_blocks) = lax.scan(backward_step, grad_query_acc, items)
    grad_keys = key_blocks.reshape(piece_rows, head_size)
    grad_values = value_blocks.reshape(piece_rows, head_size)
    grad_query_acc, grad_keys, grad_values = (grad_query_acc, grad_keys, grad_values)
    grad_key_own, grad_value_own = (
        lax.psum_scatter(grad_keys, "ctx", scatter_dimension=0, tiled=True),
        lax.psum_scatter(grad_values, "ctx", scatter_dimension=0, tiled=True),
    )
    grad_query_rot = jnp.transpose(from_parts(grad_query_acc), (1, 0, 2))
    grad_query_raw, grad_key_raw, grad_head = pull_heads((grad_query_rot, grad_key_own))
    grad_proj = jnp.concatenate(
        [
            grad_query_raw.astype(jnp.bfloat16),
            grad_key_raw.astype(jnp.bfloat16),
            grad_value_own.astype(jnp.bfloat16),
        ],
        axis=1,
    )
    grad_joined = jnp.einsum("rd,rc->dc", normed_low, grad_proj, preferred_element_type=jnp.float32)
    grad_normed = jnp.einsum("rc,dc->rd", grad_proj, joined, preferred_element_type=jnp.float32)
    grad_source_in, grad_gain_in = pull_input(grad_normed)
    input_grad = grad_source_post + grad_source_in
    grad_gains = jnp.stack([grad_gain_in, grad_gain_post, grad_gain_pre, grad_gain_last])
    share_query, share_key, share_value, share_out, share_gains, share_head = (
        lax.psum_scatter(
            grad_joined[:, :proj_width].astype(jnp.bfloat16),
            "fsdp",
            scatter_dimension=0,
            tiled=True,
        ).astype(jnp.float32),
        lax.psum_scatter(
            grad_joined[:, proj_width : proj_width + head_size].astype(jnp.bfloat16),
            "fsdp",
            scatter_dimension=0,
            tiled=True,
        ).astype(jnp.float32),
        lax.psum_scatter(
            grad_joined[:, proj_width + head_size :].astype(jnp.bfloat16),
            "fsdp",
            scatter_dimension=0,
            tiled=True,
        ).astype(jnp.float32),
        lax.psum_scatter(
            grad_out_w.astype(jnp.bfloat16), "fsdp", scatter_dimension=0, tiled=True
        ).astype(jnp.float32),
        lax.psum_scatter(
            grad_gains.astype(jnp.bfloat16), "fsdp", scatter_dimension=1, tiled=True
        ).astype(jnp.float32),
        lax.psum_scatter(
            grad_head.astype(jnp.bfloat16), "fsdp", scatter_dimension=1, tiled=True
        ).astype(jnp.float32),
    )
    (
        total_query,
        total_key,
        total_value,
        total_out,
        total_gate,
        total_up,
        total_down,
        total_gains,
        total_head,
    ) = lax.psum(
        (
            share_query,
            share_key,
            share_value,
            share_out,
            share_gate,
            share_up,
            share_down,
            share_gains,
            share_head,
        ),
        "ctx",
    )
    return (
        result.astype(jnp.bfloat16),
        input_grad,
        total_query,
        total_key,
        total_value,
        total_out,
        total_gate,
        total_up,
        total_down,
        total_gains,
        total_head,
    )


def solution(mesh):
    in_specs = (
        P(("ctx", "fsdp"), None),
        P(("ctx", "fsdp"), None),
        P(),
        P("fsdp", None),
        P("fsdp", None),
        P("fsdp", None),
        P("fsdp", None),
        P(None, "fsdp"),
        P(None, "fsdp"),
        P("fsdp", None),
        P(None, "fsdp"),
        P(None, "fsdp"),
    )
    out_specs = (
        P(("ctx", "fsdp"), None),
        P(("ctx", "fsdp"), None),
        P("fsdp", None),
        P("fsdp", None),
        P("fsdp", None),
        P("fsdp", None),
        P(None, "fsdp"),
        P(None, "fsdp"),
        P("fsdp", None),
        P(None, "fsdp"),
        P(None, "fsdp"),
    )
    return jax.shard_map(shards, mesh=mesh, in_specs=in_specs, out_specs=out_specs, check_vma=False)
```

profile of v0, /device:TPU:0, one launch (start us, length us, event | category | flops | bytes accessed | tf_op | source)
XLA Modules:
  0.0 952.6 jit_solution(6388238229130423300)
XLA Ops:
  10.7 6.1 all-gather
  18.3 10.2 %fusion.110 = s32[1024]{0:T(1024)S(1)} fusion(s32[]{:T(128)} %bitcast.37, s32[]{:T(128)} %bitcast.36, s32[]{:T(128)} %bitcast.35, s32[]{:T(128)} %bitcast.34, s32[]{:T(128)} %bitcast.33, s32[]{:T(128)} %bitcast.32, s32[]{:T(128)} %bitcast.31, s32[]{:T(128)} %bitcast.30, s32[]{:T(128)} %bitcast.29, s32[]{:T(128)} %bitcast.28, s32[]{:T(128)} %bitcast.27, ...), kind=kLoop, calls=%fused_computation.197 | loop fusion | flops 52224 | bytes 4160 | tf_op jit(solution)/shard_map/add | solution.py:42
  28.5 10.2 %fusion.140 = (f32[128]{0:T(128)S(1)}, s32[128]{0:T(128)S(1)}) fusion(s32[]{:T(128)} %bitcast.37, s32[]{:T(128)} %bitcast.36, s32[]{:T(128)} %bitcast.35, s32[]{:T(128)} %bitcast.34, s32[]{:T(128)} %bitcast.33, s32[]{:T(128)} %bitcast.32, s32[]{:T(128)} %bitcast.31, s32[]{:T(128)} %bitcast.30, s32[]{:T(128)} %bitcast.29, s32[]{:T(128)} %bitcast.28, ...), kind=kLoop, calls=%fused_computation.279 | loop fusion | flops 10112 | bytes 1092 | tf_op jit(solution)/shard_map/convert_element_type | solution.py:36
  39.5 8.6 all_gather.37
  48.1 6.3 all_gather.38
  55.0 5.0 all-gather.1
  62.7 1.4 constant_dynamic-update-slice_fusion.4
  66.0 31.9 %all_gather.40 = bf16[1024,256]{1,0:T(8,128)(2,1)S(1)} all-gather(bf16[128,256]{1,0:T(8,128)(2,1)S(1)} %pad_maximum_fusion.7), channel_id=1, replica_groups=mesh['ctx'=8,'fsdp'=4] {'ctx'}, dimensions={0}, use_global_device_ids=true | all-gather | bytes 589824 | tf_op jit(solution)/shard_map/all_gather | solution.py:150
  97.9 31.4 %all_gather.41 = bf16[1024,256]{1,0:T(8,128)(2,1)S(1)} all-gather(bf16[128,256]{1,0:T(8,128)(2,1)S(1)} %slice.262), channel_id=1, replica_groups=mesh['ctx'=8,'fsdp'=4] {'ctx'}, dimensions={0}, use_global_device_ids=true | all-gather | bytes 589824 | tf_op jit(solution)/shard_map/all_gather | solution.py:151
  130.6 62.6 %while.28 = (s32[]{:T(128)}, f32[2,256,256]{2,1,0:T(8,128)S(1)}, f32[2,256]{1,0:T(2,128)S(1)}, s32[16,64]{1,0:T(8,128)S(1)}, s32[]{:T(128)}, /*index=5*/bf16[16,...) while((s32[]{:T(128)}, f32[2,256,256]{2,1,0:T(8,128)S(1)}, ...), condition=%wide.region_15.17_spmd.clone, body=%wide.region_7.16_spmd.clone.sunk | while | flops 34013764 | bytes 3828085 | solution.py:181
  194.1 1.9 multiply_reduce_fusion.9
  196.7 2.4 fusion.148
  199.1 3.6 multiply_convert_fusion.1
  202.7 2.6 multiply_reduce_fusion.7
  207.5 1.4 multiply_convert_fusion
  214.8 114.2 %while.29 = (s32[]{:T(128)}, f32[2,256,256]{2,1,0:T(8,128)S(1)}, f32[16,64,256]{2,1,0:T(8,128)}, f32[16,64,256]{2,1,0:T(8,128)}, s32[16,64]{1,0:T(8,128)}, /*ind...) while((s32[]{:T(128)}, f32[2,256,256]{2,1,0:T(8,128)S(1)}, ...), condition=%wide.region_29.31_spmd.clone, body=%wide.region_23.30_spmd.clone.sunk | while | flops 84475968 | bytes 5783997 | solution.py:305
  214.9 1.3 fusion.198
  222.9 1.3 fusion.198
  230.0 1.3 fusion.198
  244.1 1.3 fusion.198
  251.2 1.3 fusion.198
  272.4 1.3 fusion.198
  279.5 1.3 fusion.198
  286.5 1.3 fusion.198
  293.6 1.3 fusion.198
  300.7 1.3 fusion.198
  307.8 1.3 fusion.198
  314.8 1.3 fusion.198
  321.9 1.3 fusion.198
  331.3 2.1 multiply_reduce_fusion
  335.1 1.4 fusion.68
  337.3 56.1 %reduce-scatter.16.cloned.1.call-done = f32[128,256]{1,0:T(8,128)} async-done(((f32[1024,256]{1,0:T(8,128)}), f32[128,256]{1,0:T(8,128)}) %reduce-scatter.16.cloned.1.call-update) | async-done | bytes 131088 | tf_op jit(solution)/shard_map/reduce_scatter | solution.py:310
  397.4 62.9 %reduce-scatter.18.cloned.1.call-done = f32[128,256]{1,0:T(8,128)} async-done(((f32[1024,256]{1,0:T(8,128)}), f32[128,256]{1,0:T(8,128)}) %reduce-scatter.18.cloned.1.call-update) | async-done | bytes 131088 | tf_op jit(solution)/shard_map/reduce_scatter | solution.py:311
  461.3 2.5 fusion.76
  465.5 1.5 convolution_convert_fusion.4
  467.2 1.8 convolution_convert_fusion
  471.8 3.4 convolution_convert_fusion.3
  476.2 2.4 convolution_convert_fusion.2
  479.6 2.4 convolution_convert_fusion.1
  484.6 21.4 %reduce-scatter.34.cloned.1.call-done = bf16[160,4]{1,0:T(8,128)(2,1)} async-done(((bf16[640,4]{1,0:T(8,128)(2,1)}), bf16[160,4]{1,0:T(8,128)(2,1)}) %reduce-scatter.34.cloned.1.call-update) | async-done | bytes 1296
  506.8 28.8 %reduce-scatter.26.cloned.1.call-done = bf16[256,640]{1,0:T(8,128)(2,1)} async-done(((bf16[1024,640]{1,0:T(8,128)(2,1)}), bf16[256,640]{1,0:T(8,128)(2,1)}) %reduce-scatter.26.cloned.1.call-update) | async-done | bytes 327696 | tf_op jit(solution)/shard_map/reduce_scatter | solution.py:347
  535.7 23.5 %reduce-scatter.22.cloned.1.call-done = bf16[160,256]{1,0:T(8,128)(2,1)} async-done(((bf16[640,256]{1,0:T(8,128)(2,1)}), bf16[160,256]{1,0:T(8,128)(2,1)}) %reduce-scatter.22.cloned.1.call-update) | async-done | bytes 81936 | tf_op jit(solution)/shard_map/reduce_scatter | solution.py:335
  559.2 23.5 %reduce-scatter.24.cloned.1.call-done = bf16[160,256]{1,0:T(8,128)(2,1)} async-done(((bf16[640,256]{1,0:T(8,128)(2,1)}), bf16[160,256]{1,0:T(8,128)(2,1)}) %reduce-scatter.24.cloned.1.call-update) | async-done | bytes 81936 | tf_op jit(solution)/shard_map/reduce_scatter | solution.py:341
  582.8 29.7 %reduce-scatter.20.cloned.1.call-done = bf16[160,1024]{1,0:T(8,128)(2,1)} async-done(((bf16[640,1024]{1,0:T(8,128)(2,1)}), bf16[160,1024]{1,0:T(8,128)(2,1)}) %reduce-scatter.20.cloned.1.call-update) | async-done | bytes 327696 | tf_op jit(solution)/shard_map/reduce_scatter | solution.py:329
  612.5 37.3 %reduce-scatter.28.cloned.1.call-done = bf16[640,512]{1,0:T(8,128)(2,1)} async-done(((bf16[640,2048]{1,0:T(8,128)(2,1)}), bf16[640,512]{1,0:T(8,128)(2,1)}) %reduce-scatter.28.cloned.1.call-update) | async-done | bytes 655376 | tf_op jit(solution)/shard_map/reduce_scatter | solution.py:232
  649.7 37.1 %reduce-scatter.30.cloned.1.call-done = bf16[640,512]{1,0:T(8,128)(2,1)} async-done(((bf16[640,2048]{1,0:T(8,128)(2,1)}), bf16[640,512]{1,0:T(8,128)(2,1)}) %reduce-scatter.30.cloned.1.call-update) | async-done | bytes 655376 | tf_op jit(solution)/shard_map/reduce_scatter | solution.py:235
  686.8 37.3 %reduce-scatter.32.cloned.1.call-done = bf16[512,640]{1,0:T(8,128)(2,1)} async-done(((bf16[2048,640]{1,0:T(8,128)(2,1)}), bf16[512,640]{1,0:T(8,128)(2,1)}) %reduce-scatter.32.cloned.1.call-update) | async-done | bytes 655376 | tf_op jit(solution)/shard_map/reduce_scatter | solution.py:238
  724.1 222.0 %all-reduce.8 = (f32[160,1024]{1,0:T(8,128)}, f32[160,256]{1,0:T(8,128)}, f32[160,256]{1,0:T(8,128)}, f32[256,640]{1,0:T(8,128)}, f32[640,512]{1,0:T(8,128)}, /*...) all-reduce(bf16[160,1024]{1,0:T(8,128)(2,1)} %reduce-scatter.20.clo, ...), channel_id=1, replica_groups=mesh['ctx'=8,'fsdp'=4] {'ctx'}, use_global_device_ids=true, to_apply=%region_36.38 | all-reduce | flops 1393408 | bytes 8360448 | tf_op jit(solution)/shard_map/psum | solution.py:367
  (757 shorter events, 143.8 us)
Async XLA Ops:
  7.2 3.5 copy-start.61
  7.2 10.4 %copy-start.33 = (s32[16]{0:T(128)S(1)}, s32[16]{0:T(128)}, u32[]{:S(2)}) copy-start(s32[16]{0:T(128)} %param.28) | copy-start | bytes 196
  7.2 32.3 %copy-start.34 = (bf16[160,256]{1,0:T(8,128)(2,1)S(1)}, bf16[160,256]{1,0:T(8,128)(2,1)}, u32[]{:S(2)}) copy-start(bf16[160,256]{1,0:T(8,128)(2,1)} %param.30) | copy-start | bytes 245764
  7.2 40.8 %copy-start.35 = (bf16[160,256]{1,0:T(8,128)(2,1)S(1)}, bf16[160,256]{1,0:T(8,128)(2,1)}, u32[]{:S(2)}) copy-start(bf16[160,256]{1,0:T(8,128)(2,1)} %param.31) | copy-start | bytes 245764
  7.2 47.2 %copy-start.6 = (bf16[128,640]{1,0:T(8,128)(2,1)S(1)}, bf16[128,640]{1,0:T(8,128)(2,1)}, u32[]{:S(2)}) copy-start(bf16[128,640]{1,0:T(8,128)(2,1)} %param.26) | copy-start | bytes 491524
  7.2 47.8 %copy-start.69 = (bf16[2,64]{1,0:T(2,128)(2,1)S(1)}, bf16[2,64]{1,0:T(2,128)(2,1)}, u32[]{:S(2)}) copy-start(bf16[2,64]{1,0:T(2,128)(2,1)} %param.37) | copy-start | bytes 772
  7.2 55.4 %all-gather.8.cloned.1.call-start = ((), (), s32[]{:S(2)}) async-start(), calls=%async_computation.11 | async-start | bytes 1638400 | tf_op jit(solution)/shard_map/all_gather | solution.py:84
  8.0 186.1 %all-gather.10.cloned.1.call-start = ((), (), s32[]{:S(2)}) async-start(), calls=%async_computation.12 | async-start | bytes 1638400 | tf_op jit(solution)/shard_map/all_gather | solution.py:87
  8.7 187.9 %all-gather.12.cloned.1.call-start = ((), (), s32[]{:S(2)}) async-start(), calls=%async_computation.13 | async-start | bytes 3276800 | tf_op jit(solution)/shard_map/all_gather | solution.py:198
  9.5 189.6 %all-gather.14.cloned.1.call-start = ((), (), s32[]{:S(2)}) async-start(), calls=%async_computation.14 | async-start | bytes 3276800 | tf_op jit(solution)/shard_map/all_gather | solution.py:199
  10.0 192.6 %all-gather.16.cloned.1.call-start = ((), (), s32[]{:S(2)}) async-start(), calls=%async_computation.15 | async-start | bytes 3276800 | tf_op jit(solution)/shard_map/all_gather | solution.py:200
  10.6 382.8 %reduce-scatter.16.cloned.1.call-start = ((), (), s32[]{:S(2)}) async-start(), calls=%async_computation.16 | async-start | bytes 1179648 | tf_op jit(solution)/shard_map/reduce_scatter | solution.py:310
  10.7 54.9 %copy-start.60 = (f32[128]{0:T(128)}, f32[128]{0:T(128)S(1)}, u32[]{:S(2)}) copy-start(f32[128]{0:T(128)S(1)} %multiply_power_fusion) | copy-start | bytes 1540
  38.7 26.9 %copy-start.55 = (f32[128]{0:T(128)}, f32[128]{0:T(128)S(1)}, u32[]{:S(2)}) copy-start(f32[128]{0:T(128)S(1)} %get-tuple-element.510) | copy-start | bytes 1540
  54.5 9.7 %copy-start.57 = (f32[128]{0:T(128)}, f32[128]{0:T(128)S(1)}, u32[]{:S(2)}) copy-start(f32[128]{0:T(128)S(1)} %fusion.133) | copy-start | bytes 1540
  60.1 5.4 copy-start.44
  60.1 69.8 %copy-start.46 = (f32[1,256]{1,0:T(1,128)}, f32[1,256]{1,0:T(1,128)S(1)}, u32[]{:S(2)}) copy-start(f32[1,256]{1,0:T(1,128)S(1)} %get-tuple-element.546) | copy-start | bytes 3076
  64.7 33.2 %copy-start.5 = (f32[128,1536]{1,0:T(8,128)}, f32[128,1536]{1,0:T(8,128)S(1)}, u32[]{:S(2)}) copy-start(f32[128,1536]{1,0:T(8,128)S(1)} %fusion.102) | copy-start | bytes 2359300
  64.8 33.1 %copy-start.64 = (f32[128]{0:T(128)}, f32[128]{0:T(128)S(1)}, u32[]{:S(2)}) copy-start(f32[128]{0:T(128)S(1)} %multiply_reduce_fusion.12) | copy-start | bytes 1540
  65.5 64.7 %copy-start.49 = (f32[128]{0:T(128)}, f32[128]{0:T(128)S(1)}, u32[]{:S(2)}) copy-start(f32[128]{0:T(128)S(1)} %fusion.134) | copy-start | bytes 1540
  66.0 64.3 %copy-start.27 = (f32[128,128]{1,0:T(8,128)}, f32[128,128]{1,0:T(8,128)S(1)}, u32[]{:S(2)}) copy-start(f32[128,128]{1,0:T(8,128)S(1)} %get-tuple-element.548) | copy-start | bytes 196612
  66.0 64.3 %copy-start.29 = (f32[128,128]{1,0:T(8,128)}, f32[128,128]{1,0:T(8,128)S(1)}, u32[]{:S(2)}) copy-start(f32[128,128]{1,0:T(8,128)S(1)} %get-tuple-element.549) | copy-start | bytes 196612
  194.1 5.0 copy-start.13
  202.7 4.8 copy-start.10
  202.7 4.8 copy-start.24
  208.9 3.3 copy-start.15
  208.9 3.3 copy-start.17
  329.0 131.3 %reduce-scatter.18.cloned.1.call-start = ((), (), s32[]{:S(2)}) async-start(), calls=%async_computation.17 | async-start | bytes 1179648 | tf_op jit(solution)/shard_map/reduce_scatter | solution.py:311
  329.8 4.5 copy-start.43
  329.8 154.0 %reduce-scatter.36.cloned.1.call-start = ((), (), s32[]{:S(2)}) async-start(), calls=%async_computation.26 | async-start | bytes 81920
  330.4 6.9 copy-start.48
  330.4 63.0 %copy-start.56 = (f32[128]{0:T(128)S(1)}, f32[128]{0:T(128)}, u32[]{:S(2)}) copy-start(f32[128]{0:T(128)} %copy-done.55) | copy-start | bytes 1540
  330.6 64.0 %copy-start.45 = (f32[1,256]{1,0:T(1,128)S(1)}, f32[1,256]{1,0:T(1,128)}, u32[]{:S(2)}) copy-start(f32[1,256]{1,0:T(1,128)} %copy-done.44) | copy-start | bytes 3076
  330.6 64.0 %copy-start.50 = (f32[128]{0:T(128)S(1)}, f32[128]{0:T(128)}, u32[]{:S(2)}) copy-start(f32[128]{0:T(128)} %copy-done.49) | copy-start | bytes 1540
  331.3 129.9 %copy-start.3 = (bf16[640,1536]{1,0:T(8,128)(2,1)S(1)}, bf16[640,1536]{1,0:T(8,128)(2,1)}, u32[]{:S(2)}) copy-start(bf16[640,1536]{1,0:T(8,128)(2,1)} %copy-done.2) | copy-start | bytes 5898244
  331.3 129.9 %copy-start.7 = (bf16[128,640]{1,0:T(8,128)(2,1)S(1)}, bf16[128,640]{1,0:T(8,128)(2,1)}, u32[]{:S(2)}) copy-start(bf16[128,640]{1,0:T(8,128)(2,1)} %param.26) | copy-start | bytes 491524
  331.3 129.9 %copy-start.58 = (f32[128]{0:T(128)S(1)}, f32[128]{0:T(128)}, u32[]{:S(2)}) copy-start(f32[128]{0:T(128)} %copy-done.57) | copy-start | bytes 1540
  395.7 68.0 %copy-start.59 = (f32[256]{0:T(256)S(1)}, f32[256]{0:T(256)}, u32[]{:S(2)}) copy-start(f32[256]{0:T(256)} %get-tuple-element.426) | copy-start | bytes 3076
  461.2 4.3 copy-start.14
  461.2 4.3 copy-start.20
  464.5 41.4 %reduce-scatter.34.cloned.1.call-start = ((), (), s32[]{:S(2)}) async-start(), calls=%async_computation.25 | async-start | bytes 204800
  465.5 70.2 %reduce-scatter.26.cloned.1.call-start = ((), (), s32[]{:S(2)}) async-start(), calls=%async_computation.21 | async-start | bytes 1638400 | tf_op jit(solution)/shard_map/reduce_scatter | solution.py:347
  467.1 92.1 %reduce-scatter.22.cloned.1.call-start = ((), (), s32[]{:S(2)}) async-start(), calls=%async_computation.19 | async-start | bytes 409600 | tf_op jit(solution)/shard_map/reduce_scatter | solution.py:335
  469.8 112.9 %reduce-scatter.24.cloned.1.call-start = ((), (), s32[]{:S(2)}) async-start(), calls=%async_computation.20 | async-start | bytes 409600 | tf_op jit(solution)/shard_map/reduce_scatter | solution.py:341
  470.4 142.0 %reduce-scatter.20.cloned.1.call-start = ((), (), s32[]{:S(2)}) async-start(), calls=%async_computation.18 | async-start | bytes 1638400 | tf_op jit(solution)/shard_map/reduce_scatter | solution.py:329
  471.7 178.0 %reduce-scatter.28.cloned.1.call-start = ((), (), s32[]{:S(2)}) async-start(), calls=%async_computation.22 | async-start | bytes 3276800 | tf_op jit(solution)/shard_map/reduce_scatter | solution.py:232
  475.2 211.6 %reduce-scatter.30.cloned.1.call-start = ((), (), s32[]{:S(2)}) async-start(), calls=%async_computation.23 | async-start | bytes 3276800 | tf_op jit(solution)/shard_map/reduce_scatter | solution.py:235
  478.7 245.4 %reduce-scatter.32.cloned.1.call-start = ((), (), s32[]{:S(2)}) async-start(), calls=%async_computation.24 | async-start | bytes 3276800 | tf_op jit(solution)/shard_map/reduce_scatter | solution.py:238
  (38 other events, 55.2 us)
Sparse Core Ops, SparseCore 0:
  9.6 20.9 all-gather.7
  32.1 19.9 all-gather.9
  53.7 25.5 all-gather.11
  80.7 25.5 all-gather.13
  107.7 25.5 all-gather.15
  329.2 64.2 reduce-scatter.15
  397.8 62.4 reduce-scatter.17
  464.7 18.4 reduce-scatter.35
  486.3 19.6 reduce-scatter.33
  509.1 26.5 reduce-scatter.25
  538.7 20.4 reduce-scatter.21
  562.3 20.4 reduce-scatter.23
  585.9 26.5 reduce-scatter.19
  615.0 34.6 reduce-scatter.27
  652.1 34.6 reduce-scatter.29
  689.4 34.6 reduce-scatter.31
where the time goes:
time: 957 us; the launch traced here: 953 us
  waiting for transfers between devices  362 us (38%)
  blocking collectives  311 us (32%)
  loops' own time  83.5 us (9%)
  other arithmetic  68.6 us (7%)
  local copies, waits for them, and re-layouts  58 us (6%)
  matrix products  51.7 us (5%)
  between operations  16.4 us (2%)
    psum x1, blocking collectives, shards(): lax.psum((share_query, share_key, share_value, share_out, share_gate, sha...  222 us
    reduce_scatter x1, waiting for transfers between devices, shards(): lax.psum_scatter(grad_values, 'ctx', scatter_dimension=0, tiled=True)  62.9 us
    reduce_scatter x1, waiting for transfers between devices, shards(): lax.psum_scatter(grad_keys, 'ctx', scatter_dimension=0, tiled=True)  56.1 us
    another operation x1, loops' own time, shards(): result_state, unused = lax.scan(forward_step, initial, items)  41 us
    another operation x1, loops' own time, shards(): lax.scan(backward_step, grad_query_acc, items)  40.5 us
    reduce_scatter x1, waiting for transfers between devices, shards(): lax.psum_scatter(grad_down.astype(jnp.bfloat16), 'fsdp', scatter_dimensio...  37.3 us
    reduce_scatter x1, waiting for transfers between devices, shards(): lax.psum_scatter(grad_gate_w.astype(jnp.bfloat16), 'fsdp', scatter_dimens...  37.3 us
    reduce_scatter x1, waiting for transfers between devices, shards(): lax.psum_scatter(grad_up_w.astype(jnp.bfloat16), 'fsdp', scatter_dimensio...  37.1 us
  transfers between devices with their start and end apart: 16, of which 10 were waited for; matrix products, arithmetic and copies ran while one was open for 9% of the time, Pallas kernels for 0%

commit v1 on v0

v1 whole, which is shorter than its diff:
```python
import functools
import math

import jax
import jax.numpy as jnp
from jax import lax
from jax.experimental import pallas as pl
from jax.experimental.pallas import tpu as pltpu
from jax.sharding import PartitionSpec as P

HEADS = 4
HEAD_DIM = 256
NORM_EPS = 1e-06
ROPE_BASE = 1000000.0
BF = jnp.bfloat16
F32 = jnp.float32
MIB = 1024 * 1024


def dot(a, b):
    return lax.dot_general(a, b, (((1,), (0,)), ((), ())), preferred_element_type=F32)


def dot_nt(a, b):
    return lax.dot_general(a, b, (((1,), (1,)), ((), ())), preferred_element_type=F32)


def dot_tn(a, b):
    return lax.dot_general(a, b, (((0,), (0,)), ((), ())), preferred_element_type=F32)


def unit(v):
    r = lax.rsqrt(jnp.mean(v * v, axis=-1, keepdims=True) + NORM_EPS)
    return v * r, r


def norm_back(c, u, r, g):
    cg = c * g
    grad = r * (cg - u * jnp.mean(cg * u, axis=-1, keepdims=True))
    return grad, jnp.sum(c * u, axis=0, keepdims=True)


def rotate(v, cos, sin):
    half = v.shape[-1] // 2
    a, b = v[:, :half], v[:, half:]
    return jnp.concatenate([a * cos - b * sin, b * cos + a * sin], axis=-1)


def rotate_back(v, cos, sin):
    half = v.shape[-1] // 2
    a, b = v[:, :half], v[:, half:]
    return jnp.concatenate([a * cos + b * sin, b * cos - a * sin], axis=-1)


def assemble(f, blocks, scratch):
    rows = blocks[0].shape[0]
    for k, blk in enumerate(blocks):
        start = pl.multiple_of(jnp.bitwise_xor(f, k) * rows, 16)
        scratch[pl.ds(start, rows), :] = blk[...]


def call(kernel, outs, *args, scratch=(), vmem=40, flops=0, smem_first=False):
    specs = [pl.BlockSpec(memory_space=pltpu.VMEM)] * len(args)
    if smem_first:
        specs[0] = pl.BlockSpec(memory_space=pltpu.SMEM)
    moved = sum(math.prod(a.shape) * a.dtype.itemsize for a in args)
    return pl.pallas_call(
        kernel,
        out_shape=[jax.ShapeDtypeStruct(s, d) for s, d in outs],
        in_specs=specs,
        out_specs=[pl.BlockSpec(memory_space=pltpu.VMEM)] * len(outs),
        scratch_shapes=list(scratch),
        compiler_params=pltpu.CompilerParams(vmem_limit_bytes=vmem * MIB),
        cost_estimate=pl.CostEstimate(flops=flops, bytes_accessed=moved, transcendentals=0),
    )(*args)


def kv_kernel(nf, f_ref, tok, gains, hg, cos, sin, *rest):
    blocks, (normed_o, raw_o, kv_o, w) = rest[:nf], rest[nf:]
    assemble(f_ref[0], blocks, w)
    u, _ = unit(tok[...].astype(F32))
    normed = (u * gains[0:1, :]).astype(BF)
    normed_o[...] = normed
    out = dot(normed, w[...])
    key = out[:, :HEAD_DIM]
    raw_o[...] = key
    u, _ = unit(key)
    kv_o[:, :HEAD_DIM] = rotate(u * hg[1:2, :], cos[...], sin[...]).astype(BF)
    kv_o[:, HEAD_DIM:] = out[:, HEAD_DIM:].astype(BF)


def query_kernel(nf, f_ref, normed, hg, cos, sin, *rest):
    blocks, (raw_o, q_o, w) = rest[:nf], rest[nf:]
    assemble(f_ref[0], blocks, w)
    for h in range(HEADS):
        raw = dot(normed[...], w[:, h * HEAD_DIM : (h + 1) * HEAD_DIM])
        k = jnp.bitwise_xor(f_ref[0], h)
        raw_o[k] = raw
        u, _ = unit(raw)
        q_o[k] = rotate(u * hg[0:1, :], cos[...], sin[...]).astype(BF)


def bound_of(hg):
    peak = jnp.max(jnp.abs(hg[...]), axis=1, keepdims=True)
    return math.sqrt(HEAD_DIM) * peak[0:1, :] * peak[1:2, :]


def tile_loop(count, step):
    if count == 1:
        step(0)
    else:

        def body(t, carry):
            step(t)
            return carry

        lax.fori_loop(0, count, body, 0)


def attend_kernel(tile, q, kv, hg, qpos, kpos, att_o, low_o, tot_o):
    scale = 1.0 / math.sqrt(HEAD_DIM)
    bound = bound_of(hg)
    count = kv.shape[0] // tile
    for k in range(HEADS):

        def step(t, k=k):
            rows = pl.ds(pl.multiple_of(t * tile, tile), tile) if count > 1 else slice(None)
            raw = dot_nt(q[k], kv[rows, :HEAD_DIM])
            allowed = kpos[:, rows] <= qpos[...]
            terms = jnp.where(allowed, jnp.exp(raw * scale - bound), 0.0)
            total = jnp.sum(terms, axis=1, keepdims=True)
            num = dot(terms.astype(BF), kv[rows, HEAD_DIM:])
            if count == 1:
                tot_o[k], att_o[k] = total, num
            else:
                tot_o[k] += total
                att_o[k] += num

        if count > 1:
            tot_o[k] = jnp.zeros_like(tot_o[k])
            att_o[k] = jnp.zeros_like(att_o[k])
        tile_loop(count, step)
        att = att_o[k] / tot_o[k]
        att_o[k] = att
        low_o[k] = att.astype(BF)


def gelu_parts(v):
    inner = 0.7978845608028654 * (v + 0.044715 * v * v * v)
    t = jnp.tanh(inner)
    value = 0.5 * v * (1.0 + t)
    slope = 0.5 * (1.0 + t) + 0.5 * v * (1.0 - t * t) * 0.7978845608028654 * (
        1.0 + 3 * 0.044715 * v * v
    )
    return value, slope


def ff_kernel(nf, tok, cot, gains, att, *rest):
    wo, wg, wu, wd = (rest[i * nf : (i + 1) * nf] for i in range(4))
    rest = rest[4 * nf :]
    out_o, fg_o, gbl_o, resid_o, gg_o = rest[:5]
    ex_o = rest[5 : 5 + nf]
    gate_s, up_s = rest[5 + nf :]
    d = tok.shape[1]
    width = wg[0].shape[1]
    heads = att.shape[0] // nf
    branch = None
    for k in range(nf):
        term = dot(att[k], wo[k][...])
        branch = term if branch is None else branch + term
    x = tok[...].astype(F32)
    ub, rb = unit(branch)
    middle = x + ub * gains[1:2, :]
    um, rm = unit(middle)
    ff_in = (um * gains[2:3, :]).astype(BF)
    fg_o[:, :d] = ff_in
    mixed = None
    for k in range(nf):
        gate = dot(ff_in, wg[k][...])
        up = dot(ff_in, wu[k][...])
        gate_s[k] = gate
        up_s[k] = up
        value, _ = gelu_parts(gate)
        hidden = (value * up).astype(BF)
        ex_o[k][:, :width] = hidden
        term = dot(hidden, wd[k][...])
        mixed = term if mixed is None else mixed + term
    ux, rx = unit(mixed)
    out_o[...] = (middle + ux * gains[3:4, :]).astype(BF)
    c = cot[...].astype(F32)
    grad_mixed, gain3 = norm_back(c, ux, rx, gains[3:4, :])
    gml = grad_mixed.astype(BF)
    fg_o[:, d:] = gml
    gff = None
    for k in range(nf):
        gh = dot_nt(gml, wd[k][...])
        value, slope = gelu_parts(gate_s[k])
        gg = (gh * up_s[k] * slope).astype(BF)
        gu = (gh * value).astype(BF)
        ex_o[k][:, width : 2 * width] = gg
        ex_o[k][:, 2 * width :] = gu
        term = dot_nt(gg, wg[k][...]) + dot_nt(gu, wu[k][...])
        gff = term if gff is None else gff + term
    grad, gain2 = norm_back(gff, um, rm, gains[2:3, :])
    grad_middle = c + grad
    grad_branch, gain1 = norm_back(grad_middle, ub, rb, gains[1:2, :])
    resid_o[...] = grad_middle
    gbl_o[...] = grad_branch.astype(BF)
    gg_o[...] = jnp.concatenate([gain1, gain2, gain3], axis=0)


def attend_back_kernel(nf, tile, f_ref, gbl, att, tot, q, qraw, kv, hg, cos, sin, qpos, kpos, *rest):
    wo = rest[:nf]
    gq_o, gh_o, gkv_o, sg_s, tg_s, acc, s_s, e_s = rest[nf:]
    scale = 1.0 / math.sqrt(HEAD_DIM)
    rows_q = gbl.shape[0]
    bound = bound_of(hg)
    count = kv.shape[0] // tile
    for k in range(HEADS):
        ga = dot_nt(gbl[...], wo[k][...])
        inv = 1.0 / tot[k]
        sg_s[k * rows_q : (k + 1) * rows_q, :] = (ga * inv).astype(BF)
        tg_s[k] = -jnp.sum(ga * att[k], axis=1, keepdims=True) * inv

    def step(t):
        rows = pl.ds(pl.multiple_of(t * tile, tile), tile) if count > 1 else slice(None)
        allowed = kpos[:, rows] <= qpos[...]
        for k in range(HEADS):
            mine = slice(k * rows_q, (k + 1) * rows_q)
            raw = dot_nt(q[k], kv[rows, :HEAD_DIM])
            terms = jnp.where(allowed, jnp.exp(raw * scale - bound), 0.0)
            e_s[mine, :] = terms.astype(BF)
            gp = dot_nt(sg_s[mine, :], kv[rows, HEAD_DIM:])
            s = (terms * (gp + tg_s[k]) * scale).astype(BF)
            s_s[mine, :] = s
            part = dot(s, kv[rows, :HEAD_DIM])
            if count == 1:
                acc[k] = part
            else:
                acc[k] += part
        queries = q[...].reshape(HEADS * rows_q, HEAD_DIM)
        gkv_o[rows, :HEAD_DIM] = dot_tn(s_s[...], queries).astype(BF)
        gkv_o[rows, HEAD_DIM:] = dot_tn(e_s[...], sg_s[...]).astype(BF)

    if count > 1:
        acc[...] = jnp.zeros_like(acc)
    tile_loop(count, step)
    gain = None
    for k in range(HEADS):
        u, r = unit(qraw[k])
        c = rotate_back(acc[k], cos[...], sin[...])
        grad, g = norm_back(c, u, r, hg[0:1, :])
        gain = g if gain is None else gain + g
        h = jnp.bitwise_xor(f_ref[0], k)
        gq_o[:, pl.ds(pl.multiple_of(h * HEAD_DIM, HEAD_DIM), HEAD_DIM)] = grad.astype(BF)
    gh_o[...] = gain


def input_back_kernel(nf, f_ref, tok, gkv, kraw, gq, resid, gains, hg, cos, sin, gg, ghq, *rest):
    bq, bkv = rest[:nf], rest[nf : 2 * nf]
    pay_o, grad_o, wq, wkv = rest[2 * nf :]
    f = f_ref[0]
    rows = tok.shape[0]
    assemble(f, bkv, wkv)
    assemble(f, bq, wq)
    u, r = unit(kraw[...])
    c = rotate_back(gkv[:, :HEAD_DIM], cos[...], sin[...])
    gk, ghk = norm_back(c, u, r, hg[1:2, :])
    gkl = gk.astype(BF)
    gvl = gkv[:, HEAD_DIM:].astype(BF)
    pay_o[:rows, :HEAD_DIM] = gkl
    pay_o[:rows, HEAD_DIM:] = gvl
    gn = dot_nt(gq[...], wq[...]) + dot_nt(gkl, wkv[:, :HEAD_DIM]) + dot_nt(gvl, wkv[:, HEAD_DIM:])
    u, r = unit(tok[...].astype(F32))
    gx, gain0 = norm_back(gn, u, r, gains[0:1, :])
    grad_o[...] = resid[...] + gx
    all_gains = jnp.concatenate([gain0, gg[...]], axis=0)
    wide = 2 * HEAD_DIM
    tail = jnp.concatenate([all_gains[i : i + 1, wide:] for i in range(4)], axis=1)
    heads = jnp.concatenate([ghq[...], ghk], axis=1)
    pad = jnp.zeros((10, wide), F32)
    pay_o[rows:, :] = jnp.concatenate([all_gains[:, :wide], tail, heads, pad], axis=0).astype(BF)


def ff_grad_kernel(nf, *refs):
    fg, ex = refs[:nf], refs[nf : 2 * nf]
    gu_o, down_o, fg_s, ex_s = refs[2 * nf :]
    rows = fg[0].shape[0]
    for k in range(nf):
        fg_s[k * rows : (k + 1) * rows, :] = fg[k][...]
        ex_s[k * rows : (k + 1) * rows, :] = ex[k][...]
    d = down_o.shape[1]
    width = down_o.shape[0]
    gu_o[...] = dot_tn(fg_s[:, :d], ex_s[:, width:]).astype(BF)
    down_o[...] = dot_tn(ex_s[:, :width], fg_s[:, d:]).astype(BF)


def pair_grad_kernel(nf, rows, *refs):
    a, b = refs[:nf], refs[nf : 2 * nf]
    outs, (a_s, b_s) = refs[2 * nf : -2], refs[-2:]
    for k in range(nf):
        a_s[k * rows : (k + 1) * rows, :] = a[k][...]
        b_s[k * rows : (k + 1) * rows, :] = b[k][:rows, :]
    outs[0][...] = dot_tn(a_s[...], b_s[...]).astype(BF)
    if len(outs) > 1:
        total = b[0][rows:, :].astype(F32)
        for k in range(1, nf):
            total = total + b[k][rows:, :].astype(F32)
        outs[1][...] = total.astype(BF)


def swap(x, axis, n, bit):
    return lax.ppermute(x, axis, [(i, i ^ bit) for i in range(n)])


def gather_xor(x, axis, n):
    have = {0: x}
    bit = n // 2
    while bit:
        for k in list(have):
            have[k | bit] = swap(have[k], axis, n, bit)
        bit //= 2
    return [have[k] for k in range(n)]


def exchange_xor(blocks, axis, n):
    return [b if k == 0 else swap(b, axis, n, k) for k, b in enumerate(blocks)]


def gather_ctx(x, n):
    if n > 8:
        bit = 1
        while bit < n:
            x = jnp.concatenate([x, swap(x, "ctx", n, bit)], axis=0)
            bit *= 2
        return x
    far = {0: x}
    for k in range(n - 2, 0, -2):
        far[k] = swap(x, "ctx", n, k)
    have = {}
    for k in sorted(far):
        have[k] = far[k]
        have[k + 1] = swap(far[k], "ctx", n, 1)
    return jnp.concatenate([have[k] for k in range(n)], axis=0)


def scatter_sum_ctx(x, n):
    rows = x.shape[0] // n
    if n > 8:
        bit = n // 2
        while bit:
            keep, send = x[: bit * rows], x[bit * rows :]
            got = swap(send, "ctx", n, bit)
            x = (keep.astype(F32) + got.astype(F32)).astype(BF)
            bit //= 2
        return x.astype(F32)
    blocks = [x[k * rows : (k + 1) * rows] for k in range(n)]
    got = {k: swap(blocks[k], "ctx", n, 1) for k in range(n - 1, 0, -2)}
    total = None
    for k in range(n - 2, -1, -2):
        part = blocks[k].astype(F32) + got[k + 1].astype(F32)
        if k:
            part = swap(part.astype(BF), "ctx", n, k).astype(F32)
        total = part if total is None else total + part
    return total


def sum_ctx(x, n, c, bits):
    if x.shape[0] % n:
        return lax.psum(x.astype(F32), "ctx")
    for bit in bits:
        half = x.shape[0] // 2
        upper = (c & bit) != 0
        keep = jnp.where(upper, x[half:], x[:half])
        send = jnp.where(upper, x[:half], x[half:])
        got = swap(send, "ctx", n, bit)
        x = (keep.astype(F32) + got.astype(F32)).astype(BF)
    for bit in reversed(bits):
        upper = (c & bit) != 0
        got = swap(x, "ctx", n, bit)
        x = jnp.concatenate([jnp.where(upper, got, x), jnp.where(upper, x, got)], axis=0)
    return x.astype(F32)


def sum_ctx_direct(x, gains, n, c):
    if n > 8 or x.shape[0] % n:
        return lax.psum(x.astype(F32), "ctx"), lax.psum(gains.astype(F32), "ctx")
    rows = x.shape[0] // n
    pieces = x.reshape(n, rows, x.shape[1])
    total = None
    for k in range(n):
        piece = lax.dynamic_index_in_dim(pieces, c ^ k, 0, keepdims=False)
        piece = jnp.concatenate([piece, gains], axis=0)
        if k:
            piece = swap(piece, "ctx", n, k)
        piece = piece.astype(F32)
        total = piece if total is None else total + piece
    mine = total[:rows].astype(BF)
    got = jnp.stack([mine] + [swap(mine, "ctx", n, k) for k in range(1, n)])
    got = jnp.take(got, c ^ jnp.arange(n), axis=0)
    return got.reshape(x.shape).astype(F32), total[rows:]


def layer(
    nf,
    nc,
    tokens,
    cotangent,
    block_order,
    query_weight,
    key_weight,
    value_weight,
    out_weight,
    gate_weight,
    up_weight,
    down_weight,
    norm_gains,
    head_gains,
):
    rows, d = tokens.shape
    block_len = rows // 2
    f = lax.axis_index("fsdp")
    c = lax.axis_index("ctx")
    f_arr = f.reshape(1).astype(jnp.int32)
    seq = nc * rows
    tile = min(seq, 1024)
    proj = HEADS * HEAD_DIM
    width = gate_weight.shape[1]

    gain_pack = jnp.concatenate([norm_gains.reshape(-1), head_gains.reshape(-1)]).reshape(-1, 128)
    gain_blocks = gather_xor(gain_pack, "fsdp", nf)
    wkv = gather_xor(jnp.concatenate([key_weight, value_weight], axis=1), "fsdp", nf)
    wq = gather_xor(query_weight, "fsdp", nf)
    wo = gather_xor(out_weight, "fsdp", nf)
    wg = gather_xor(gate_weight, "fsdp", nf)
    wu = gather_xor(up_weight, "fsdp", nf)
    wd = gather_xor(down_weight, "fsdp", nf)

    pack = jnp.stack(gain_blocks).reshape(nf, -1).astype(F32)
    pack = jnp.take(pack, f ^ jnp.arange(nf), axis=0)
    split = norm_gains.size
    gains = pack[:, :split].reshape(nf, 4, -1).transpose(1, 0, 2).reshape(4, d)
    hg = pack[:, split:].reshape(nf, 2, -1).transpose(1, 0, 2).reshape(2, HEAD_DIM)

    order = jnp.take(block_order.reshape(nc, 2), c ^ jnp.arange(nc), axis=0)
    kpos = (order.reshape(-1, 1) * block_len + jnp.arange(block_len)[None, :]).reshape(1, seq)
    qpos = kpos[0, :rows].reshape(rows, 1)
    inv_freq = ROPE_BASE ** (-2.0 * jnp.arange(HEAD_DIM // 2, dtype=F32) / HEAD_DIM)
    angles = qpos.astype(F32) * inv_freq[None, :]
    cos, sin = jnp.cos(angles), jnp.sin(angles)

    normed, kraw, kv = call(
        functools.partial(kv_kernel, nf),
        [((rows, d), BF), ((rows, HEAD_DIM), F32), ((rows, 2 * HEAD_DIM), BF)],
        f_arr, tokens, gains, hg, cos, sin, *wkv,
        scratch=[pltpu.VMEM((d, 2 * HEAD_DIM), BF)], smem_first=True,
        flops=2 * rows * d * 2 * HEAD_DIM,
    )
    kv_all = gather_ctx(kv, nc)
    qraw, q = call(
        functools.partial(query_kernel, nf),
        [((HEADS, rows, HEAD_DIM), F32), ((HEADS, rows, HEAD_DIM), BF)],
        f_arr, normed, hg, cos, sin, *wq,
        scratch=[pltpu.VMEM((d, proj), BF)], smem_first=True, flops=2 * rows * d * proj,
    )
    att, att_low, tot = call(
        functools.partial(attend_kernel, tile),
        [((HEADS, rows, HEAD_DIM), F32), ((HEADS, rows, HEAD_DIM), BF), ((HEADS, rows, 1), F32)],
        q, kv_all, hg, qpos, kpos, flops=4 * rows * proj * seq,
    )
    ff_outs = call(
        functools.partial(ff_kernel, nf),
        [
            ((rows, d), BF),
            ((rows, 2 * d), BF),
            ((rows, d), BF),
            ((rows, d), F32),
            ((3, d), F32),
        ]
        + [((rows, 3 * width), BF)] * nf,
        tokens, cotangent, gains, att_low, *wo, *wg, *wu, *wd,
        scratch=[pltpu.VMEM((nf, rows, width), F32)] * 2, flops=2 * rows * d * width * nf * 8,
    )
    output, fg, gbl, resid, gg = ff_outs[:5]
    ex = ff_outs[5:]

    fg_all = gather_xor(fg, "fsdp", nf)
    ex_all = exchange_xor(ex, "fsdp", nf)
    gq, ghq, gkv = call(
        functools.partial(attend_back_kernel, nf, tile),
        [((rows, proj), BF), ((1, HEAD_DIM), F32), ((seq, 2 * HEAD_DIM), BF)],
        f_arr, gbl, att, tot, q, qraw, kv_all, hg, cos, sin, qpos, kpos, *wo,
        scratch=[
            pltpu.VMEM((HEADS * rows, HEAD_DIM), BF),
            pltpu.VMEM((HEADS, rows, 1), F32),
            pltpu.VMEM((HEADS, rows, HEAD_DIM), F32),
            pltpu.VMEM((HEADS * rows, tile), BF),
            pltpu.VMEM((HEADS * rows, tile), BF),
        ],
        smem_first=True, flops=10 * rows * proj * seq,
    )
    gkv_own = scatter_sum_ctx(gkv, nc)

    gu_part, down_part = call(
        functools.partial(ff_grad_kernel, nf),
        [((d, 2 * width), BF), ((width, d), BF)],
        *fg_all, *ex_all,
        scratch=[pltpu.VMEM((nf * rows, 2 * d), BF), pltpu.VMEM((nf * rows, 3 * width), BF)],
        flops=6 * nf * rows * d * width,
    )
    up_bits = [1 << i for i in range(nc.bit_length() - 1)]
    alt_bits = up_bits[1:2] + up_bits[:1] + up_bits[2:]
    gu = sum_ctx(gu_part, nc, c, up_bits)
    grad_down = sum_ctx(down_part, nc, c, alt_bits)

    def pair_grad(a, b, shape, extra=()):
        return call(
            functools.partial(pair_grad_kernel, nf, rows),
            [(shape, BF)] + list(extra),
            *a, *b,
            scratch=[
                pltpu.VMEM((nf * rows, shape[0]), BF),
                pltpu.VMEM((nf * rows, shape[1]), BF),
            ],
            flops=2 * nf * rows * shape[0] * shape[1],
        )

    att_cols = exchange_xor([att_low[k] for k in range(nf)], "fsdp", nf)
    gbl_all = gather_xor(gbl, "fsdp", nf)
    (out_part,) = pair_grad(att_cols, gbl_all, (proj // nf, d))
    grad_out = sum_ctx(out_part, nc, c, alt_bits)

    share = d // nf
    cols = exchange_xor(
        [lax.dynamic_slice_in_dim(normed, (f ^ k) * share, share, 1) for k in range(nf)], "fsdp", nf
    )
    gq_all = gather_xor(gq, "fsdp", nf)
    (q_part,) = pair_grad(cols, gq_all, (share, proj))
    grad_q = sum_ctx(q_part, nc, c, up_bits)

    pay, input_grad = call(
        functools.partial(input_back_kernel, nf),
        [((rows + 16, 2 * HEAD_DIM), BF), ((rows, d), F32)],
        f_arr, tokens, gkv_own, kraw, gq, resid, gains, hg, cos, sin, gg, ghq, *wq, *wkv,
        scratch=[pltpu.VMEM((d, proj), BF), pltpu.VMEM((d, 2 * HEAD_DIM), BF)],
        smem_first=True, flops=2 * rows * d * (proj + 2 * HEAD_DIM),
    )
    pay_all = gather_xor(pay, "fsdp", nf)
    kv_part, gain_part = pair_grad(
        cols, pay_all, (share, 2 * HEAD_DIM), [((16, 2 * HEAD_DIM), BF)]
    )
    grad_kv, gain_sum = sum_ctx_direct(kv_part, gain_part, nc, c)

    wide = 2 * HEAD_DIM
    norm_sum = jnp.concatenate([gain_sum[:4], gain_sum[4].reshape(4, -1)], axis=1)
    head_sum = gain_sum[5].reshape(2, HEAD_DIM)
    grad_gains = lax.dynamic_slice_in_dim(norm_sum, f * share, share, 1)
    grad_heads = lax.dynamic_slice_in_dim(head_sum, f * (HEAD_DIM // nf), HEAD_DIM // nf, 1)
    return (
        output,
        input_grad,
        grad_q,
        grad_kv[:, :HEAD_DIM],
        grad_kv[:, HEAD_DIM:],
        grad_out,
        gu[:, :width],
        gu[:, width:],
        grad_down,
        grad_gains,
        grad_heads,
    )


def solution(mesh):
    row = P(("ctx", "fsdp"), None)
    first, second = P("fsdp", None), P(None, "fsdp")
    body = functools.partial(layer, mesh.shape["fsdp"], mesh.shape["ctx"])
    return jax.shard_map(
        body,
        mesh=mesh,
        in_specs=(row, row, P(), first, first, first, first, second, second, first, second, second),
        out_specs=(row, row, first, first, first, first, second, second, first, second, second),
        check_vma=False,
    )
```

time: 957 us -> 296 us (0.31)
  blocking collectives: 311 us -> 0 us
  waiting for transfers between devices: 362 us -> 174 us
  loops' own time: 83.5 us -> 0 us
  starting transfers between devices: 0.86 us -> 75.1 us
  other arithmetic: 68.6 us -> 8.62 us
  matrix products: 51.7 us -> 0 us
  local copies, waits for them, and re-layouts: 58 us -> 16 us
  Pallas kernels: 0 us -> 19.4 us
  between operations: 16.4 us -> 1.64 us
    reduce_scatter x9 -> x0, waiting for transfers between devices: 336 us -> none  [the longest x1 62.9 us: shards(): lax.psum_scatter(grad_values, 'ctx', scatter_dimension=0, tiled=True)]
    psum x1 -> x0, blocking collectives: 222 us -> none  [shards(): lax.psum((share_query, share_key, share_value, share_out, share_gate, sha...]
    ppermute x0 -> x94, waiting for transfers between devices: none -> 174 us  [swap(): return lax.ppermute(x, axis, [(i, i ^ bit) for i in range(n)])]
    all_gather x6 -> x0, blocking collectives: 89.4 us -> none  [the longest x1 31.9 us: shards(): lax.all_gather(key_low, 'ctx', axis=0, tiled=True)]
    another operation x66 -> x0, loops' own time: 83.5 us -> none  [the longest x1 41 us: shards(): result_state, unused = lax.scan(forward_step, initial, items)]
    ppermute x0 -> x94, starting transfers between devices: none -> 75.1 us  [swap(): return lax.ppermute(x, axis, [(i, i ^ bit) for i in range(n)])]
    dot_general x134 -> x0, matrix products: 51.7 us -> none  [the longest x34 6.95 us: exponent(): jnp.einsum('qd,kd->qk', query_part, piece_key, preferred_element_type=jnp...]
    squeeze x32 -> x0, other arithmetic: 31.3 us -> none  [shards(): result_state, unused = lax.scan(forward_step, initial, items)]
  transfers between devices with their start and end apart: 16 -> 94, of which waited for: 10 -> 45; matrix products, arithmetic and copies ran while one was open for 9% -> 5% of each run, Pallas kernels for 0% -> 4%
where the time goes in v1:
time: 296 us; the launch traced here: 295 us
  waiting for transfers between devices  174 us (59%)
  starting transfers between devices  75.1 us (25%)
  Pallas kernels  19.4 us (7%)
  local copies, waits for them, and re-layouts  16 us (5%)
  other arithmetic  8.62 us (3%)
    ppermute x94, waiting for transfers between devices, swap(): return lax.ppermute(x, axis, [(i, i ^ bit) for i in range(n)])  174 us
    ppermute x94, starting transfers between devices, swap(): return lax.ppermute(x, axis, [(i, i ^ bit) for i in range(n)])  75.1 us
    pallas_call x10, Pallas kernels, call(): pl.pallas_call(kernel, out_shape=[jax.ShapeDtypeStruct(s, d) for s, d in...  19.4 us
    unnamed x69, local copies, waits for them, and re-layouts  6.45 us
  transfers between devices with their start and end apart: 94, of which 45 were waited for; matrix products, arithmetic and copies ran while one was open for 5% of the time, Pallas kernels for 4%

profile of v1, /device:TPU:0, one launch (start us, length us, event | category | flops | bytes accessed | tf_op | source)
XLA Modules:
  0.0 295.2 jit_solution(1326173571781001131)
XLA Ops:
  2.6 3.0 %collective-permute-start.1 = (bf16[6,128]{1,0:T(8,128)(2,1)S(1)}, bf16[6,128]{1,0:T(8,128)(2,1)S(1)}, u32[]{:S(2)}, u32[]{:S(2)}) collective-permute-start(bf16[6,128]{1,0:T(8,128)(2,1)S(1)} %bitcast.81), channel_id=1, source_target_pairs={{0,2},{1,3},{2,0},{3,1},{4,6},{5,7},{6,4},{7,5},{8,10},{9,11},{10,... | collective-permute-start | bytes 4616 | tf_op jit(solution)/shard_map/ppermute | solution.py:313
  19.1 2.3 collective-permute-done.7.rest_2_
  21.4 2.6 collective-permute-start.12
  25.3 2.7 collective-permute-done.17.rest_2_
  30.1 3.8 %collective-permute-done.12 = bf16[128,512]{1,0:T(8,128)(2,1)S(1)} collective-permute-done((bf16[128,512]{1,0:T(8,128)(2,1)S(1)}, bf16[128,512]{1,0:T(8,128)(2,1)S(1)}, u32[]{:S(2)}, u32[]{:S(2)}) %collective-permute-start.12) | collective-permute-done | bytes 131104 | tf_op jit(solution)/shard_map/ppermute | solution.py:313
  38.0 2.2 collective-permute-done.13
  44.9 8.6 %collective-permute-done.20.rest_6_ = bf16[640,512]{1,0:T(8,128)(2,1)} collective-permute-done((bf16[640,512]{1,0:T(8,128)(2,1)S(1)}, bf16[640,512]{1,0:T(8,128)(2,1)}, u32[]{:S(2)}, u32[]{:S(2)}) %collective-permute-start.20) | collective-permute-done | bytes 655392 | tf_op jit(solution)/shard_map/ppermute | solution.py:313
  53.6 14.0 %collective-permute-done.23.rest_10_ = bf16[640,512]{1,0:T(8,128)(2,1)} collective-permute-done((bf16[640,512]{1,0:T(8,128)(2,1)}, bf16[640,512]{1,0:T(8,128)(2,1)}, u32[]{:S(2)}, u32[]{:S(2)}) %collective-permute-start.23) | collective-permute-done | bytes 655392 | tf_op jit(solution)/shard_map/ppermute | solution.py:313
  67.6 13.6 %collective-permute-done.26.rest_14_ = bf16[512,640]{1,0:T(8,128)(2,1)} collective-permute-done((bf16[512,640]{1,0:T(8,128)(2,1)}, bf16[512,640]{1,0:T(8,128)(2,1)}, u32[]{:S(2)}, u32[]{:S(2)}) %collective-permute-start.26) | collective-permute-done | bytes 655392 | tf_op jit(solution)/shard_map/ppermute | solution.py:313
  85.5 7.9 %shard_map.206 = (bf16[128,640]{1,0:T(8,128)(2,1)}, bf16[128,1280]{1,0:T(8,128)(2,1)}, bf16[128,640]{1,0:T(8,128)(2,1)S(1)}, f32[128,640]{1,0:T(8,128)S(1)}, f32...) custom-call(bf16[128,640]{1,0:T(8,128)(2,1)S(1)} %copy-done.2, ...), custom_call_target="tpu_custom_call" | custom-call | flops 2684354560 | bytes 9775104 | tf_op jit(solution)/shard_map/pallas_call | solution.py:67
  94.4 4.0 %shard_map.207 = (bf16[128,1024]{1,0:T(8,128)(2,1)S(1)}, f32[1,256]{1,0:T(1,128)S(1)}, bf16[1024,512]{1,0:T(8,128)(2,1)S(1)}) custom-call(s32[1]{0:T(128)} %bitcast.3.f_ref, bf16[128,640]{1,0:T(8,128)(2,1)S(1)} %get-tuple-element.42.gbl.refs_4_, f32[4,128,256]{2,1,0:T(8,128)S(1)} %get-tuple-element.43.att, f32[4,128,1]{2,1,0:T(8,128)S(1)} %get-tuple-element.44.tot, ...), custom_call_target="tpu_custom_call" | custom-call | flops 1342177280 | bytes 3973636 | tf_op jit(solution)/shard_map/pallas_call | solution.py:67
  102.4 2.6 collective-permute-done.28
  107.8 1.9 collective-permute-done.32
  112.1 2.7 collective-permute-start.29
  119.9 8.0 %collective-permute-done.31 = bf16[128,512]{1,0:T(8,128)(2,1)S(1)} collective-permute-done((bf16[128,512]{1,0:T(8,128)(2,1)S(1)}, bf16[128,512]{1,0:T(8,128)(2,1)S(1)}, u32[]{:S(2)}, u32[]{:S(2)}) %collective-permute-start.31) | collective-permute-done | bytes 131104 | tf_op jit(solution)/shard_map/ppermute | solution.py:313
  130.3 5.8 %collective-permute-done.39.refs_6_ = bf16[128,1024]{1,0:T(8,128)(2,1)S(1)} collective-permute-done((bf16[128,1024]{1,0:T(8,128)(2,1)S(1)}, bf16[128,1024]{1,0:T(8,128)(2,1)S(1)}, u32[]{:S(2)}, u32[]{:S(2)}) %collective-permute-start.39) | collective-permute-done | bytes 262176 | tf_op jit(solution)/shard_map/ppermute | solution.py:313
  137.2 5.4 %collective-permute-done.48.refs_6_ = bf16[144,512]{1,0:T(8,128)(2,1)S(1)} collective-permute-done((bf16[144,512]{1,0:T(8,128)(2,1)S(1)}, bf16[144,512]{1,0:T(8,128)(2,1)S(1)}, u32[]{:S(2)}, u32[]{:S(2)}) %collective-permute-start.48) | collective-permute-done | bytes 147488 | tf_op jit(solution)/shard_map/ppermute | solution.py:313
  146.2 1.9 collective-permute-start.52
  149.4 2.7 collective-permute-start.54
  152.1 2.7 collective-permute-start.55
  159.1 2.4 collective-permute-done.56
  163.3 2.2 collective-permute-done.57
  165.5 3.8 %collective-permute-done.58 = bf16[20,512]{1,0:T(8,128)(2,1)S(1)} collective-permute-done((bf16[20,512]{1,0:T(8,128)(2,1)S(1)}, bf16[20,512]{1,0:T(8,128)(2,1)S(1)}, u32[]{:S(2)}, u32[]{:S(2)}) %collective-permute-start.58) | collective-permute-done | bytes 20512 | tf_op jit(solution)/shard_map/ppermute | solution.py:313
  169.3 4.7 %collective-permute-done.59 = bf16[20,512]{1,0:T(8,128)(2,1)S(1)} collective-permute-done((bf16[20,512]{1,0:T(8,128)(2,1)S(1)}, bf16[20,512]{1,0:T(8,128)(2,1)S(1)}, u32[]{:S(2)}, u32[]{:S(2)}) %collective-permute-start.59) | collective-permute-done | bytes 20512 | tf_op jit(solution)/shard_map/ppermute | solution.py:313
  174.0 4.7 %collective-permute-done.60 = bf16[20,512]{1,0:T(8,128)(2,1)S(1)} collective-permute-done((bf16[20,512]{1,0:T(8,128)(2,1)S(1)}, bf16[20,512]{1,0:T(8,128)(2,1)S(1)}, u32[]{:S(2)}, u32[]{:S(2)}) %collective-permute-start.60) | collective-permute-done | bytes 20512 | tf_op jit(solution)/shard_map/ppermute | solution.py:313
  179.0 5.3 %collective-permute-done.61 = bf16[20,512]{1,0:T(8,128)(2,1)S(1)} collective-permute-done((bf16[20,512]{1,0:T(8,128)(2,1)S(1)}, bf16[20,512]{1,0:T(8,128)(2,1)S(1)}, u32[]{:S(2)}, u32[]{:S(2)}) %collective-permute-start.61) | collective-permute-done | bytes 20512 | tf_op jit(solution)/shard_map/ppermute | solution.py:313
  185.7 4.3 %collective-permute-done.62 = bf16[20,512]{1,0:T(8,128)(2,1)S(1)} collective-permute-done((bf16[20,512]{1,0:T(8,128)(2,1)S(1)}, bf16[20,512]{1,0:T(8,128)(2,1)S(1)}, u32[]{:S(2)}, u32[]{:S(2)}) %collective-permute-start.62) | collective-permute-done | bytes 20512 | tf_op jit(solution)/shard_map/ppermute | solution.py:313
  191.7 4.8 %collective-permute-done.63 = bf16[20,512]{1,0:T(8,128)(2,1)S(1)} collective-permute-done((bf16[20,512]{1,0:T(8,128)(2,1)S(1)}, bf16[20,512]{1,0:T(8,128)(2,1)S(1)}, u32[]{:S(2)}, u32[]{:S(2)}) %collective-permute-start.63) | collective-permute-done | bytes 20512 | tf_op jit(solution)/shard_map/ppermute | solution.py:313
  197.3 4.3 %collective-permute-done.72 = bf16[32,640]{1,0:T(8,128)(2,1)S(1)} collective-permute-done((bf16[32,640]{1,0:T(8,128)(2,1)}, bf16[32,640]{1,0:T(8,128)(2,1)S(1)}, u32[]{:S(2)}, u32[]{:S(2)}) %collective-permute-start.72) | collective-permute-done | bytes 40992 | tf_op jit(solution)/shard_map/ppermute | solution.py:313
  203.0 4.6 %collective-permute-done.81.refs_7_ = bf16[128,1536]{1,0:T(8,128)(2,1)S(1)} collective-permute-done((bf16[128,1536]{1,0:T(8,128)(2,1)S(1)}, bf16[128,1536]{1,0:T(8,128)(2,1)S(1)}, u32[]{:S(2)}, u32[]{:S(2)}) %collective-permute-start.81) | collective-permute-done | bytes 393248 | tf_op jit(solution)/shard_map/ppermute | solution.py:313
  208.6 2.3 shard_map.212
  210.9 2.3 collective-permute-start.88
  215.7 6.5 %collective-permute-done.42 = bf16[40,1024]{1,0:T(8,128)(2,1)S(1)} collective-permute-done((bf16[40,1024]{1,0:T(8,128)(2,1)S(1)}, bf16[40,1024]{1,0:T(8,128)(2,1)S(1)}, u32[]{:S(2)}, u32[]{:S(2)}) %collective-permute-start.42) | collective-permute-done | bytes 81952 | tf_op jit(solution)/shard_map/ppermute | solution.py:313
  222.3 2.0 collective-permute-start.43
  224.4 6.8 %collective-permute-done.74 = bf16[64,640]{1,0:T(8,128)(2,1)S(1)} collective-permute-done((bf16[64,640]{1,0:T(8,128)(2,1)S(1)}, bf16[64,640]{1,0:T(8,128)(2,1)S(1)}, u32[]{:S(2)}, u32[]{:S(2)}) %collective-permute-start.74) | collective-permute-done | bytes 81952 | tf_op jit(solution)/shard_map/ppermute | solution.py:313
  232.5 1.8 collective-permute-start.75
  234.3 2.5 collective-permute-done.44
  237.2 1.9 collective-permute-done.75
  244.5 4.2 %collective-permute-done.89 = bf16[128,640]{1,0:T(8,128)(2,1)S(1)} collective-permute-done((bf16[128,640]{1,0:T(8,128)(2,1)S(1)}, bf16[128,640]{1,0:T(8,128)(2,1)S(1)}, u32[]{:S(2)}, u32[]{:S(2)}) %collective-permute-start.89) | collective-permute-done | bytes 163872 | tf_op jit(solution)/shard_map/ppermute | solution.py:313
  250.3 2.7 collective-permute-done.83
  254.9 4.5 %collective-permute-done.90 = bf16[64,640]{1,0:T(8,128)(2,1)S(1)} collective-permute-done((bf16[64,640]{1,0:T(8,128)(2,1)S(1)}, bf16[64,640]{1,0:T(8,128)(2,1)S(1)}, u32[]{:S(2)}, u32[]{:S(2)}) %collective-permute-start.90) | collective-permute-done | bytes 81952 | tf_op jit(solution)/shard_map/ppermute | solution.py:313
  259.6 6.0 %collective-permute-done.84 = bf16[80,1024]{1,0:T(8,128)(2,1)S(1)} collective-permute-done((bf16[80,1024]{1,0:T(8,128)(2,1)S(1)}, bf16[80,1024]{1,0:T(8,128)(2,1)S(1)}, u32[]{:S(2)}, u32[]{:S(2)}) %collective-permute-start.84) | collective-permute-done | bytes 163872 | tf_op jit(solution)/shard_map/ppermute | solution.py:313
  267.2 1.8 collective-permute-start.92
  269.0 4.6 %collective-permute-done.85 = bf16[80,1024]{1,0:T(8,128)(2,1)S(1)} collective-permute-done((bf16[80,1024]{1,0:T(8,128)(2,1)S(1)}, bf16[80,1024]{1,0:T(8,128)(2,1)S(1)}, u32[]{:S(2)}, u32[]{:S(2)}) %collective-permute-start.85) | collective-permute-done | bytes 163872 | tf_op jit(solution)/shard_map/ppermute | solution.py:313
  274.0 1.9 collective-permute-start.93
  275.9 6.1 %collective-permute-done.86 = bf16[160,1024]{1,0:T(8,128)(2,1)S(1)} collective-permute-done((bf16[160,1024]{1,0:T(8,128)(2,1)S(1)}, bf16[160,1024]{1,0:T(8,128)(2,1)S(1)}, u32[]{:S(2)}, u32[]{:S(2)}) %collective-permute-start.86) | collective-permute-done | bytes 327712 | tf_op jit(solution)/shard_map/ppermute | solution.py:313
  282.2 1.8 collective-permute-start.87
  286.8 6.1 %collective-permute-done.87 = bf16[320,1024]{1,0:T(8,128)(2,1)S(1)} collective-permute-done((bf16[320,1024]{1,0:T(8,128)(2,1)S(1)}, bf16[320,1024]{1,0:T(8,128)(2,1)S(1)}, u32[]{:S(2)}, u32[]{:S(2)}) %collective-permute-start.87) | collective-permute-done | bytes 655392 | tf_op jit(solution)/shard_map/ppermute | solution.py:313
  (322 shorter events, 88.2 us)
Async XLA Ops:
  2.6 9.0 %collective-permute-start.1 = (bf16[6,128]{1,0:T(8,128)(2,1)S(1)}, bf16[6,128]{1,0:T(8,128)(2,1)S(1)}, u32[]{:S(2)}, u32[]{:S(2)}) collective-permute-start(bf16[6,128]{1,0:T(8,128)(2,1)S(1)} %bitcast.81), channel_id=1, source_target_pairs={{0,2},{1,3},{2,0},{3,1},{4,6},{5,7},{6,4},{7,5},{8,10},{9,11},{10,... | collective-permute-start | bytes 4616 | tf_op jit(solution)/shard_map/ppermute | solution.py:313
  7.9 13.4 %collective-permute-start.7 = (bf16[160,1024]{1,0:T(8,128)(2,1)}, bf16[160,1024]{1,0:T(8,128)(2,1)S(1)}, u32[]{:S(2)}, u32[]{:S(2)}) collective-permute-start(bf16[160,1024]{1,0:T(8,128)(2,1)} %rest_0_.7), channel_id=1, source_target_pairs={{0,2},{1,3},{2,0},{3,1},{4,6},{5,7},{6,4},{7,5},{8,10},{9,11},{10,... | collective-permute-start | bytes 983048 | tf_op jit(solution)/shard_map/ppermute | solution.py:313
  11.7 12.2 %collective-permute-start.6 = (bf16[160,1024]{1,0:T(8,128)(2,1)}, bf16[160,1024]{1,0:T(8,128)(2,1)S(1)}, u32[]{:S(2)}, u32[]{:S(2)}) collective-permute-start(bf16[160,1024]{1,0:T(8,128)(2,1)} %rest_0_.7), channel_id=1, source_target_pairs={{0,1},{1,0},{2,3},{3,2},{4,5},{5,4},{6,7},{7,6},{8,9},{9,8},{10,11... | collective-permute-start | bytes 983048 | tf_op jit(solution)/shard_map/ppermute | solution.py:313
  12.8 15.2 %collective-permute-start.17 = (bf16[256,640]{1,0:T(8,128)(2,1)}, bf16[256,640]{1,0:T(8,128)(2,1)S(1)}, u32[]{:S(2)}, u32[]{:S(2)}) collective-permute-start(bf16[256,640]{1,0:T(8,128)(2,1)} %rest_0_.6), channel_id=1, source_target_pairs={{0,2},{1,3},{2,0},{3,1},{4,6},{5,7},{6,4},{7,5},{8,10},{9,11},{10,... | collective-permute-start | bytes 983048 | tf_op jit(solution)/shard_map/ppermute | solution.py:313
  14.4 21.5 %collective-permute-start.16 = (bf16[256,640]{1,0:T(8,128)(2,1)}, bf16[256,640]{1,0:T(8,128)(2,1)}, u32[]{:S(2)}, u32[]{:S(2)}) collective-permute-start(bf16[256,640]{1,0:T(8,128)(2,1)} %rest_0_.6), channel_id=1, source_target_pairs={{0,1},{1,0},{2,3},{3,2},{4,5},{5,4},{6,7},{7,6},{8,9},{9,8},{10,11... | collective-permute-start | bytes 983048 | tf_op jit(solution)/shard_map/ppermute | solution.py:313
  17.4 12.1 %collective-permute-start.10 = (bf16[128,512]{1,0:T(8,128)(2,1)S(1)}, bf16[128,512]{1,0:T(8,128)(2,1)S(1)}, u32[]{:S(2)}, u32[]{:S(2)}) collective-permute-start(bf16[128,512]{1,0:T(8,128)(2,1)S(1)} %get-tuple-element.39), channel_id=1, source_target_pairs={{0,8},{4,12},{8,0},{12,4},{16,24},{20,28},{24,16},{28,20},{1,9},{5... | collective-permute-start | bytes 393224 | tf_op jit(solution)/shard_map/ppermute | solution.py:313
  21.4 12.4 %collective-permute-start.12 = (bf16[128,512]{1,0:T(8,128)(2,1)S(1)}, bf16[128,512]{1,0:T(8,128)(2,1)S(1)}, u32[]{:S(2)}, u32[]{:S(2)}) collective-permute-start(bf16[128,512]{1,0:T(8,128)(2,1)S(1)} %get-tuple-element.39), channel_id=1, source_target_pairs={{0,16},{4,20},{8,24},{12,28},{16,0},{20,4},{24,8},{28,12},{1,17},{... | collective-permute-start | bytes 393224 | tf_op jit(solution)/shard_map/ppermute | solution.py:313
  24.0 11.3 %collective-permute-start.14 = (bf16[128,512]{1,0:T(8,128)(2,1)S(1)}, bf16[128,512]{1,0:T(8,128)(2,1)S(1)}, u32[]{:S(2)}, u32[]{:S(2)}) collective-permute-start(bf16[128,512]{1,0:T(8,128)(2,1)S(1)} %get-tuple-element.39), channel_id=1, source_target_pairs={{0,24},{4,28},{8,16},{12,20},{16,8},{20,12},{24,0},{28,4},{1,25},{... | collective-permute-start | bytes 393224 | tf_op jit(solution)/shard_map/ppermute | solution.py:313
  28.0 7.8 %collective-permute-start.9 = (bf16[128,512]{1,0:T(8,128)(2,1)S(1)}, bf16[128,512]{1,0:T(8,128)(2,1)}, u32[]{:S(2)}, u32[]{:S(2)}) collective-permute-start(bf16[128,512]{1,0:T(8,128)(2,1)S(1)} %get-tuple-element.39), channel_id=1, source_target_pairs={{0,4},{4,0},{8,12},{12,8},{16,20},{20,16},{24,28},{28,24},{1,5},{5... | collective-permute-start | bytes 393224 | tf_op jit(solution)/shard_map/ppermute | solution.py:313
  35.9 17.7 %collective-permute-start.20 = (bf16[640,512]{1,0:T(8,128)(2,1)S(1)}, bf16[640,512]{1,0:T(8,128)(2,1)}, u32[]{:S(2)}, u32[]{:S(2)}) collective-permute-start(bf16[640,512]{1,0:T(8,128)(2,1)S(1)} %copy-done.3), channel_id=1, source_target_pairs={{0,2},{1,3},{2,0},{3,1},{4,6},{5,7},{6,4},{7,5},{8,10},{9,11},{10,... | collective-permute-start | bytes 1966088 | tf_op jit(solution)/shard_map/ppermute | solution.py:313
  37.2 30.4 %collective-permute-start.23 = (bf16[640,512]{1,0:T(8,128)(2,1)}, bf16[640,512]{1,0:T(8,128)(2,1)}, u32[]{:S(2)}, u32[]{:S(2)}) collective-permute-start(bf16[640,512]{1,0:T(8,128)(2,1)} %rest_8_.1), channel_id=1, source_target_pairs={{0,2},{1,3},{2,0},{3,1},{4,6},{5,7},{6,4},{7,5},{8,10},{9,11},{10,... | collective-permute-start | bytes 1966088 | tf_op jit(solution)/shard_map/ppermute | solution.py:313
  40.2 41.0 %collective-permute-start.26 = (bf16[512,640]{1,0:T(8,128)(2,1)}, bf16[512,640]{1,0:T(8,128)(2,1)}, u32[]{:S(2)}, u32[]{:S(2)}) collective-permute-start(bf16[512,640]{1,0:T(8,128)(2,1)} %rest_12_.1), channel_id=1, source_target_pairs={{0,2},{1,3},{2,0},{3,1},{4,6},{5,7},{6,4},{7,5},{8,10},{9,11},{10,... | collective-permute-start | bytes 1966088 | tf_op jit(solution)/shard_map/ppermute | solution.py:313
  42.2 39.0 %collective-permute-start.19 = (bf16[640,512]{1,0:T(8,128)(2,1)S(1)}, bf16[640,512]{1,0:T(8,128)(2,1)}, u32[]{:S(2)}, u32[]{:S(2)}) collective-permute-start(bf16[640,512]{1,0:T(8,128)(2,1)S(1)} %copy-done.3), channel_id=1, source_target_pairs={{0,1},{1,0},{2,3},{3,2},{4,5},{5,4},{6,7},{7,6},{8,9},{9,8},{10,11... | collective-permute-start | bytes 1966088 | tf_op jit(solution)/shard_map/ppermute | solution.py:313
  44.8 39.2 %collective-permute-start.22 = (bf16[640,512]{1,0:T(8,128)(2,1)}, bf16[640,512]{1,0:T(8,128)(2,1)S(1)}, u32[]{:S(2)}, u32[]{:S(2)}) collective-permute-start(bf16[640,512]{1,0:T(8,128)(2,1)} %rest_8_.1), channel_id=1, source_target_pairs={{0,1},{1,0},{2,3},{3,2},{4,5},{5,4},{6,7},{7,6},{8,9},{9,8},{10,11... | collective-permute-start | bytes 1966088 | tf_op jit(solution)/shard_map/ppermute | solution.py:313
  53.6 30.4 %collective-permute-start.25 = (bf16[512,640]{1,0:T(8,128)(2,1)}, bf16[512,640]{1,0:T(8,128)(2,1)S(1)}, u32[]{:S(2)}, u32[]{:S(2)}) collective-permute-start(bf16[512,640]{1,0:T(8,128)(2,1)} %rest_12_.1), channel_id=1, source_target_pairs={{0,1},{1,0},{2,3},{3,2},{4,5},{5,4},{6,7},{7,6},{8,9},{9,8},{10,11... | collective-permute-start | bytes 1966088 | tf_op jit(solution)/shard_map/ppermute | solution.py:313
  67.6 16.4 %collective-permute-start.21 = (bf16[640,512]{1,0:T(8,128)(2,1)}, bf16[640,512]{1,0:T(8,128)(2,1)S(1)}, u32[]{:S(2)}, u32[]{:S(2)}) collective-permute-start(bf16[640,512]{1,0:T(8,128)(2,1)} %collective-permute-done.20.rest_6_), channel_id=1, source_target_pairs={{0,1},{1,0},{2,3},{3,2},{4,5},{5,4},{6,7},{7,6},{8,9},{9,8},{10,11... | collective-permute-start | bytes 1966088 | tf_op jit(solution)/shard_map/ppermute | solution.py:313
  94.1 15.6 %collective-permute-start.68 = (bf16[128,640]{1,0:T(8,128)(2,1)S(1)}, bf16[128,640]{1,0:T(8,128)(2,1)S(1)}, u32[]{:S(2)}, u32[]{:S(2)}) collective-permute-start(bf16[128,640]{1,0:T(8,128)(2,1)S(1)} %get-tuple-element.42.gbl.refs_4_), channel_id=1, source_target_pairs={{0,2},{1,3},{2,0},{3,1},{4,6},{5,7},{6,4},{7,5},{8,10},{9,11},{10,... | collective-permute-start | bytes 491528 | tf_op jit(solution)/shard_map/ppermute | solution.py:313
  100.7 9.1 %collective-permute-start.32 = (bf16[128,512]{1,0:T(8,128)(2,1)S(1)}, bf16[128,512]{1,0:T(8,128)(2,1)S(1)}, u32[]{:S(2)}, u32[]{:S(2)}) collective-permute-start(bf16[128,512]{1,0:T(8,128)(2,1)S(1)} %get-tuple-element.74), channel_id=1, source_target_pairs={{0,4},{4,0},{8,12},{12,8},{16,20},{20,16},{24,28},{28,24},{1,5},{5... | collective-permute-start | bytes 393224 | tf_op jit(solution)/shard_map/ppermute | solution.py:313
  102.3 8.0 %collective-permute-start.64 = (bf16[128,256]{1,0:T(8,128)(2,1)S(1)}, bf16[128,256]{1,0:T(8,128)(2,1)S(1)}, u32[]{:S(2)}, u32[]{:S(2)}) collective-permute-start(bf16[128,256]{1,0:T(8,128)(2,1)S(1)} %get-tuple-element.92), channel_id=1, source_target_pairs={{0,1},{1,0},{2,3},{3,2},{4,5},{5,4},{6,7},{7,6},{8,9},{9,8},{10,11... | collective-permute-start | bytes 196616 | tf_op jit(solution)/shard_map/ppermute | solution.py:313
  110.4 26.4 %collective-permute-start.35 = (bf16[128,160]{1,0:T(8,128)(2,1)S(1)}, bf16[128,160]{1,0:T(8,128)(2,1)S(1)}, u32[]{:S(2)}, u32[]{:S(2)}) collective-permute-start(bf16[128,160]{1,0:T(8,128)(2,1)S(1)} %get-tuple-element.110), channel_id=1, source_target_pairs={{0,1},{1,0},{2,3},{3,2},{4,5},{5,4},{6,7},{7,6},{8,9},{9,8},{10,11... | collective-permute-start | bytes 122888 | tf_op jit(solution)/shard_map/ppermute | solution.py:313
  114.8 13.1 %collective-permute-start.31 = (bf16[128,512]{1,0:T(8,128)(2,1)S(1)}, bf16[128,512]{1,0:T(8,128)(2,1)S(1)}, u32[]{:S(2)}, u32[]{:S(2)}) collective-permute-start(bf16[128,512]{1,0:T(8,128)(2,1)S(1)} %get-tuple-element.71), channel_id=1, source_target_pairs={{0,16},{4,20},{8,24},{12,28},{16,0},{20,4},{24,8},{28,12},{1,17},{... | collective-permute-start | bytes 393224 | tf_op jit(solution)/shard_map/ppermute | solution.py:313
  116.1 12.5 %collective-permute-start.33 = (bf16[128,512]{1,0:T(8,128)(2,1)S(1)}, bf16[128,512]{1,0:T(8,128)(2,1)S(1)}, u32[]{:S(2)}, u32[]{:S(2)}) collective-permute-start(bf16[128,512]{1,0:T(8,128)(2,1)S(1)} %get-tuple-element.70), channel_id=1, source_target_pairs={{0,8},{4,12},{8,0},{12,4},{16,24},{20,28},{24,16},{28,20},{1,9},{5... | collective-permute-start | bytes 393224 | tf_op jit(solution)/shard_map/ppermute | solution.py:313
  117.1 20.0 %collective-permute-start.36 = (bf16[128,160]{1,0:T(8,128)(2,1)S(1)}, bf16[128,160]{1,0:T(8,128)(2,1)S(1)}, u32[]{:S(2)}, u32[]{:S(2)}) collective-permute-start(bf16[128,160]{1,0:T(8,128)(2,1)S(1)} %get-tuple-element.109), channel_id=1, source_target_pairs={{0,2},{1,3},{2,0},{3,1},{4,6},{5,7},{6,4},{7,5},{8,10},{9,11},{10,... | collective-permute-start | bytes 122888 | tf_op jit(solution)/shard_map/ppermute | solution.py:313
  119.7 22.9 %collective-permute-start.37 = (bf16[128,160]{1,0:T(8,128)(2,1)S(1)}, bf16[128,160]{1,0:T(8,128)(2,1)S(1)}, u32[]{:S(2)}, u32[]{:S(2)}) collective-permute-start(bf16[128,160]{1,0:T(8,128)(2,1)S(1)} %get-tuple-element.108), channel_id=1, source_target_pairs={{0,3},{1,2},{2,1},{3,0},{4,7},{5,6},{6,5},{7,4},{8,11},{9,10},{10,... | collective-permute-start | bytes 122888 | tf_op jit(solution)/shard_map/ppermute | solution.py:313
  127.9 8.3 %collective-permute-start.39 = (bf16[128,1024]{1,0:T(8,128)(2,1)S(1)}, bf16[128,1024]{1,0:T(8,128)(2,1)S(1)}, u32[]{:S(2)}, u32[]{:S(2)}) collective-permute-start(bf16[128,1024]{1,0:T(8,128)(2,1)S(1)} %get-tuple-element.48.gq.refs_4_), channel_id=1, source_target_pairs={{0,2},{1,3},{2,0},{3,1},{4,6},{5,7},{6,4},{7,5},{8,10},{9,11},{10,... | collective-permute-start | bytes 786440 | tf_op jit(solution)/shard_map/ppermute | solution.py:313
  146.2 8.6 %collective-permute-start.51 = (bf16[36,512]{1,0:T(8,128)(2,1)S(1)}, bf16[36,512]{1,0:T(8,128)(2,1)S(1)}, u32[]{:S(2)}, u32[]{:S(2)}) collective-permute-start(bf16[36,512]{1,0:T(8,128)(2,1)S(1)} %get-tuple-element.119), channel_id=1, source_target_pairs={{0,8},{4,12},{8,0},{12,4},{16,24},{20,28},{24,16},{28,20},{1,9},{5... | collective-permute-start | bytes 110600 | tf_op jit(solution)/shard_map/ppermute | solution.py:313
  146.2 10.3 %collective-permute-start.52 = (bf16[36,512]{1,0:T(8,128)(2,1)S(1)}, bf16[36,512]{1,0:T(8,128)(2,1)S(1)}, u32[]{:S(2)}, u32[]{:S(2)}) collective-permute-start(bf16[36,512]{1,0:T(8,128)(2,1)S(1)} %get-tuple-element.120), channel_id=1, source_target_pairs={{0,12},{4,8},{8,4},{12,0},{16,28},{20,24},{24,20},{28,16},{1,13},{... | collective-permute-start | bytes 110600 | tf_op jit(solution)/shard_map/ppermute | solution.py:313
  148.1 9.9 %collective-permute-start.53 = (bf16[36,512]{1,0:T(8,128)(2,1)S(1)}, bf16[36,512]{1,0:T(8,128)(2,1)S(1)}, u32[]{:S(2)}, u32[]{:S(2)}) collective-permute-start(bf16[36,512]{1,0:T(8,128)(2,1)S(1)} %get-tuple-element.121), channel_id=1, source_target_pairs={{0,16},{4,20},{8,24},{12,28},{16,0},{20,4},{24,8},{28,12},{1,17},{... | collective-permute-start | bytes 110600 | tf_op jit(solution)/shard_map/ppermute | solution.py:313
  149.4 8.7 %collective-permute-start.54 = (bf16[36,512]{1,0:T(8,128)(2,1)S(1)}, bf16[36,512]{1,0:T(8,128)(2,1)S(1)}, u32[]{:S(2)}, u32[]{:S(2)}) collective-permute-start(bf16[36,512]{1,0:T(8,128)(2,1)S(1)} %get-tuple-element.122), channel_id=1, source_target_pairs={{0,20},{4,16},{8,28},{12,24},{16,4},{20,0},{24,12},{28,8},{1,21},{... | collective-permute-start | bytes 110600 | tf_op jit(solution)/shard_map/ppermute | solution.py:313
  156.5 40.7 %collective-permute-start.77 = (bf16[128,1280]{1,0:T(8,128)(2,1)}, bf16[128,1280]{1,0:T(8,128)(2,1)S(1)}, u32[]{:S(2)}, u32[]{:S(2)}) collective-permute-start(bf16[128,1280]{1,0:T(8,128)(2,1)} %get-tuple-element.56.refs_0_), channel_id=1, source_target_pairs={{0,2},{1,3},{2,0},{3,1},{4,6},{5,7},{6,4},{7,5},{8,10},{9,11},{10,... | collective-permute-start | bytes 983048 | tf_op jit(solution)/shard_map/ppermute | solution.py:313
  158.1 44.3 %collective-permute-start.76 = (bf16[128,1280]{1,0:T(8,128)(2,1)}, bf16[128,1280]{1,0:T(8,128)(2,1)S(1)}, u32[]{:S(2)}, u32[]{:S(2)}) collective-permute-start(bf16[128,1280]{1,0:T(8,128)(2,1)} %get-tuple-element.56.refs_0_), channel_id=1, source_target_pairs={{0,1},{1,0},{2,3},{3,2},{4,5},{5,4},{6,7},{7,6},{8,9},{9,8},{10,11... | collective-permute-start | bytes 983048 | tf_op jit(solution)/shard_map/ppermute | solution.py:313
  158.1 44.7 %collective-permute-start.79 = (bf16[128,1536]{1,0:T(8,128)(2,1)S(1)}, bf16[128,1536]{1,0:T(8,128)(2,1)S(1)}, u32[]{:S(2)}, u32[]{:S(2)}) collective-permute-start(bf16[128,1536]{1,0:T(8,128)(2,1)S(1)} %copy-done.9), channel_id=1, source_target_pairs={{0,1},{1,0},{2,3},{3,2},{4,5},{5,4},{6,7},{7,6},{8,9},{9,8},{10,11... | collective-permute-start | bytes 1179656 | tf_op jit(solution)/shard_map/ppermute | solution.py:313
  158.6 44.4 %collective-permute-start.80 = (bf16[128,1536]{1,0:T(8,128)(2,1)S(1)}, bf16[128,1536]{1,0:T(8,128)(2,1)S(1)}, u32[]{:S(2)}, u32[]{:S(2)}) collective-permute-start(bf16[128,1536]{1,0:T(8,128)(2,1)S(1)} %copy-done.7), channel_id=1, source_target_pairs={{0,2},{1,3},{2,0},{3,1},{4,6},{5,7},{6,4},{7,5},{8,10},{9,11},{10,... | collective-permute-start | bytes 1179656 | tf_op jit(solution)/shard_map/ppermute | solution.py:313
  197.3 10.3 %collective-permute-start.81 = (bf16[128,1536]{1,0:T(8,128)(2,1)S(1)}, bf16[128,1536]{1,0:T(8,128)(2,1)S(1)}, u32[]{:S(2)}, u32[]{:S(2)}) collective-permute-start(bf16[128,1536]{1,0:T(8,128)(2,1)S(1)} %get-tuple-element.60), channel_id=1, source_target_pairs={{0,3},{1,2},{2,1},{3,0},{4,7},{5,6},{6,5},{7,4},{8,11},{9,10},{10,... | collective-permute-start | bytes 1179656 | tf_op jit(solution)/shard_map/ppermute | solution.py:313
  202.4 12.5 %collective-permute-start.41 = (bf16[80,1024]{1,0:T(8,128)(2,1)S(1)}, bf16[80,1024]{1,0:T(8,128)(2,1)S(1)}, u32[]{:S(2)}, u32[]{:S(2)}) collective-permute-start(bf16[80,1024]{1,0:T(8,128)(2,1)S(1)} %copy-done.16), channel_id=1, source_target_pairs={{0,4},{4,0},{8,12},{12,8},{16,20},{20,16},{24,28},{28,24},{1,5},{5... | collective-permute-start | bytes 491528 | tf_op jit(solution)/shard_map/ppermute | solution.py:313
  202.8 12.1 %collective-permute-start.73 = (bf16[32,640]{1,0:T(8,128)(2,1)S(1)}, bf16[32,640]{1,0:T(8,128)(2,1)S(1)}, u32[]{:S(2)}, u32[]{:S(2)}) collective-permute-start(bf16[32,640]{1,0:T(8,128)(2,1)S(1)} %add_convert_fusion.14), channel_id=1, source_target_pairs={{0,16},{4,20},{8,24},{12,28},{16,0},{20,4},{24,8},{28,12},{1,17},{... | collective-permute-start | bytes 122888 | tf_op jit(solution)/shard_map/ppermute | solution.py:313
  210.9 32.2 %collective-permute-start.88 = (bf16[256,640]{1,0:T(8,128)(2,1)S(1)}, bf16[256,640]{1,0:T(8,128)(2,1)S(1)}, u32[]{:S(2)}, u32[]{:S(2)}) collective-permute-start(bf16[256,640]{1,0:T(8,128)(2,1)S(1)} %broadcast_select_fusion.5), channel_id=1, source_target_pairs={{0,8},{4,12},{8,0},{12,4},{16,24},{20,28},{24,16},{28,20},{1,9},{5... | collective-permute-start | bytes 983048 | tf_op jit(solution)/shard_map/ppermute | solution.py:313
  213.3 30.4 %collective-permute-start.82 = (bf16[320,1024]{1,0:T(8,128)(2,1)S(1)}, bf16[320,1024]{1,0:T(8,128)(2,1)S(1)}, u32[]{:S(2)}, u32[]{:S(2)}) collective-permute-start(bf16[320,1024]{1,0:T(8,128)(2,1)S(1)} %broadcast_select_fusion.2), channel_id=1, source_target_pairs={{0,4},{4,0},{8,12},{12,8},{16,20},{20,16},{24,28},{28,24},{1,5},{5... | collective-permute-start | bytes 1966088 | tf_op jit(solution)/shard_map/ppermute | solution.py:313
  215.1 16.0 %collective-permute-start.74 = (bf16[64,640]{1,0:T(8,128)(2,1)S(1)}, bf16[64,640]{1,0:T(8,128)(2,1)S(1)}, u32[]{:S(2)}, u32[]{:S(2)}) collective-permute-start(bf16[64,640]{1,0:T(8,128)(2,1)S(1)} %pad_maximum_fusion.15), channel_id=1, source_target_pairs={{0,4},{4,0},{8,12},{12,8},{16,20},{20,16},{24,28},{28,24},{1,5},{5... | collective-permute-start | bytes 245768 | tf_op jit(solution)/shard_map/ppermute | solution.py:313
  222.3 8.8 %collective-permute-start.43 = (bf16[20,1024]{1,0:T(8,128)(2,1)S(1)}, bf16[20,1024]{1,0:T(8,128)(2,1)S(1)}, u32[]{:S(2)}, u32[]{:S(2)}) collective-permute-start(bf16[20,1024]{1,0:T(8,128)(2,1)S(1)} %broadcast_select_fusion.32), channel_id=1, source_target_pairs={{0,16},{4,20},{8,24},{12,28},{16,0},{20,4},{24,8},{28,12},{1,17},{... | collective-permute-start | bytes 122888 | tf_op jit(solution)/shard_map/ppermute | solution.py:313
  241.4 42.6 %collective-permute-start.46 = (bf16[80,1024]{1,0:T(8,128)(2,1)S(1)}, bf16[80,1024]{1,0:T(8,128)(2,1)S(1)}, u32[]{:S(2)}, u32[]{:S(2)}) collective-permute-start(bf16[80,1024]{1,0:T(8,128)(2,1)S(1)} %pad_maximum_fusion.3), channel_id=1, source_target_pairs={{0,4},{4,0},{8,12},{12,8},{16,20},{20,16},{24,28},{28,24},{1,5},{5... | collective-permute-start | bytes 491528 | tf_op jit(solution)/shard_map/ppermute | solution.py:313
  244.1 8.9 %collective-permute-start.83 = (bf16[160,1024]{1,0:T(8,128)(2,1)S(1)}, bf16[160,1024]{1,0:T(8,128)(2,1)S(1)}, u32[]{:S(2)}, u32[]{:S(2)}) collective-permute-start(bf16[160,1024]{1,0:T(8,128)(2,1)S(1)} %broadcast_select_fusion.8), channel_id=1, source_target_pairs={{0,8},{4,12},{8,0},{12,4},{16,24},{20,28},{24,16},{28,20},{1,9},{5... | collective-permute-start | bytes 983048 | tf_op jit(solution)/shard_map/ppermute | solution.py:313
  248.8 10.7 %collective-permute-start.90 = (bf16[64,640]{1,0:T(8,128)(2,1)S(1)}, bf16[64,640]{1,0:T(8,128)(2,1)S(1)}, u32[]{:S(2)}, u32[]{:S(2)}) collective-permute-start(bf16[64,640]{1,0:T(8,128)(2,1)S(1)} %broadcast_select_fusion.23), channel_id=1, source_target_pairs={{0,16},{4,20},{8,24},{12,28},{16,0},{20,4},{24,8},{28,12},{1,17},{... | collective-permute-start | bytes 245768 | tf_op jit(solution)/shard_map/ppermute | solution.py:313
  253.2 12.4 %collective-permute-start.84 = (bf16[80,1024]{1,0:T(8,128)(2,1)S(1)}, bf16[80,1024]{1,0:T(8,128)(2,1)S(1)}, u32[]{:S(2)}, u32[]{:S(2)}) collective-permute-start(bf16[80,1024]{1,0:T(8,128)(2,1)S(1)} %broadcast_select_fusion.14), channel_id=1, source_target_pairs={{0,16},{4,20},{8,24},{12,28},{16,0},{20,4},{24,8},{28,12},{1,17},{... | collective-permute-start | bytes 491528 | tf_op jit(solution)/shard_map/ppermute | solution.py:313
  265.7 7.9 %collective-permute-start.85 = (bf16[80,1024]{1,0:T(8,128)(2,1)S(1)}, bf16[80,1024]{1,0:T(8,128)(2,1)S(1)}, u32[]{:S(2)}, u32[]{:S(2)}) collective-permute-start(bf16[80,1024]{1,0:T(8,128)(2,1)S(1)} %add_convert_fusion.4), channel_id=1, source_target_pairs={{0,16},{4,20},{8,24},{12,28},{16,0},{20,4},{24,8},{28,12},{1,17},{... | collective-permute-start | bytes 491528 | tf_op jit(solution)/shard_map/ppermute | solution.py:313
  273.6 8.4 %collective-permute-start.86 = (bf16[160,1024]{1,0:T(8,128)(2,1)S(1)}, bf16[160,1024]{1,0:T(8,128)(2,1)S(1)}, u32[]{:S(2)}, u32[]{:S(2)}) collective-permute-start(bf16[160,1024]{1,0:T(8,128)(2,1)S(1)} %pad_maximum_fusion.1), channel_id=1, source_target_pairs={{0,8},{4,12},{8,0},{12,4},{16,24},{20,28},{24,16},{28,20},{1,9},{5... | collective-permute-start | bytes 983048 | tf_op jit(solution)/shard_map/ppermute | solution.py:313
  274.0 11.5 %collective-permute-start.93 = (bf16[256,640]{1,0:T(8,128)(2,1)S(1)}, bf16[256,640]{1,0:T(8,128)(2,1)S(1)}, u32[]{:S(2)}, u32[]{:S(2)}) collective-permute-start(bf16[256,640]{1,0:T(8,128)(2,1)S(1)} %pad_maximum_fusion.2), channel_id=1, source_target_pairs={{0,8},{4,12},{8,0},{12,4},{16,24},{20,28},{24,16},{28,20},{1,9},{5... | collective-permute-start | bytes 983048 | tf_op jit(solution)/shard_map/ppermute | solution.py:313
  282.2 10.7 %collective-permute-start.87 = (bf16[320,1024]{1,0:T(8,128)(2,1)S(1)}, bf16[320,1024]{1,0:T(8,128)(2,1)S(1)}, u32[]{:S(2)}, u32[]{:S(2)}) collective-permute-start(bf16[320,1024]{1,0:T(8,128)(2,1)S(1)} %pad_maximum_fusion), channel_id=1, source_target_pairs={{0,4},{4,0},{8,12},{12,8},{16,20},{20,16},{24,28},{28,24},{1,5},{5... | collective-permute-start | bytes 1966088 | tf_op jit(solution)/shard_map/ppermute | solution.py:313
  (71 other events, 612.9 us)

commit v2 on v1

v2 whole, which is shorter than its diff:
```python
import functools
import math

import jax
import jax.numpy as jnp
from jax import lax
from jax.experimental import pallas as pl
from jax.experimental.pallas import tpu as pltpu
from jax.sharding import PartitionSpec as P

HEADS = 4
HEAD_DIM = 256
NORM_EPS = 1e-06
ROPE_BASE = 1000000.0
BF = jnp.bfloat16
F32 = jnp.float32
MIB = 1024 * 1024


def dot(a, b):
    return lax.dot_general(a, b, (((1,), (0,)), ((), ())), preferred_element_type=F32)


def dot_nt(a, b):
    return lax.dot_general(a, b, (((1,), (1,)), ((), ())), preferred_element_type=F32)


def dot_tn(a, b):
    return lax.dot_general(a, b, (((0,), (0,)), ((), ())), preferred_element_type=F32)


def unit(v):
    r = lax.rsqrt(jnp.mean(v * v, axis=-1, keepdims=True) + NORM_EPS)
    return v * r, r


def norm_back(c, u, r, g):
    cg = c * g
    grad = r * (cg - u * jnp.mean(cg * u, axis=-1, keepdims=True))
    return grad, jnp.sum(c * u, axis=0, keepdims=True)


def rotate(v, cos, sin):
    half = v.shape[-1] // 2
    a, b = v[:, :half], v[:, half:]
    return jnp.concatenate([a * cos - b * sin, b * cos + a * sin], axis=-1)


def rotate_back(v, cos, sin):
    half = v.shape[-1] // 2
    a, b = v[:, :half], v[:, half:]
    return jnp.concatenate([a * cos + b * sin, b * cos - a * sin], axis=-1)


def call(kernel, outs, *args, scratch=(), vmem=40, flops=0, smem_first=False):
    specs = [pl.BlockSpec(memory_space=pltpu.VMEM)] * len(args)
    if smem_first:
        specs[0] = pl.BlockSpec(memory_space=pltpu.SMEM)
    moved = sum(math.prod(a.shape) * a.dtype.itemsize for a in args)
    return pl.pallas_call(
        kernel,
        out_shape=[jax.ShapeDtypeStruct(s, d) for s, d in outs],
        in_specs=specs,
        out_specs=[pl.BlockSpec(memory_space=pltpu.VMEM)] * len(outs),
        scratch_shapes=list(scratch),
        compiler_params=pltpu.CompilerParams(vmem_limit_bytes=vmem * MIB),
        cost_estimate=pl.CostEstimate(flops=flops, bytes_accessed=moved, transcendentals=0),
    )(*args)


def bound_of(hg):
    peak = jnp.max(jnp.abs(hg[...]), axis=1, keepdims=True)
    return math.sqrt(HEAD_DIM) * peak[0:1, :] * peak[1:2, :]


def tile_loop(count, step):
    if count == 1:
        step(0)
    else:

        def body(t, carry):
            step(t)
            return carry

        lax.fori_loop(0, count, body, 0)


def tile_rows(t, tile, count):
    return pl.ds(pl.multiple_of(t * tile, tile), tile) if count > 1 else slice(None)


def front_kernel(nf, tile, f_ref, tok, gains, hg, cos, sin, qpos, kpos, *rest):
    blocks = rest[:nf]
    normed_o, kraw_o, kv_o, qraw_o, q_o, att_o, low_o, tot_o, w = rest[nf:]
    f = f_ref[0]
    share = w.shape[0] // nf
    rows = qpos.shape[0]
    proj = HEADS * HEAD_DIM
    scale = 1.0 / math.sqrt(HEAD_DIM)
    count = tok.shape[0] // tile
    bound = bound_of(hg)
    for k in range(nf):
        start = pl.multiple_of(jnp.bitwise_xor(f, k) * share, 16)
        w[pl.ds(start, share), :] = blocks[k][:share, :]

    def keys(t):
        part = tile_rows(t, tile, count)
        u, _ = unit(tok[part, :].astype(F32))
        normed = (u * gains[0:1, :]).astype(BF)
        normed_o[part, :] = normed
        out = dot(normed, w[:, proj:])
        key = out[:, :HEAD_DIM]
        kraw_o[part, :] = key
        u, _ = unit(key)
        kv_o[part, :HEAD_DIM] = rotate(u * hg[1:2, :], cos[part, :], sin[part, :]).astype(BF)
        kv_o[part, HEAD_DIM:] = out[:, HEAD_DIM:].astype(BF)

    tile_loop(count, keys)
    for h in range(HEADS):
        raw = dot(normed_o[:rows, :], w[:, h * HEAD_DIM : (h + 1) * HEAD_DIM])
        k = jnp.bitwise_xor(f, h)
        qraw_o[k] = raw
        u, _ = unit(raw)
        q_o[k] = rotate(u * hg[0:1, :], cos[:rows, :], sin[:rows, :]).astype(BF)
    for k in range(HEADS):

        def step(t, k=k):
            part = tile_rows(t, tile, count)
            raw = dot_nt(q_o[k], kv_o[part, :HEAD_DIM])
            allowed = kpos[:, part] <= qpos[...]
            terms = jnp.where(allowed, jnp.exp(raw * scale - bound), 0.0)
            total = jnp.sum(terms, axis=1, keepdims=True)
            num = dot(terms.astype(BF), kv_o[part, HEAD_DIM:])
            if count == 1:
                tot_o[k], att_o[k] = total, num
            else:
                tot_o[k] += total
                att_o[k] += num

        if count > 1:
            tot_o[k] = jnp.zeros_like(tot_o[k])
            att_o[k] = jnp.zeros_like(att_o[k])
        tile_loop(count, step)
        att = att_o[k] / tot_o[k]
        att_o[k] = att
        low_o[k] = att.astype(BF)


def mid_kernel(nf, tok, gains, att, *rest):
    wo = rest[:nf]
    branch_o, middle_o, ff_o = rest[nf:]
    branch = None
    for k in range(nf):
        term = dot(att[k], wo[k][...])
        branch = term if branch is None else branch + term
    branch_o[...] = branch
    u, _ = unit(branch)
    middle = tok[...].astype(F32) + u * gains[1:2, :]
    middle_o[...] = middle
    u, _ = unit(middle)
    ff_o[...] = (u * gains[2:3, :]).astype(BF)


def gelu_parts(v):
    t = jnp.tanh(0.7978845608028654 * (v + 0.044715 * v * v * v))
    half = 0.5 * (1.0 + t)
    slope = half + 0.5 * v * (1.0 - t * t) * 0.7978845608028654 * (1.0 + 3 * 0.044715 * v * v)
    return v * half, slope


def ff_kernel(mine, other, wg0, wu0, wd0, wg1, wu1, wd1, own_o, send_o, pack_o, hid_o, a_o, b_o):
    rows, d = mine.shape
    pack_o[:rows, :d] = mine[...]
    pack_o[rows:, :d] = other[...]
    x = pack_o[:, :d]
    mixed = None
    for i, (wg, wu, wd) in enumerate(((wg0, wu0, wd0), (wg1, wu1, wd1))):
        gate = dot(x, wg[...])
        up = dot(x, wu[...])
        value, slope = gelu_parts(gate)
        a_o[i] = value
        b_o[i] = up * slope
        hidden = (value * up).astype(BF)
        if i == 0:
            hid_o[...] = hidden
        else:
            pack_o[:, d:] = hidden
        term = dot(hidden, wd[...])
        mixed = term if mixed is None else mixed + term
    own_o[...] = mixed[:rows, :]
    send_o[...] = mixed[rows:, :].astype(BF)


def finish_kernel(own, got, middle, cot, gains, out_o, low_o, gain_o):
    u, r = unit(own[...] + got[...].astype(F32))
    out_o[...] = (middle[...] + u * gains[3:4, :]).astype(BF)
    grad, gain = norm_back(cot[...].astype(F32), u, r, gains[3:4, :])
    low_o[...] = grad.astype(BF)
    gain_o[...] = gain


def ff_back_kernel(
    mine, other, a, b, wg0, wu0, wd0, wg1, wu1, wd1, own_o, send_o, pack_o, gg_o
):
    rows, d = mine.shape
    width = wg0.shape[1]
    pack_o[:rows, :d] = mine[...]
    pack_o[rows:, :d] = other[...]
    c = pack_o[:, :d]
    total = None
    for i, (wg, wu, wd) in enumerate(((wg0, wu0, wd0), (wg1, wu1, wd1))):
        gh = dot_nt(c, wd[...])
        gg = (gh * b[i]).astype(BF)
        gu = (gh * a[i]).astype(BF)
        if i == 0:
            gg_o[:, :width] = gg
            gg_o[:, width:] = gu
        else:
            pack_o[:, d : d + width] = gg
            pack_o[:, d + width :] = gu
        term = dot_nt(gg, wg[...]) + dot_nt(gu, wu[...])
        total = term if total is None else total + term
    own_o[...] = total[:rows, :]
    send_o[...] = total[rows:, :].astype(BF)


def ff_grad_kernel(pack1, hid, got1, pack2, gg, got2, gu_o, down_o, x_s, h_s, c_s, g_s):
    rows = hid.shape[0]
    d = down_o.shape[1]
    width = down_o.shape[0]
    x_s[:rows, :] = pack1[:, :d]
    x_s[rows:, :] = got1[:, :d]
    h_s[:rows, :] = hid[...]
    h_s[rows:, :] = got1[:, d:]
    c_s[:rows, :] = pack2[:, :d]
    c_s[rows:, :] = got2[:, :d]
    g_s[:rows, :] = gg[...]
    g_s[rows:, :] = got2[:, d:]
    gu_o[...] = dot_tn(x_s[...], g_s[...]).astype(BF)
    down_o[...] = dot_tn(h_s[...], c_s[...]).astype(BF)


def back_kernel(
    nf, tile, f_ref, own, got, middle, branch, cot, gains, gain3, att, tot, q, qraw, kv, normed,
    kraw, hg, cos, sin, qpos, kpos, *rest,
):
    wo = rest[:nf]
    pack_o, resid_o, odd_o, even_o = rest[nf : nf + 4]
    kvw_o = rest[nf + 4 : 2 * nf + 4]
    sg_s, tg_s, acc, s_s, e_s, kvw_s = rest[2 * nf + 4 :]
    f = f_ref[0]
    scale = 1.0 / math.sqrt(HEAD_DIM)
    rows, d = cot.shape
    proj = HEADS * HEAD_DIM
    bound = bound_of(hg)
    count = kv.shape[0] // tile
    um, rm = unit(middle[...])
    grad, gain2 = norm_back(own[...] + got[...].astype(F32), um, rm, gains[2:3, :])
    grad_middle = cot[...].astype(F32) + grad
    resid_o[...] = grad_middle
    ub, rb = unit(branch[...])
    grad_branch, gain1 = norm_back(grad_middle, ub, rb, gains[1:2, :])
    gbl = grad_branch.astype(BF)
    pack_o[:rows, proj:] = gbl
    for k in range(HEADS):
        ga = dot_nt(gbl, wo[k][...])
        inv = 1.0 / tot[k]
        sg_s[k * rows : (k + 1) * rows, :] = (ga * inv).astype(BF)
        tg_s[k] = -jnp.sum(ga * att[k], axis=1, keepdims=True) * inv

    def step(t):
        part = tile_rows(t, tile, count)
        allowed = kpos[:, part] <= qpos[...]
        for k in range(HEADS):
            mine = slice(k * rows, (k + 1) * rows)
            raw = dot_nt(q[k], kv[part, :HEAD_DIM])
            terms = jnp.where(allowed, jnp.exp(raw * scale - bound), 0.0)
            e_s[mine, :] = terms.astype(BF)
            gp = dot_nt(sg_s[mine, :], kv[part, HEAD_DIM:])
            s = (terms * (gp + tg_s[k]) * scale).astype(BF)
            s_s[mine, :] = s
            term = dot(s, kv[part, :HEAD_DIM])
            if count == 1:
                acc[k] = term
            else:
                acc[k] += term
        queries = q[...].reshape(HEADS * rows, HEAD_DIM)
        c = rotate_back(dot_tn(s_s[...], queries), cos[part, :], sin[part, :])
        u, r = unit(kraw[part, :])
        gk, gain = norm_back(c, u, r, hg[1:2, :])
        gkl = gk.astype(BF)
        gvl = dot_tn(e_s[...], sg_s[...]).astype(BF)
        kk = dot_tn(normed[part, :], gkl)
        vv = dot_tn(normed[part, :], gvl)
        if count == 1:
            kvw_s[:d, :HEAD_DIM] = kk
            kvw_s[:d, HEAD_DIM:] = vv
            kvw_s[d : d + 1, :HEAD_DIM] = gain
        else:
            kvw_s[:d, :HEAD_DIM] += kk
            kvw_s[:d, HEAD_DIM:] += vv
            kvw_s[d : d + 1, :HEAD_DIM] += gain
        for j in range(tile // rows):
            out = even_o if j % 2 == 0 else odd_o
            start = (j // 2) * rows
            if count > 1:
                start = pl.multiple_of(t * (tile // 2) + start, rows)
            out[pl.ds(start, rows), :HEAD_DIM] = gkl[j * rows : (j + 1) * rows, :]
            out[pl.ds(start, rows), HEAD_DIM:] = gvl[j * rows : (j + 1) * rows, :]

    if count > 1:
        acc[...] = jnp.zeros_like(acc)
        kvw_s[...] = jnp.zeros_like(kvw_s)
    tile_loop(count, step)
    share = kvw_o[0].shape[0]
    for k in range(nf):
        start = pl.multiple_of(jnp.bitwise_xor(f, k) * share, 16)
        kvw_o[k][...] = kvw_s[pl.ds(start, share), :].astype(BF)
    gain = None
    for k in range(HEADS):
        u, r = unit(qraw[k])
        c = rotate_back(acc[k], cos[:rows, :], sin[:rows, :])
        grad, g = norm_back(c, u, r, hg[0:1, :])
        gain = g if gain is None else gain + g
        h = jnp.bitwise_xor(f, k)
        pack_o[:rows, pl.ds(pl.multiple_of(h * HEAD_DIM, HEAD_DIM), HEAD_DIM)] = grad.astype(BF)
    wide = pack_o.shape[1]
    first = jnp.concatenate([gain1, gain2, jnp.zeros((1, wide - 2 * d), F32)], axis=1)
    heads = jnp.concatenate([gain, kvw_s[d : d + 1, :HEAD_DIM]], axis=1)
    second = jnp.concatenate(
        [gain3[...], heads, jnp.zeros((1, wide - d - 2 * HEAD_DIM), F32)], axis=1
    )
    pad = jnp.zeros((pack_o.shape[0] - rows - 2, wide), F32)
    pack_o[rows:, :] = jnp.concatenate([first, second, pad], axis=0).astype(BF)


def attention_grad_kernel(nf, *refs):
    pack, cols, kvw = refs[:nf], refs[nf : 2 * nf], refs[2 * nf : 3 * nf]
    out_o, gain_o, g_s, b_s, a_s, n_s = refs[3 * nf :]
    rows = cols[0].shape[0]
    proj = HEADS * HEAD_DIM
    head = a_s.shape[1]
    share = n_s.shape[1]
    for k in range(nf):
        mine = slice(k * rows, (k + 1) * rows)
        g_s[mine, :] = pack[k][:rows, :proj]
        b_s[mine, :] = pack[k][:rows, proj:]
        a_s[mine, :] = cols[k][:, :head]
        n_s[mine, :] = cols[k][:, head : head + share]
    qw = dot_tn(n_s[...], g_s[...])
    half = proj // 2
    out_o[:share, :] = qw[:, :half].astype(BF)
    out_o[share : 2 * share, :] = qw[:, half:].astype(BF)
    total = kvw[0][...].astype(F32)
    gain = pack[0][rows:, :].astype(F32)
    for k in range(1, nf):
        total = total + kvw[k][...].astype(F32)
        gain = gain + pack[k][rows:, :].astype(F32)
    out_o[2 * share : 3 * share, :] = total.astype(BF)
    gain_o[...] = gain.astype(BF)
    ow = dot_tn(a_s[...], b_s[...])
    at = 3 * share
    out_o[at : at + head, :] = ow[:, :half].astype(BF)
    at += head
    quarter = head // 4
    strip = jnp.concatenate(
        [ow[i * quarter : (i + 1) * quarter, half:] for i in range(4)], axis=1
    )
    out_o[at : at + quarter, :] = strip.astype(BF)
    at += quarter
    out_o[at:, :] = jnp.zeros((out_o.shape[0] - at, half), BF)


def input_back_kernel(nf, f_ref, tok, gkv, pack, resid, gains, *rest):
    blocks, (grad_o, w) = rest[:nf], rest[nf:]
    f = f_ref[0]
    rows = tok.shape[0]
    share = w.shape[0] // nf
    proj = HEADS * HEAD_DIM
    for k in range(nf):
        start = pl.multiple_of(jnp.bitwise_xor(f, k) * share, 16)
        w[pl.ds(start, share), :] = blocks[k][:share, :]
    low = gkv[...].astype(BF)
    gn = dot_nt(pack[:rows, :proj], w[:, :proj]) + dot_nt(low, w[:, proj:])
    u, r = unit(tok[...].astype(F32))
    gx, _ = norm_back(gn, u, r, gains[0:1, :])
    grad_o[...] = resid[...] + gx


def swap(x, axis, n, bit):
    return lax.ppermute(x, axis, [(i, i ^ bit) for i in range(n)])


def gather_fsdp(x, n):
    far = swap(x, "fsdp", n, 2)
    both = swap(jnp.concatenate([x, far], axis=0), "fsdp", n, 1)
    rows = x.shape[0]
    return [x, both[:rows], far, both[rows:]]


def exchange_fsdp(blocks, n):
    return [b if k == 0 else swap(b, "fsdp", n, k) for k, b in enumerate(blocks)]


def gather_ctx(x, n):
    if n > 8:
        bit = 1
        while bit < n:
            x = jnp.concatenate([x, swap(x, "ctx", n, bit)], axis=0)
            bit *= 2
        return x
    far = {0: x}
    for k in range(n - 2, 0, -2):
        far[k] = swap(x, "ctx", n, k)
    have = {}
    for k in sorted(far):
        have[k] = far[k]
        have[k + 1] = swap(far[k], "ctx", n, 1)
    return jnp.concatenate([have[k] for k in range(n)], axis=0)


def scatter_sum_ctx(odd, even, n):
    x = even.astype(F32) + swap(odd, "ctx", n, 1).astype(F32)
    rows = x.shape[0] * 2 // n
    if n > 8:
        bit = n // 2
        while bit > 1:
            half = x.shape[0] // 2
            x = x[:half] + swap(x[half:].astype(BF), "ctx", n, bit).astype(F32)
            bit //= 2
        return x
    total = x[:rows]
    for k in range(n // 2 - 1, 0, -1):
        part = x[k * rows : (k + 1) * rows].astype(BF)
        total = total + swap(part, "ctx", n, 2 * k).astype(F32)
    return total


def sum_ctx(x, n, c, bits):
    if x.shape[0] % n:
        return lax.psum(x.astype(F32), "ctx")
    for bit in bits:
        half = x.shape[0] // 2
        upper = (c & bit) != 0
        keep = jnp.where(upper, x[half:], x[:half])
        send = jnp.where(upper, x[:half], x[half:])
        got = swap(send, "ctx", n, bit)
        x = (keep.astype(F32) + got.astype(F32)).astype(BF)
    for bit in reversed(bits):
        upper = (c & bit) != 0
        got = swap(x, "ctx", n, bit)
        x = jnp.concatenate([jnp.where(upper, got, x), jnp.where(upper, x, got)], axis=0)
    return x.astype(F32)


def sum_small(x, n):
    x = x.astype(F32)
    bit = 1
    while bit < n:
        x = x + swap(x.astype(BF), "ctx", n, bit).astype(F32)
        bit *= 2
    return x


def layer(
    nf,
    nc,
    tokens,
    cotangent,
    block_order,
    query_weight,
    key_weight,
    value_weight,
    out_weight,
    gate_weight,
    up_weight,
    down_weight,
    norm_gains,
    head_gains,
):
    rows, d = tokens.shape
    block_len = rows // 2
    f = lax.axis_index("fsdp")
    c = lax.axis_index("ctx")
    f_arr = f.reshape(1).astype(jnp.int32)
    seq = nc * rows
    tile = min(seq, 1024)
    proj = HEADS * HEAD_DIM
    width = gate_weight.shape[1]
    share = d // nf
    qkv = proj + 2 * HEAD_DIM
    hd = (HEADS, rows, HEAD_DIM)

    pack = jnp.concatenate([norm_gains.reshape(1, -1), head_gains.reshape(1, -1)], axis=1)
    pack = jnp.pad(pack, ((0, 15), (0, qkv - pack.shape[1])))
    weights = jnp.concatenate([query_weight, key_weight, value_weight], axis=1)
    wqkv = gather_fsdp(jnp.concatenate([weights, pack], axis=0), nf)
    tok_all = gather_ctx(tokens, nc)
    wo = gather_fsdp(out_weight, nf)
    own_ff = (gate_weight, up_weight, down_weight)
    next_ff = [swap(w, "fsdp", nf, 1) for w in own_ff]

    split = norm_gains.size
    rest = split + head_gains.size
    pack = jnp.concatenate([w[share : share + 1, :rest] for w in wqkv], axis=0).astype(F32)
    pack = jnp.take(pack, f ^ jnp.arange(nf), axis=0)
    gains = pack[:, :split].reshape(nf, 4, -1).transpose(1, 0, 2).reshape(4, d)
    hg = pack[:, split:].reshape(nf, 2, -1).transpose(1, 0, 2).reshape(2, HEAD_DIM)

    order = jnp.take(block_order.reshape(nc, 2), c ^ jnp.arange(nc), axis=0)
    pos = (order.reshape(-1, 1) * block_len + jnp.arange(block_len)[None, :]).reshape(seq)
    kpos = pos.reshape(1, seq)
    qpos = pos[:rows].reshape(rows, 1)
    inv_freq = ROPE_BASE ** (-2.0 * jnp.arange(HEAD_DIM // 2, dtype=F32) / HEAD_DIM)
    angles = pos.astype(F32)[:, None] * inv_freq[None, :]
    cos, sin = jnp.cos(angles), jnp.sin(angles)

    normed, kraw, kv, qraw, q, att, att_low, tot = call(
        functools.partial(front_kernel, nf, tile),
        [
            ((seq, d), BF), ((seq, HEAD_DIM), F32), ((seq, 2 * HEAD_DIM), BF),
            (hd, F32), (hd, BF), (hd, F32), (hd, BF), ((HEADS, rows, 1), F32),
        ],
        f_arr, tok_all, gains, hg, cos, sin, qpos, kpos, *wqkv,
        scratch=[pltpu.VMEM((d, qkv), BF)], smem_first=True, vmem=60,
        flops=4 * rows * proj * seq + 2 * seq * d * qkv,
    )
    branch, middle, ff_in = call(
        functools.partial(mid_kernel, nf),
        [((rows, d), F32), ((rows, d), F32), ((rows, d), BF)],
        tokens, gains, att_low, *wo, flops=2 * rows * d * proj,
    )
    cols = exchange_fsdp(
        [
            jnp.concatenate(
                [att_low[k], lax.dynamic_slice_in_dim(normed[:rows], (f ^ k) * share, share, 1)],
                axis=1,
            )
            for k in range(nf)
        ],
        nf,
    )
    two = 2 * rows
    own, send, pack1, hid, act, slope = call(
        ff_kernel,
        [
            ((rows, d), F32), ((rows, d), BF), ((two, d + width), BF), ((two, width), BF),
            ((2, two, width), F32), ((2, two, width), F32),
        ],
        ff_in, swap(ff_in, "fsdp", nf, 2), *own_ff, *next_ff, flops=6 * two * d * width * 2,
    )
    got1 = swap(pack1, "fsdp", nf, 1)
    output, gml, gain3 = call(
        finish_kernel,
        [((rows, d), BF), ((rows, d), BF), ((1, d), F32)],
        own, swap(send, "fsdp", nf, 2), middle, cotangent, gains,
    )
    own, send, pack2, gg = call(
        ff_back_kernel,
        [((rows, d), F32), ((rows, d), BF), ((two, d + 2 * width), BF), ((two, 2 * width), BF)],
        gml, swap(gml, "fsdp", nf, 2), act, slope, *own_ff, *next_ff,
        flops=6 * two * d * width * 2,
    )
    got2 = swap(pack2, "fsdp", nf, 1)
    back = call(
        functools.partial(back_kernel, nf, tile),
        [
            ((rows + 16, proj + d), BF),
            ((rows, d), F32),
            ((seq // 2, 2 * HEAD_DIM), BF),
            ((seq // 2, 2 * HEAD_DIM), BF),
        ]
        + [((share, 2 * HEAD_DIM), BF)] * nf,
        f_arr, own, swap(send, "fsdp", nf, 2), middle, branch, cotangent, gains, gain3, att, tot,
        q, qraw, kv, normed, kraw, hg, cos, sin, qpos, kpos, *wo,
        scratch=[
            pltpu.VMEM((HEADS * rows, HEAD_DIM), BF),
            pltpu.VMEM((HEADS, rows, 1), F32),
            pltpu.VMEM(hd, F32),
            pltpu.VMEM((HEADS * rows, tile), BF),
            pltpu.VMEM((HEADS * rows, tile), BF),
            pltpu.VMEM((d + 8, 2 * HEAD_DIM), F32),
        ],
        smem_first=True, vmem=60, flops=10 * rows * proj * seq,
    )
    pack3, resid, odd, even = back[:4]
    kvw = exchange_fsdp(back[4:], nf)
    pack_all = gather_fsdp(pack3, nf)
    gkv = scatter_sum_ctx(odd, even, nc)

    gu_part, down_part = call(
        ff_grad_kernel,
        [((d, 2 * width), BF), ((width, d), BF)],
        pack1, hid, got1, pack2, gg, got2,
        scratch=[
            pltpu.VMEM((2 * two, d), BF),
            pltpu.VMEM((2 * two, width), BF),
            pltpu.VMEM((2 * two, d), BF),
            pltpu.VMEM((2 * two, 2 * width), BF),
        ],
        flops=12 * two * d * width,
    )
    up_bits = [1 << i for i in range(nc.bit_length() - 1)]
    alt_bits = up_bits[1:2] + up_bits[:1] + up_bits[2:]
    gu = sum_ctx(gu_part, nc, c, up_bits)
    grad_down = sum_ctx(down_part, nc, c, alt_bits)

    (input_grad,) = call(
        functools.partial(input_back_kernel, nf),
        [((rows, d), F32)],
        f_arr, tokens, gkv, pack3, resid, gains, *wqkv,
        scratch=[pltpu.VMEM((d, qkv), BF)], smem_first=True, flops=2 * rows * d * qkv,
    )

    head = proj // nf
    half = proj // 2
    used = 3 * share + head + head // 4
    lines = -(-used // 128) * 128
    att_part, gain_part = call(
        functools.partial(attention_grad_kernel, nf),
        [((lines, half), BF), ((16, proj + d), BF)],
        *pack_all, *cols, *kvw,
        scratch=[
            pltpu.VMEM((nf * rows, proj), BF),
            pltpu.VMEM((nf * rows, d), BF),
            pltpu.VMEM((nf * rows, head), BF),
            pltpu.VMEM((nf * rows, share), BF),
        ],
        flops=2 * nf * rows * share * (proj + d),
    )
    total = sum_ctx(att_part, nc, c, alt_bits)
    gain_sum = sum_small(gain_part, nc)
    grad_q = jnp.concatenate([total[:share], total[share : 2 * share]], axis=1)
    grad_kv = total[2 * share : 3 * share]
    at = 3 * share
    strip = total[at + head : at + head + head // 4]
    piece = strip.shape[1] // 4
    strip = jnp.concatenate([strip[:, i * piece : (i + 1) * piece] for i in range(4)], axis=0)
    grad_out = jnp.concatenate([total[at : at + head], strip], axis=1)
    gain0 = jnp.sum(grad_q * query_weight.astype(F32), axis=1)
    gain0 += jnp.sum(
        grad_kv * jnp.concatenate([key_weight, value_weight], axis=1).astype(F32), axis=1
    )
    gain0 = gain0 / norm_gains[0].astype(F32)
    others = jnp.concatenate(
        [gain_sum[0:1, :d], gain_sum[0:1, d : 2 * d], gain_sum[1:2, :d]], axis=0
    )
    others = lax.dynamic_slice_in_dim(others, f * share, share, 1)
    heads = gain_sum[1, d : d + 2 * HEAD_DIM].reshape(2, HEAD_DIM)
    return (
        output,
        input_grad,
        grad_q,
        grad_kv[:, :HEAD_DIM],
        grad_kv[:, HEAD_DIM:],
        grad_out,
        gu[:, :width],
        gu[:, width:],
        grad_down,
        jnp.concatenate([gain0[None, :], others], axis=0),
        lax.dynamic_slice_in_dim(heads, f * (HEAD_DIM // nf), HEAD_DIM // nf, 1),
    )


def solution(mesh):
    row = P(("ctx", "fsdp"), None)
    first, second = P("fsdp", None), P(None, "fsdp")
    body = functools.partial(layer, mesh.shape["fsdp"], mesh.shape["ctx"])
    return jax.shard_map(
        body,
        mesh=mesh,
        in_specs=(row, row, P(), first, first, first, first, second, second, first, second, second),
        out_specs=(row, row, first, first, first, first, second, second, first, second, second),
        check_vma=False,
    )
```

time: 296 us -> 245 us (0.83)
  waiting for transfers between devices: 174 us -> 125 us
  starting transfers between devices: 75.1 us -> 52.8 us
  Pallas kernels: 19.4 us -> 28.7 us
  local copies, waits for them, and re-layouts: 16 us -> 23.9 us
  other arithmetic: 8.62 us -> 12.3 us
    ppermute x94 -> x53, waiting for transfers between devices: 174 us -> 125 us  [swap(): return lax.ppermute(x, axis, [(i, i ^ bit) for i in range(n)])]
    ppermute x94 -> x53, starting transfers between devices: 75.1 us -> 52.8 us  [swap(): return lax.ppermute(x, axis, [(i, i ^ bit) for i in range(n)])]
    pallas_call x10 -> x9, Pallas kernels: 19.4 us -> 28.7 us  [call(): pl.pallas_call(kernel, out_shape=[jax.ShapeDtypeStruct(s, d) for s, d in...]
    unnamed x69 -> x102, local copies, waits for them, and re-layouts: 6.45 us -> 12.1 us
  transfers between devices with their start and end apart: 94 -> 53, of which waited for: 45 -> 25; matrix products, arithmetic and copies ran while one was open for 5% -> 10% of each run, Pallas kernels for 4% -> 8%
where the time goes in v2:
time: 245 us; the launch traced here: 244 us
  waiting for transfers between devices  125 us (51%)
  starting transfers between devices  52.8 us (22%)
  Pallas kernels  28.7 us (12%)
  local copies, waits for them, and re-layouts  23.9 us (10%)
  other arithmetic  12.3 us (5%)
    ppermute x53, waiting for transfers between devices, swap(): return lax.ppermute(x, axis, [(i, i ^ bit) for i in range(n)])  125 us
    ppermute x53, starting transfers between devices, swap(): return lax.ppermute(x, axis, [(i, i ^ bit) for i in range(n)])  52.8 us
    pallas_call x9, Pallas kernels, call(): pl.pallas_call(kernel, out_shape=[jax.ShapeDtypeStruct(s, d) for s, d in...  28.7 us
    unnamed x102, local copies, waits for them, and re-layouts  12.1 us
  transfers between devices with their start and end apart: 53, of which 25 were waited for; matrix products, arithmetic and copies ran while one was open for 10% of the time, Pallas kernels for 8%

profile of v2, /device:TPU:0, one launch (start us, length us, event | category | flops | bytes accessed | tf_op | source)
XLA Modules:
  0.0 244.3 jit_solution(3346582946783367255)
XLA Ops:
  0.7 3.0 %collective-permute-start.2 = (bf16[128,640]{1,0:T(8,128)(2,1)}, bf16[128,640]{1,0:T(8,128)(2,1)S(1)}, u32[]{:S(2)}, u32[]{:S(2)}) collective-permute-start(bf16[128,640]{1,0:T(8,128)(2,1)} %tok.3), channel_id=1, source_target_pairs={{0,4},{4,0},{8,12},{12,8},{16,20},{20,16},{24,28},{28,24},{1,5},{5... | collective-permute-start | bytes 491528 | tf_op jit(solution)/shard_map/ppermute | solution.py:391
  3.7 1.6 collective-permute-start.3
  5.2 2.6 %collective-permute-start.5 = (bf16[128,640]{1,0:T(8,128)(2,1)}, bf16[128,640]{1,0:T(8,128)(2,1)}, u32[]{:S(2)}, u32[]{:S(2)}) collective-permute-start(bf16[128,640]{1,0:T(8,128)(2,1)} %tok.3), channel_id=1, source_target_pairs={{0,16},{4,20},{8,24},{12,28},{16,0},{20,4},{24,8},{28,12},{1,17},{... | collective-permute-start | bytes 491528 | tf_op jit(solution)/shard_map/ppermute | solution.py:391
  12.5 1.6 collective-permute-start
  15.1 3.1 %multiply_sine_fusion = (f32[1024,128]{1,0:T(8,128)}, f32[1024,128]{1,0:T(8,128)}) fusion(f32[128]{0:T(128)S(1)} %multiply_power_fusion, f32[1024]{0:T(1024)S(1)} %convert_element_type.154), kind=kLoop, calls=%fused_computation.9 | loop fusion | flops 131072 | bytes 1053184 | tf_op jit(solution)/shard_map/sin | solution.py:516
  20.2 7.5 %collective-permute-done.rest_2_ = bf16[176,1536]{1,0:T(8,128)(2,1)S(1)} collective-permute-done((bf16[176,1536]{1,0:T(8,128)(2,1)S(1)}, bf16[176,1536]{1,0:T(8,128)(2,1)S(1)}, u32[]{:S(2)}, u32[]{:S(2)}) %collective-permute-start) | collective-permute-done | bytes 540704 | tf_op jit(solution)/shard_map/ppermute | solution.py:391
  28.3 4.2 %collective-permute-done.9.rest_2_ = bf16[256,640]{1,0:T(8,128)(2,1)S(1)} collective-permute-done((bf16[256,640]{1,0:T(8,128)(2,1)S(1)}, bf16[256,640]{1,0:T(8,128)(2,1)S(1)}, u32[]{:S(2)}, u32[]{:S(2)}) %collective-permute-start.9) | collective-permute-done | bytes 327712 | tf_op jit(solution)/shard_map/ppermute | solution.py:391
  35.8 4.8 %collective-permute-done.6 = bf16[128,640]{1,0:T(8,128)(2,1)S(1)} collective-permute-done((bf16[128,640]{1,0:T(8,128)(2,1)}, bf16[128,640]{1,0:T(8,128)(2,1)S(1)}, u32[]{:S(2)}, u32[]{:S(2)}) %collective-permute-start.6) | collective-permute-done | bytes 163872 | tf_op jit(solution)/shard_map/ppermute | solution.py:391
  42.1 4.1 %collective-permute-done.8 = bf16[128,640]{1,0:T(8,128)(2,1)S(1)} collective-permute-done((bf16[128,640]{1,0:T(8,128)(2,1)}, bf16[128,640]{1,0:T(8,128)(2,1)S(1)}, u32[]{:S(2)}, u32[]{:S(2)}) %collective-permute-start.8) | collective-permute-done | bytes 163872 | tf_op jit(solution)/shard_map/ppermute | solution.py:391
  49.8 6.1 %shard_map.203 = (bf16[1024,640]{1,0:T(8,128)(2,1)}, f32[1024,256]{1,0:T(8,128)}, bf16[1024,512]{1,0:T(8,128)(2,1)}, f32[4,128,256]{2,1,0:T(8,128)}, bf16[4,128,...) custom-call(s32[1]{0:T(128)} %bitcast.2.f_ref, ...), custom_call_target="tpu_custom_call" | custom-call | flops 2550136832 | bytes 4538884 | tf_op jit(solution)/shard_map/pallas_call | solution.py:60
  57.5 1.6 collective-permute-start.11
  59.1 5.1 %collective-permute-done.11.other = bf16[128,640]{1,0:T(8,128)(2,1)S(1)} collective-permute-done((bf16[128,640]{1,0:T(8,128)(2,1)S(1)}, bf16[128,640]{1,0:T(8,128)(2,1)S(1)}, u32[]{:S(2)}, u32[]{:S(2)}) %collective-permute-start.11) | collective-permute-done | bytes 163872 | tf_op jit(solution)/shard_map/ppermute | solution.py:391
  64.2 3.6 %shard_map.205 = (f32[128,640]{1,0:T(8,128)S(1)}, bf16[128,640]{1,0:T(8,128)(2,1)S(1)}, bf16[256,1152]{1,0:T(8,128)(2,1)}, bf16[256,512]{1,0:T(8,128)(2,1)S(1)},...) custom-call(bf16[128,640]{1,0:T(8,128)(2,1)S(1)} %get-tuple-element.48.mine, ...), custom_call_target="tpu_custom_call" | custom-call | flops 1006632960 | bytes 4259840 | tf_op jit(solution)/shard_map/pallas_call | solution.py:60
  70.3 4.3 %collective-permute-done.15.got = bf16[128,640]{1,0:T(8,128)(2,1)S(1)} collective-permute-done((bf16[128,640]{1,0:T(8,128)(2,1)S(1)}, bf16[128,640]{1,0:T(8,128)(2,1)S(1)}, u32[]{:S(2)}, u32[]{:S(2)}) %collective-permute-start.15) | collective-permute-done | bytes 163872 | tf_op jit(solution)/shard_map/ppermute | solution.py:391
  76.1 1.5 collective-permute-start.16
  78.5 3.0 %collective-permute-done.16.other = bf16[128,640]{1,0:T(8,128)(2,1)} collective-permute-done((bf16[128,640]{1,0:T(8,128)(2,1)S(1)}, bf16[128,640]{1,0:T(8,128)(2,1)}, u32[]{:S(2)}, u32[]{:S(2)}) %collective-permute-start.16) | collective-permute-done | bytes 163872 | tf_op jit(solution)/shard_map/ppermute | solution.py:391
  83.6 3.7 %shard_map.207 = (f32[128,640]{1,0:T(8,128)S(1)}, bf16[128,640]{1,0:T(8,128)(2,1)S(1)}, bf16[256,1664]{1,0:T(8,128)(2,1)}, bf16[256,1024]{1,0:T(8,128)(2,1)S(1)}) custom-call(bf16[128,640]{1,0:T(8,128)(2,1)S(1)} %copy-done.28, bf16[128,640]{1,0:T(8,128)(2,1)} %collective-permute-done.16.other, f32[2,256,512]{2,1,0:T(8,128)S(1)} %get-tuple-element.54.a, ...), custom_call_target="tpu_custom_call" | custom-call | flops 1006632960 | bytes 6356992 | tf_op jit(solution)/shard_map/pallas_call | solution.py:60
  88.1 1.6 collective-permute-start.17
  90.4 3.9 %collective-permute-done.17.got = bf16[128,640]{1,0:T(8,128)(2,1)S(1)} collective-permute-done((bf16[128,640]{1,0:T(8,128)(2,1)S(1)}, bf16[128,640]{1,0:T(8,128)(2,1)S(1)}, u32[]{:S(2)}, u32[]{:S(2)}) %collective-permute-start.17) | collective-permute-done | bytes 163872 | tf_op jit(solution)/shard_map/ppermute | solution.py:391
  94.9 8.8 %shard_map.208 = (bf16[144,1664]{1,0:T(8,128)(2,1)}, f32[128,640]{1,0:T(8,128)}, bf16[512,512]{1,0:T(8,128)(2,1)}, bf16[512,512]{1,0:T(8,128)(2,1)}, bf16[160,51...) custom-call(s32[1]{0:T(128)} %bitcast.2.f_ref, ...), custom_call_target="tpu_custom_call" | custom-call | flops 1342177280 | bytes 8410116 | tf_op jit(solution)/shard_map/pallas_call | solution.py:60
  103.7 1.6 collective-permute-start.22
  106.0 2.6 %shard_map.211 = (bf16[640,1024]{1,0:T(8,128)(2,1)S(1)}, bf16[512,640]{1,0:T(8,128)(2,1)S(1)}) custom-call(bf16[256,1152]{1,0:T(8,128)(2,1)} %get-tuple-element.76.pack1, bf16[256,512]{1,0:T(8,128)(2,1)S(1)} %copy-done.33, bf16[256,1152]{1,0:T(8,128)(2,1)S(1)} %collective-permute-done.36.got1, bf16[256,1664]{1,0:T(8,128)(2,1)} %get-tuple-element.78.pack2, ...), custom_call_target="tpu_custom_call" | custom-call | flops 1006632960 | bytes 3670016 | tf_op jit(solution)/shard_map/pallas_call | solution.py:60
  109.4 6.7 %collective-permute-done.22.refs_2_ = bf16[144,1664]{1,0:T(8,128)(2,1)S(1)} collective-permute-done((bf16[144,1664]{1,0:T(8,128)(2,1)}, bf16[144,1664]{1,0:T(8,128)(2,1)S(1)}, u32[]{:S(2)}, u32[]{:S(2)}) %collective-permute-start.22) | collective-permute-done | bytes 479264 | tf_op jit(solution)/shard_map/ppermute | solution.py:391
  116.1 2.2 collective-permute-done.18
  120.0 3.5 %collective-permute-start.20 = (bf16[128,512]{1,0:T(8,128)(2,1)S(1)}, bf16[128,512]{1,0:T(8,128)(2,1)S(1)}, u32[]{:S(2)}, u32[]{:S(2)}) collective-permute-start(bf16[128,512]{1,0:T(8,128)(2,1)S(1)} %get-tuple-element.115), channel_id=1, source_target_pairs={{0,16},{4,20},{8,24},{12,28},{16,0},{20,4},{24,8},{28,12},{1,17},{... | collective-permute-start | bytes 393224 | tf_op jit(solution)/shard_map/ppermute | solution.py:391
  124.2 1.7 collective-permute-start.46
  126.0 10.5 %collective-permute-done.46 = bf16[64,640]{1,0:T(8,128)(2,1)S(1)} collective-permute-done((bf16[64,640]{1,0:T(8,128)(2,1)S(1)}, bf16[64,640]{1,0:T(8,128)(2,1)S(1)}, u32[]{:S(2)}, u32[]{:S(2)}) %collective-permute-start.46) | collective-permute-done | bytes 81952 | tf_op jit(solution)/shard_map/ppermute | solution.py:391
  138.9 1.7 shard_map.209
  140.5 5.5 %collective-permute-done.47 = bf16[64,640]{1,0:T(8,128)(2,1)S(1)} collective-permute-done((bf16[64,640]{1,0:T(8,128)(2,1)S(1)}, bf16[64,640]{1,0:T(8,128)(2,1)S(1)}, u32[]{:S(2)}, u32[]{:S(2)}) %collective-permute-start.47) | collective-permute-done | bytes 81952 | tf_op jit(solution)/shard_map/ppermute | solution.py:391
  147.2 3.8 %collective-permute-done.38 = bf16[320,1024]{1,0:T(8,128)(2,1)S(1)} collective-permute-done((bf16[320,1024]{1,0:T(8,128)(2,1)S(1)}, bf16[320,1024]{1,0:T(8,128)(2,1)S(1)}, u32[]{:S(2)}, u32[]{:S(2)}) %collective-permute-start.38) | collective-permute-done | bytes 655392 | tf_op jit(solution)/shard_map/ppermute | solution.py:391
  153.4 1.6 collective-permute-start.48
  155.0 3.9 %collective-permute-done.28.refs_10_ = bf16[160,512]{1,0:T(8,128)(2,1)S(1)} collective-permute-done((bf16[160,512]{1,0:T(8,128)(2,1)S(1)}, bf16[160,512]{1,0:T(8,128)(2,1)S(1)}, u32[]{:S(2)}, u32[]{:S(2)}) %collective-permute-start.28) | collective-permute-done | bytes 163872 | tf_op jit(solution)/shard_map/ppermute | solution.py:391
  159.0 1.8 collective-permute-done.29.refs_11_
  161.6 1.6 collective-permute-start.50
  163.3 3.0 %collective-permute-done.50 = bf16[16,1664]{1,0:T(8,128)(2,1)S(1)} collective-permute-done((bf16[16,1664]{1,0:T(8,128)(2,1)S(1)}, bf16[16,1664]{1,0:T(8,128)(2,1)S(1)}, u32[]{:S(2)}, u32[]{:S(2)}) %collective-permute-start.50) | collective-permute-done | bytes 53280 | tf_op jit(solution)/shard_map/ppermute | solution.py:391
  166.5 11.1 %collective-permute-done.51 = bf16[16,1664]{1,0:T(8,128)(2,1)S(1)} collective-permute-done((bf16[16,1664]{1,0:T(8,128)(2,1)S(1)}, bf16[16,1664]{1,0:T(8,128)(2,1)S(1)}, u32[]{:S(2)}, u32[]{:S(2)}) %collective-permute-start.51) | collective-permute-done | bytes 53280 | tf_op jit(solution)/shard_map/ppermute | solution.py:391
  178.8 1.9 collective-permute-start.49
  180.6 2.6 %collective-permute-done.52 = bf16[16,1664]{1,0:T(8,128)(2,1)S(1)} collective-permute-done((bf16[16,1664]{1,0:T(8,128)(2,1)S(1)}, bf16[16,1664]{1,0:T(8,128)(2,1)S(1)}, u32[]{:S(2)}, u32[]{:S(2)}) %collective-permute-start.52) | collective-permute-done | bytes 53280 | tf_op jit(solution)/shard_map/ppermute | solution.py:391
  184.3 9.6 %collective-permute-done.40 = bf16[80,1024]{1,0:T(8,128)(2,1)S(1)} collective-permute-done((bf16[80,1024]{1,0:T(8,128)(2,1)S(1)}, bf16[80,1024]{1,0:T(8,128)(2,1)S(1)}, u32[]{:S(2)}, u32[]{:S(2)}) %collective-permute-start.40) | collective-permute-done | bytes 163872 | tf_op jit(solution)/shard_map/ppermute | solution.py:391
  195.3 6.1 %collective-permute-done.41 = bf16[80,1024]{1,0:T(8,128)(2,1)S(1)} collective-permute-done((bf16[80,1024]{1,0:T(8,128)(2,1)S(1)}, bf16[80,1024]{1,0:T(8,128)(2,1)S(1)}, u32[]{:S(2)}, u32[]{:S(2)}) %collective-permute-start.41) | collective-permute-done | bytes 163872 | tf_op jit(solution)/shard_map/ppermute | solution.py:391
  201.6 1.9 collective-permute-start.32
  203.5 2.2 collective-permute-start.42
  207.5 3.1 %collective-permute-start.33 = (bf16[112,512]{1,0:T(8,128)(2,1)S(1)}, bf16[112,512]{1,0:T(8,128)(2,1)S(1)}, u32[]{:S(2)}, u32[]{:S(2)}) collective-permute-start(bf16[112,512]{1,0:T(8,128)(2,1)S(1)} %add_convert_fusion.7), channel_id=1, source_target_pairs={{0,16},{4,20},{8,24},{12,28},{16,0},{20,4},{24,8},{28,12},{1,17},{... | collective-permute-start | bytes 344072 | tf_op jit(solution)/shard_map/ppermute | solution.py:391
  210.5 3.4 %collective-permute-done.42 = bf16[160,1024]{1,0:T(8,128)(2,1)S(1)} collective-permute-done((bf16[160,1024]{1,0:T(8,128)(2,1)S(1)}, bf16[160,1024]{1,0:T(8,128)(2,1)S(1)}, u32[]{:S(2)}, u32[]{:S(2)}) %collective-permute-start.42) | collective-permute-done | bytes 327712 | tf_op jit(solution)/shard_map/ppermute | solution.py:391
  214.3 3.3 %collective-permute-start.34 = (bf16[224,512]{1,0:T(8,128)(2,1)S(1)}, bf16[224,512]{1,0:T(8,128)(2,1)S(1)}, u32[]{:S(2)}, u32[]{:S(2)}) collective-permute-start(bf16[224,512]{1,0:T(8,128)(2,1)S(1)} %pad_maximum_fusion.9), channel_id=1, source_target_pairs={{0,4},{4,0},{8,12},{12,8},{16,20},{20,16},{24,28},{28,24},{1,5},{5... | collective-permute-start | bytes 688136 | tf_op jit(solution)/shard_map/ppermute | solution.py:391
  218.8 11.6 %collective-permute-done.34 = bf16[224,512]{1,0:T(8,128)(2,1)S(1)} collective-permute-done((bf16[224,512]{1,0:T(8,128)(2,1)S(1)}, bf16[224,512]{1,0:T(8,128)(2,1)S(1)}, u32[]{:S(2)}, u32[]{:S(2)}) %collective-permute-start.34) | collective-permute-done | bytes 229408 | tf_op jit(solution)/shard_map/ppermute | solution.py:391
  232.4 1.7 fusion.11
  234.1 4.9 %collective-permute-done.35 = bf16[448,512]{1,0:T(8,128)(2,1)S(1)} collective-permute-done((bf16[448,512]{1,0:T(8,128)(2,1)S(1)}, bf16[448,512]{1,0:T(8,128)(2,1)S(1)}, u32[]{:S(2)}, u32[]{:S(2)}) %collective-permute-start.35) | collective-permute-done | bytes 458784 | tf_op jit(solution)/shard_map/ppermute | solution.py:391
  (278 shorter events, 52.2 us)
Async XLA Ops:
  0.7 27.5 %collective-permute-start.2 = (bf16[128,640]{1,0:T(8,128)(2,1)}, bf16[128,640]{1,0:T(8,128)(2,1)S(1)}, u32[]{:S(2)}, u32[]{:S(2)}) collective-permute-start(bf16[128,640]{1,0:T(8,128)(2,1)} %tok.3), channel_id=1, source_target_pairs={{0,4},{4,0},{8,12},{12,8},{16,20},{20,16},{24,28},{28,24},{1,5},{5... | collective-permute-start | bytes 491528 | tf_op jit(solution)/shard_map/ppermute | solution.py:391
  3.7 16.0 %collective-permute-start.3 = (bf16[128,640]{1,0:T(8,128)(2,1)}, bf16[128,640]{1,0:T(8,128)(2,1)}, u32[]{:S(2)}, u32[]{:S(2)}) collective-permute-start(bf16[128,640]{1,0:T(8,128)(2,1)} %tok.3), channel_id=1, source_target_pairs={{0,8},{4,12},{8,0},{12,4},{16,24},{20,28},{24,16},{28,20},{1,9},{5... | collective-permute-start | bytes 491528 | tf_op jit(solution)/shard_map/ppermute | solution.py:391
  5.2 28.4 %collective-permute-start.5 = (bf16[128,640]{1,0:T(8,128)(2,1)}, bf16[128,640]{1,0:T(8,128)(2,1)}, u32[]{:S(2)}, u32[]{:S(2)}) collective-permute-start(bf16[128,640]{1,0:T(8,128)(2,1)} %tok.3), channel_id=1, source_target_pairs={{0,16},{4,20},{8,24},{12,28},{16,0},{20,4},{24,8},{28,12},{1,17},{... | collective-permute-start | bytes 491528 | tf_op jit(solution)/shard_map/ppermute | solution.py:391
  7.8 27.9 %collective-permute-start.7 = (bf16[128,640]{1,0:T(8,128)(2,1)}, bf16[128,640]{1,0:T(8,128)(2,1)}, u32[]{:S(2)}, u32[]{:S(2)}) collective-permute-start(bf16[128,640]{1,0:T(8,128)(2,1)} %tok.3), channel_id=1, source_target_pairs={{0,24},{4,28},{8,16},{12,20},{16,8},{20,12},{24,0},{28,4},{1,25},{... | collective-permute-start | bytes 491528 | tf_op jit(solution)/shard_map/ppermute | solution.py:391
  12.5 15.3 %collective-permute-start = (bf16[176,1536]{1,0:T(8,128)(2,1)S(1)}, bf16[176,1536]{1,0:T(8,128)(2,1)S(1)}, u32[]{:S(2)}, u32[]{:S(2)}) collective-permute-start(bf16[176,1536]{1,0:T(8,128)(2,1)S(1)} %pad_maximum_fusion.5.rest_0_), channel_id=1, source_target_pairs={{0,2},{1,3},{2,0},{3,1},{4,6},{5,7},{6,4},{7,5},{8,10},{9,11},{10,... | collective-permute-start | bytes 1622024 | tf_op jit(solution)/shard_map/ppermute | solution.py:391
  19.6 12.9 %collective-permute-start.9 = (bf16[256,640]{1,0:T(8,128)(2,1)S(1)}, bf16[256,640]{1,0:T(8,128)(2,1)S(1)}, u32[]{:S(2)}, u32[]{:S(2)}) collective-permute-start(bf16[256,640]{1,0:T(8,128)(2,1)S(1)} %copy-done.1), channel_id=1, source_target_pairs={{0,2},{1,3},{2,0},{3,1},{4,6},{5,7},{6,4},{7,5},{8,10},{9,11},{10,... | collective-permute-start | bytes 983048 | tf_op jit(solution)/shard_map/ppermute | solution.py:391
  27.8 6.4 %collective-permute-start.4 = (bf16[128,640]{1,0:T(8,128)(2,1)}, bf16[128,640]{1,0:T(8,128)(2,1)S(1)}, u32[]{:S(2)}, u32[]{:S(2)}) collective-permute-start(bf16[128,640]{1,0:T(8,128)(2,1)} %collective-permute-done.3), channel_id=1, source_target_pairs={{0,4},{4,0},{8,12},{12,8},{16,20},{20,16},{24,28},{28,24},{1,5},{5... | collective-permute-start | bytes 491528 | tf_op jit(solution)/shard_map/ppermute | solution.py:391
  28.2 18.1 %collective-permute-start.1 = (bf16[352,1536]{1,0:T(8,128)(2,1)S(1)}, bf16[352,1536]{1,0:T(8,128)(2,1)S(1)}, u32[]{:S(2)}, u32[]{:S(2)}) collective-permute-start(bf16[352,1536]{1,0:T(8,128)(2,1)S(1)} %pad_maximum_fusion), channel_id=1, source_target_pairs={{0,1},{1,0},{2,3},{3,2},{4,5},{5,4},{6,7},{7,6},{8,9},{9,8},{10,11... | collective-permute-start | bytes 3244040 | tf_op jit(solution)/shard_map/ppermute | solution.py:391
  32.6 13.6 %collective-permute-start.10 = (bf16[512,640]{1,0:T(8,128)(2,1)S(1)}, bf16[512,640]{1,0:T(8,128)(2,1)S(1)}, u32[]{:S(2)}, u32[]{:S(2)}) collective-permute-start(bf16[512,640]{1,0:T(8,128)(2,1)S(1)} %pad_maximum_fusion.2), channel_id=1, source_target_pairs={{0,1},{1,0},{2,3},{3,2},{4,5},{5,4},{6,7},{7,6},{8,9},{9,8},{10,11... | collective-permute-start | bytes 1966088 | tf_op jit(solution)/shard_map/ppermute | solution.py:391
  33.6 25.5 %collective-permute-start.12 = (bf16[640,512]{1,0:T(8,128)(2,1)S(1)}, bf16[640,512]{1,0:T(8,128)(2,1)}, u32[]{:S(2)}, u32[]{:S(2)}) collective-permute-start(bf16[640,512]{1,0:T(8,128)(2,1)S(1)} %copy-done.5), channel_id=1, source_target_pairs={{0,1},{1,0},{2,3},{3,2},{4,5},{5,4},{6,7},{7,6},{8,9},{9,8},{10,11... | collective-permute-start | bytes 1966088 | tf_op jit(solution)/shard_map/ppermute | solution.py:391
  34.2 6.4 %collective-permute-start.6 = (bf16[128,640]{1,0:T(8,128)(2,1)}, bf16[128,640]{1,0:T(8,128)(2,1)S(1)}, u32[]{:S(2)}, u32[]{:S(2)}) collective-permute-start(bf16[128,640]{1,0:T(8,128)(2,1)} %collective-permute-done.5), channel_id=1, source_target_pairs={{0,4},{4,0},{8,12},{12,8},{16,20},{20,16},{24,28},{28,24},{1,5},{5... | collective-permute-start | bytes 491528 | tf_op jit(solution)/shard_map/ppermute | solution.py:391
  35.7 23.4 %collective-permute-start.13 = (bf16[640,512]{1,0:T(8,128)(2,1)S(1)}, bf16[640,512]{1,0:T(8,128)(2,1)}, u32[]{:S(2)}, u32[]{:S(2)}) collective-permute-start(bf16[640,512]{1,0:T(8,128)(2,1)S(1)} %copy-done.6), channel_id=1, source_target_pairs={{0,1},{1,0},{2,3},{3,2},{4,5},{5,4},{6,7},{7,6},{8,9},{9,8},{10,11... | collective-permute-start | bytes 1966088 | tf_op jit(solution)/shard_map/ppermute | solution.py:391
  46.2 13.0 %collective-permute-start.14 = (bf16[512,640]{1,0:T(8,128)(2,1)S(1)}, bf16[512,640]{1,0:T(8,128)(2,1)}, u32[]{:S(2)}, u32[]{:S(2)}) collective-permute-start(bf16[512,640]{1,0:T(8,128)(2,1)S(1)} %copy-done.7), channel_id=1, source_target_pairs={{0,1},{1,0},{2,3},{3,2},{4,5},{5,4},{6,7},{7,6},{8,9},{9,8},{10,11... | collective-permute-start | bytes 1966088 | tf_op jit(solution)/shard_map/ppermute | solution.py:391
  57.5 6.7 %collective-permute-start.11 = (bf16[128,640]{1,0:T(8,128)(2,1)S(1)}, bf16[128,640]{1,0:T(8,128)(2,1)S(1)}, u32[]{:S(2)}, u32[]{:S(2)}) collective-permute-start(bf16[128,640]{1,0:T(8,128)(2,1)S(1)} %get-tuple-element.48.mine), channel_id=1, source_target_pairs={{0,2},{1,3},{2,0},{3,1},{4,6},{5,7},{6,4},{7,5},{8,10},{9,11},{10,... | collective-permute-start | bytes 491528 | tf_op jit(solution)/shard_map/ppermute | solution.py:391
  68.8 5.8 %collective-permute-start.15 = (bf16[128,640]{1,0:T(8,128)(2,1)S(1)}, bf16[128,640]{1,0:T(8,128)(2,1)S(1)}, u32[]{:S(2)}, u32[]{:S(2)}) collective-permute-start(bf16[128,640]{1,0:T(8,128)(2,1)S(1)} %get-tuple-element.50), channel_id=1, source_target_pairs={{0,2},{1,3},{2,0},{3,1},{4,6},{5,7},{6,4},{7,5},{8,10},{9,11},{10,... | collective-permute-start | bytes 491528 | tf_op jit(solution)/shard_map/ppermute | solution.py:391
  87.3 18.6 %collective-permute-start.37 = (bf16[256,1664]{1,0:T(8,128)(2,1)}, bf16[256,1664]{1,0:T(8,128)(2,1)S(1)}, u32[]{:S(2)}, u32[]{:S(2)}) collective-permute-start(bf16[256,1664]{1,0:T(8,128)(2,1)} %get-tuple-element.78.pack2), channel_id=1, source_target_pairs={{0,1},{1,0},{2,3},{3,2},{4,5},{5,4},{6,7},{7,6},{8,9},{9,8},{10,11... | collective-permute-start | bytes 2555912 | tf_op jit(solution)/shard_map/ppermute | solution.py:391
  87.4 18.6 %collective-permute-start.36 = (bf16[256,1152]{1,0:T(8,128)(2,1)}, bf16[256,1152]{1,0:T(8,128)(2,1)S(1)}, u32[]{:S(2)}, u32[]{:S(2)}) collective-permute-start(bf16[256,1152]{1,0:T(8,128)(2,1)} %get-tuple-element.76.pack1), channel_id=1, source_target_pairs={{0,1},{1,0},{2,3},{3,2},{4,5},{5,4},{6,7},{7,6},{8,9},{9,8},{10,11... | collective-permute-start | bytes 1769480 | tf_op jit(solution)/shard_map/ppermute | solution.py:391
  88.1 6.2 %collective-permute-start.17 = (bf16[128,640]{1,0:T(8,128)(2,1)S(1)}, bf16[128,640]{1,0:T(8,128)(2,1)S(1)}, u32[]{:S(2)}, u32[]{:S(2)}) collective-permute-start(bf16[128,640]{1,0:T(8,128)(2,1)S(1)} %get-tuple-element.57), channel_id=1, source_target_pairs={{0,2},{1,3},{2,0},{3,1},{4,6},{5,7},{6,4},{7,5},{8,10},{9,11},{10,... | collective-permute-start | bytes 491528 | tf_op jit(solution)/shard_map/ppermute | solution.py:391
  90.3 61.1 %collective-permute-start.24 = (bf16[128,416]{1,0:T(8,128)(2,1)}, bf16[128,416]{1,0:T(8,128)(2,1)S(1)}, u32[]{:S(2)}, u32[]{:S(2)}) collective-permute-start(bf16[128,416]{1,0:T(8,128)(2,1)} %pad_maximum_fusion.12), channel_id=1, source_target_pairs={{0,1},{1,0},{2,3},{3,2},{4,5},{5,4},{6,7},{7,6},{8,9},{9,8},{10,11... | collective-permute-start | bytes 319496 | tf_op jit(solution)/shard_map/ppermute | solution.py:391
  103.7 12.3 %collective-permute-start.22 = (bf16[144,1664]{1,0:T(8,128)(2,1)}, bf16[144,1664]{1,0:T(8,128)(2,1)S(1)}, u32[]{:S(2)}, u32[]{:S(2)}) collective-permute-start(bf16[144,1664]{1,0:T(8,128)(2,1)} %get-tuple-element.69.pack.refs_0_), channel_id=1, source_target_pairs={{0,2},{1,3},{2,0},{3,1},{4,6},{5,7},{6,4},{7,5},{8,10},{9,11},{10,... | collective-permute-start | bytes 1437704 | tf_op jit(solution)/shard_map/ppermute | solution.py:391
  105.3 13.0 %collective-permute-start.18 = (bf16[512,512]{1,0:T(8,128)(2,1)}, bf16[512,512]{1,0:T(8,128)(2,1)S(1)}, u32[]{:S(2)}, u32[]{:S(2)}) collective-permute-start(bf16[512,512]{1,0:T(8,128)(2,1)} %get-tuple-element.68), channel_id=1, source_target_pairs={{0,4},{4,0},{8,12},{12,8},{16,20},{20,16},{24,28},{28,24},{1,5},{5... | collective-permute-start | bytes 1572872 | tf_op jit(solution)/shard_map/ppermute | solution.py:391
  108.7 9.8 %collective-permute-start.44 = (bf16[256,640]{1,0:T(8,128)(2,1)S(1)}, bf16[256,640]{1,0:T(8,128)(2,1)S(1)}, u32[]{:S(2)}, u32[]{:S(2)}) collective-permute-start(bf16[256,640]{1,0:T(8,128)(2,1)S(1)} %broadcast_select_fusion.8), channel_id=1, source_target_pairs={{0,8},{4,12},{8,0},{12,4},{16,24},{20,28},{24,16},{28,20},{1,9},{5... | collective-permute-start | bytes 983048 | tf_op jit(solution)/shard_map/ppermute | solution.py:391
  119.3 18.7 %collective-permute-start.21 = (bf16[128,512]{1,0:T(8,128)(2,1)S(1)}, bf16[128,512]{1,0:T(8,128)(2,1)S(1)}, u32[]{:S(2)}, u32[]{:S(2)}) collective-permute-start(bf16[128,512]{1,0:T(8,128)(2,1)S(1)} %get-tuple-element.114), channel_id=1, source_target_pairs={{0,8},{4,12},{8,0},{12,4},{16,24},{20,28},{24,16},{28,20},{1,9},{5... | collective-permute-start | bytes 393224 | tf_op jit(solution)/shard_map/ppermute | solution.py:391
  120.0 18.6 %collective-permute-start.20 = (bf16[128,512]{1,0:T(8,128)(2,1)S(1)}, bf16[128,512]{1,0:T(8,128)(2,1)S(1)}, u32[]{:S(2)}, u32[]{:S(2)}) collective-permute-start(bf16[128,512]{1,0:T(8,128)(2,1)S(1)} %get-tuple-element.115), channel_id=1, source_target_pairs={{0,16},{4,20},{8,24},{12,28},{16,0},{20,4},{24,8},{28,12},{1,17},{... | collective-permute-start | bytes 393224 | tf_op jit(solution)/shard_map/ppermute | solution.py:391
  123.5 15.2 %collective-permute-start.19 = (bf16[128,512]{1,0:T(8,128)(2,1)S(1)}, bf16[128,512]{1,0:T(8,128)(2,1)S(1)}, u32[]{:S(2)}, u32[]{:S(2)}) collective-permute-start(bf16[128,512]{1,0:T(8,128)(2,1)S(1)} %get-tuple-element.113), channel_id=1, source_target_pairs={{0,24},{4,28},{8,16},{12,20},{16,8},{20,12},{24,0},{28,4},{1,25},{... | collective-permute-start | bytes 393224 | tf_op jit(solution)/shard_map/ppermute | solution.py:391
  124.2 12.3 %collective-permute-start.46 = (bf16[64,640]{1,0:T(8,128)(2,1)S(1)}, bf16[64,640]{1,0:T(8,128)(2,1)S(1)}, u32[]{:S(2)}, u32[]{:S(2)}) collective-permute-start(bf16[64,640]{1,0:T(8,128)(2,1)S(1)} %broadcast_select_fusion.26), channel_id=1, source_target_pairs={{0,16},{4,20},{8,24},{12,28},{16,0},{20,4},{24,8},{28,12},{1,17},{... | collective-permute-start | bytes 245768 | tf_op jit(solution)/shard_map/ppermute | solution.py:391
  136.5 14.5 %collective-permute-start.38 = (bf16[320,1024]{1,0:T(8,128)(2,1)S(1)}, bf16[320,1024]{1,0:T(8,128)(2,1)S(1)}, u32[]{:S(2)}, u32[]{:S(2)}) collective-permute-start(bf16[320,1024]{1,0:T(8,128)(2,1)S(1)} %broadcast_select_fusion.2), channel_id=1, source_target_pairs={{0,4},{4,0},{8,12},{12,8},{16,20},{20,16},{24,28},{28,24},{1,5},{5... | collective-permute-start | bytes 1966088 | tf_op jit(solution)/shard_map/ppermute | solution.py:391
  138.0 15.4 %collective-permute-start.25 = (bf16[128,416]{1,0:T(8,128)(2,1)S(1)}, bf16[128,416]{1,0:T(8,128)(2,1)S(1)}, u32[]{:S(2)}, u32[]{:S(2)}) collective-permute-start(bf16[128,416]{1,0:T(8,128)(2,1)S(1)} %pad_maximum_fusion.13), channel_id=1, source_target_pairs={{0,2},{1,3},{2,0},{3,1},{4,6},{5,7},{6,4},{7,5},{8,10},{9,11},{10,... | collective-permute-start | bytes 319496 | tf_op jit(solution)/shard_map/ppermute | solution.py:391
  138.6 13.8 %collective-permute-start.23 = (bf16[288,1664]{1,0:T(8,128)(2,1)S(1)}, bf16[288,1664]{1,0:T(8,128)(2,1)S(1)}, u32[]{:S(2)}, u32[]{:S(2)}) collective-permute-start(bf16[288,1664]{1,0:T(8,128)(2,1)S(1)} %pad_maximum_fusion.1), channel_id=1, source_target_pairs={{0,1},{1,0},{2,3},{3,2},{4,5},{5,4},{6,7},{7,6},{8,9},{9,8},{10,11... | collective-permute-start | bytes 2875400 | tf_op jit(solution)/shard_map/ppermute | solution.py:391
  138.6 7.4 %collective-permute-start.47 = (bf16[64,640]{1,0:T(8,128)(2,1)S(1)}, bf16[64,640]{1,0:T(8,128)(2,1)S(1)}, u32[]{:S(2)}, u32[]{:S(2)}) collective-permute-start(bf16[64,640]{1,0:T(8,128)(2,1)S(1)} %add_convert_fusion.8), channel_id=1, source_target_pairs={{0,16},{4,20},{8,24},{12,28},{16,0},{20,4},{24,8},{28,12},{1,17},{... | collective-permute-start | bytes 245768 | tf_op jit(solution)/shard_map/ppermute | solution.py:391
  146.0 9.0 %collective-permute-start.26 = (bf16[128,416]{1,0:T(8,128)(2,1)S(1)}, bf16[128,416]{1,0:T(8,128)(2,1)S(1)}, u32[]{:S(2)}, u32[]{:S(2)}) collective-permute-start(bf16[128,416]{1,0:T(8,128)(2,1)S(1)} %pad_maximum_fusion.14), channel_id=1, source_target_pairs={{0,3},{1,2},{2,1},{3,0},{4,7},{5,6},{6,5},{7,4},{8,11},{9,10},{10,... | collective-permute-start | bytes 319496 | tf_op jit(solution)/shard_map/ppermute | solution.py:391
  151.9 7.1 %collective-permute-start.28 = (bf16[160,512]{1,0:T(8,128)(2,1)S(1)}, bf16[160,512]{1,0:T(8,128)(2,1)S(1)}, u32[]{:S(2)}, u32[]{:S(2)}) collective-permute-start(bf16[160,512]{1,0:T(8,128)(2,1)S(1)} %copy-done.44), channel_id=1, source_target_pairs={{0,2},{1,3},{2,0},{3,1},{4,6},{5,7},{6,4},{7,5},{8,10},{9,11},{10,... | collective-permute-start | bytes 491528 | tf_op jit(solution)/shard_map/ppermute | solution.py:391
  152.5 8.3 %collective-permute-start.29 = (bf16[160,512]{1,0:T(8,128)(2,1)S(1)}, bf16[160,512]{1,0:T(8,128)(2,1)S(1)}, u32[]{:S(2)}, u32[]{:S(2)}) collective-permute-start(bf16[160,512]{1,0:T(8,128)(2,1)S(1)} %copy-done.43), channel_id=1, source_target_pairs={{0,3},{1,2},{2,1},{3,0},{4,7},{5,6},{6,5},{7,4},{8,11},{9,10},{10,... | collective-permute-start | bytes 491528 | tf_op jit(solution)/shard_map/ppermute | solution.py:391
  153.4 13.0 %collective-permute-start.48 = (bf16[128,640]{1,0:T(8,128)(2,1)S(1)}, bf16[128,640]{1,0:T(8,128)(2,1)S(1)}, u32[]{:S(2)}, u32[]{:S(2)}) collective-permute-start(bf16[128,640]{1,0:T(8,128)(2,1)S(1)} %pad_maximum_fusion.10), channel_id=1, source_target_pairs={{0,4},{4,0},{8,12},{12,8},{16,20},{20,16},{24,28},{28,24},{1,5},{5... | collective-permute-start | bytes 491528 | tf_op jit(solution)/shard_map/ppermute | solution.py:391
  155.0 28.3 %collective-permute-start.39 = (bf16[160,1024]{1,0:T(8,128)(2,1)S(1)}, bf16[160,1024]{1,0:T(8,128)(2,1)S(1)}, u32[]{:S(2)}, u32[]{:S(2)}) collective-permute-start(bf16[160,1024]{1,0:T(8,128)(2,1)S(1)} %broadcast_select_fusion.11), channel_id=1, source_target_pairs={{0,8},{4,12},{8,0},{12,4},{16,24},{20,28},{24,16},{28,20},{1,9},{5... | collective-permute-start | bytes 983048 | tf_op jit(solution)/shard_map/ppermute | solution.py:391
  163.2 31.3 %collective-permute-start.30 = (bf16[448,512]{1,0:T(8,128)(2,1)S(1)}, bf16[448,512]{1,0:T(8,128)(2,1)S(1)}, u32[]{:S(2)}, u32[]{:S(2)}) collective-permute-start(bf16[448,512]{1,0:T(8,128)(2,1)S(1)} %broadcast_select_fusion.5), channel_id=1, source_target_pairs={{0,8},{4,12},{8,0},{12,4},{16,24},{20,28},{24,16},{28,20},{1,9},{5... | collective-permute-start | bytes 1376264 | tf_op jit(solution)/shard_map/ppermute | solution.py:391
  166.3 11.2 %collective-permute-start.51 = (bf16[16,1664]{1,0:T(8,128)(2,1)S(1)}, bf16[16,1664]{1,0:T(8,128)(2,1)S(1)}, u32[]{:S(2)}, u32[]{:S(2)}) collective-permute-start(bf16[16,1664]{1,0:T(8,128)(2,1)S(1)} %fusion.3), channel_id=1, source_target_pairs={{0,8},{4,12},{8,0},{12,4},{16,24},{20,28},{24,16},{28,20},{1,9},{5... | collective-permute-start | bytes 159752 | tf_op jit(solution)/shard_map/ppermute | solution.py:391
  177.6 5.7 %collective-permute-start.52 = (bf16[16,1664]{1,0:T(8,128)(2,1)S(1)}, bf16[16,1664]{1,0:T(8,128)(2,1)S(1)}, u32[]{:S(2)}, u32[]{:S(2)}) collective-permute-start(bf16[16,1664]{1,0:T(8,128)(2,1)S(1)} %fusion.4), channel_id=1, source_target_pairs={{0,16},{4,20},{8,24},{12,28},{16,0},{20,4},{24,8},{28,12},{1,17},{... | collective-permute-start | bytes 159752 | tf_op jit(solution)/shard_map/ppermute | solution.py:391
  178.8 38.8 %collective-permute-start.49 = (bf16[256,640]{1,0:T(8,128)(2,1)S(1)}, bf16[256,640]{1,0:T(8,128)(2,1)S(1)}, u32[]{:S(2)}, u32[]{:S(2)}) collective-permute-start(bf16[256,640]{1,0:T(8,128)(2,1)S(1)} %pad_maximum_fusion.8), channel_id=1, source_target_pairs={{0,8},{4,12},{8,0},{12,4},{16,24},{20,28},{24,16},{28,20},{1,9},{5... | collective-permute-start | bytes 983048 | tf_op jit(solution)/shard_map/ppermute | solution.py:391
  183.5 10.4 %collective-permute-start.40 = (bf16[80,1024]{1,0:T(8,128)(2,1)S(1)}, bf16[80,1024]{1,0:T(8,128)(2,1)S(1)}, u32[]{:S(2)}, u32[]{:S(2)}) collective-permute-start(bf16[80,1024]{1,0:T(8,128)(2,1)S(1)} %broadcast_select_fusion.20), channel_id=1, source_target_pairs={{0,16},{4,20},{8,24},{12,28},{16,0},{20,4},{24,8},{28,12},{1,17},{... | collective-permute-start | bytes 491528 | tf_op jit(solution)/shard_map/ppermute | solution.py:391
  194.0 7.4 %collective-permute-start.41 = (bf16[80,1024]{1,0:T(8,128)(2,1)S(1)}, bf16[80,1024]{1,0:T(8,128)(2,1)S(1)}, u32[]{:S(2)}, u32[]{:S(2)}) collective-permute-start(bf16[80,1024]{1,0:T(8,128)(2,1)S(1)} %add_convert_fusion.6), channel_id=1, source_target_pairs={{0,16},{4,20},{8,24},{12,28},{16,0},{20,4},{24,8},{28,12},{1,17},{... | collective-permute-start | bytes 491528 | tf_op jit(solution)/shard_map/ppermute | solution.py:391
  194.7 6.7 %collective-permute-start.31 = (bf16[224,512]{1,0:T(8,128)(2,1)S(1)}, bf16[224,512]{1,0:T(8,128)(2,1)S(1)}, u32[]{:S(2)}, u32[]{:S(2)}) collective-permute-start(bf16[224,512]{1,0:T(8,128)(2,1)S(1)} %broadcast_select_fusion.14), channel_id=1, source_target_pairs={{0,4},{4,0},{8,12},{12,8},{16,20},{20,16},{24,28},{28,24},{1,5},{5... | collective-permute-start | bytes 688136 | tf_op jit(solution)/shard_map/ppermute | solution.py:391
  201.6 5.9 %collective-permute-start.32 = (bf16[112,512]{1,0:T(8,128)(2,1)S(1)}, bf16[112,512]{1,0:T(8,128)(2,1)S(1)}, u32[]{:S(2)}, u32[]{:S(2)}) collective-permute-start(bf16[112,512]{1,0:T(8,128)(2,1)S(1)} %broadcast_select_fusion.23), channel_id=1, source_target_pairs={{0,16},{4,20},{8,24},{12,28},{16,0},{20,4},{24,8},{28,12},{1,17},{... | collective-permute-start | bytes 344072 | tf_op jit(solution)/shard_map/ppermute | solution.py:391
  203.5 10.4 %collective-permute-start.42 = (bf16[160,1024]{1,0:T(8,128)(2,1)S(1)}, bf16[160,1024]{1,0:T(8,128)(2,1)S(1)}, u32[]{:S(2)}, u32[]{:S(2)}) collective-permute-start(bf16[160,1024]{1,0:T(8,128)(2,1)S(1)} %pad_maximum_fusion.7), channel_id=1, source_target_pairs={{0,8},{4,12},{8,0},{12,4},{16,24},{20,28},{24,16},{28,20},{1,9},{5... | collective-permute-start | bytes 983048 | tf_op jit(solution)/shard_map/ppermute | solution.py:391
  207.5 6.7 %collective-permute-start.33 = (bf16[112,512]{1,0:T(8,128)(2,1)S(1)}, bf16[112,512]{1,0:T(8,128)(2,1)S(1)}, u32[]{:S(2)}, u32[]{:S(2)}) collective-permute-start(bf16[112,512]{1,0:T(8,128)(2,1)S(1)} %add_convert_fusion.7), channel_id=1, source_target_pairs={{0,16},{4,20},{8,24},{12,28},{16,0},{20,4},{24,8},{28,12},{1,17},{... | collective-permute-start | bytes 344072 | tf_op jit(solution)/shard_map/ppermute | solution.py:391
  214.1 17.6 %collective-permute-start.43 = (bf16[320,1024]{1,0:T(8,128)(2,1)S(1)}, bf16[320,1024]{1,0:T(8,128)(2,1)S(1)}, u32[]{:S(2)}, u32[]{:S(2)}) collective-permute-start(bf16[320,1024]{1,0:T(8,128)(2,1)S(1)} %pad_maximum_fusion.4), channel_id=1, source_target_pairs={{0,4},{4,0},{8,12},{12,8},{16,20},{20,16},{24,28},{28,24},{1,5},{5... | collective-permute-start | bytes 1966088 | tf_op jit(solution)/shard_map/ppermute | solution.py:391
  214.3 16.1 %collective-permute-start.34 = (bf16[224,512]{1,0:T(8,128)(2,1)S(1)}, bf16[224,512]{1,0:T(8,128)(2,1)S(1)}, u32[]{:S(2)}, u32[]{:S(2)}) collective-permute-start(bf16[224,512]{1,0:T(8,128)(2,1)S(1)} %pad_maximum_fusion.9), channel_id=1, source_target_pairs={{0,4},{4,0},{8,12},{12,8},{16,20},{20,16},{24,28},{28,24},{1,5},{5... | collective-permute-start | bytes 688136 | tf_op jit(solution)/shard_map/ppermute | solution.py:391
  230.5 8.5 %collective-permute-start.35 = (bf16[448,512]{1,0:T(8,128)(2,1)S(1)}, bf16[448,512]{1,0:T(8,128)(2,1)S(1)}, u32[]{:S(2)}, u32[]{:S(2)}) collective-permute-start(bf16[448,512]{1,0:T(8,128)(2,1)S(1)} %pad_maximum_fusion.6), channel_id=1, source_target_pairs={{0,8},{4,12},{8,0},{12,4},{16,24},{20,28},{24,16},{28,20},{1,9},{5... | collective-permute-start | bytes 1376264 | tf_op jit(solution)/shard_map/ppermute | solution.py:391
  (52 other events, 390.0 us)

commit v3 on v2

v3 whole, which is shorter than its diff:
```python
import functools
import math

import jax
import jax.numpy as jnp
from jax import lax
from jax.experimental import pallas as pl
from jax.experimental.pallas import tpu as pltpu
from jax.sharding import PartitionSpec as P

HEADS = 4
HEAD_DIM = 256
NORM_EPS = 1e-06
ROPE_BASE = 1000000.0
BF = jnp.bfloat16
F32 = jnp.float32
MIB = 1024 * 1024


def dot(a, b):
    return lax.dot_general(a, b, (((1,), (0,)), ((), ())), preferred_element_type=F32)


def dot_nt(a, b):
    return lax.dot_general(a, b, (((1,), (1,)), ((), ())), preferred_element_type=F32)


def dot_tn(a, b):
    return lax.dot_general(a, b, (((0,), (0,)), ((), ())), preferred_element_type=F32)


def unit(v):
    r = lax.rsqrt(jnp.mean(v * v, axis=-1, keepdims=True) + NORM_EPS)
    return v * r, r


def norm_back(c, u, r, g):
    cg = c * g
    grad = r * (cg - u * jnp.mean(cg * u, axis=-1, keepdims=True))
    return grad, jnp.sum(c * u, axis=0, keepdims=True)


def rotate(v, cos, sin):
    half = v.shape[-1] // 2
    a, b = v[:, :half], v[:, half:]
    return jnp.concatenate([a * cos - b * sin, b * cos + a * sin], axis=-1)


def rotate_back(v, cos, sin):
    half = v.shape[-1] // 2
    a, b = v[:, :half], v[:, half:]
    return jnp.concatenate([a * cos + b * sin, b * cos - a * sin], axis=-1)


def call(kernel, outs, *args, scratch=(), vmem=20, us=1.0, smem=0, after=()):
    specs = [pl.BlockSpec(memory_space=pltpu.VMEM)] * len(args)
    for i in range(smem):
        specs[i] = pl.BlockSpec(memory_space=pltpu.SMEM)
    specs += [pl.BlockSpec(memory_space=pl.ANY)] * len(after)
    moved = sum(math.prod(a.shape) * a.dtype.itemsize for a in args)
    used, skip = len(args), len(args) + len(after)

    def body(*refs):
        kernel(*refs[:used], *refs[skip:])

    return pl.pallas_call(
        body,
        out_shape=[jax.ShapeDtypeStruct(s, d) for s, d in outs],
        in_specs=specs,
        out_specs=[pl.BlockSpec(memory_space=pltpu.VMEM)] * len(outs),
        scratch_shapes=list(scratch),
        compiler_params=pltpu.CompilerParams(vmem_limit_bytes=vmem * MIB),
        cost_estimate=pl.CostEstimate(
            flops=int(us * 1.1e9), bytes_accessed=moved, transcendentals=0
        ),
    )(*args, *after)


def bound_of(hg):
    peak = jnp.max(jnp.abs(hg[...]), axis=1, keepdims=True)
    return math.sqrt(HEAD_DIM) * peak[0:1, :] * peak[1:2, :]


def tile_loop(count, step):
    if count == 1:
        step(0)
    else:

        def body(t, carry):
            step(t)
            return carry

        lax.fori_loop(0, count, body, 0)


def tile_rows(t, tile, count):
    return pl.ds(pl.multiple_of(t * tile, tile), tile) if count > 1 else slice(None)


def pack_kernel(wk, wv, ng, hg, out):
    share = wk.shape[0]
    out[:share, :HEAD_DIM] = wk[...]
    out[:share, HEAD_DIM:] = wv[...]
    tail = jnp.concatenate(
        [
            ng[...].astype(F32),
            jnp.concatenate(
                [hg[...].astype(F32), jnp.zeros((2, share - hg.shape[1]), F32)], axis=1
            ),
            jnp.zeros((10, share), F32),
        ],
        axis=0,
    )
    out[share:, :] = jnp.zeros((16, out.shape[1]), BF)
    out[share:, :share] = tail.astype(BF)


def ordered(f, parts):
    out = []
    for p in range(len(parts)):
        value = parts[0]
        for k in range(1, len(parts)):
            value = jnp.where(jnp.bitwise_xor(f, k) == p, parts[k], value)
        out.append(value)
    return out


def fill(f, blocks, w, first):
    share = w.shape[0] // len(blocks)
    for k, blk in enumerate(blocks):
        start = pl.multiple_of(jnp.bitwise_xor(f, k) * share, 16)
        w[pl.ds(start, share), first : first + blk.shape[1]] = blk[:share, :]


def front_kernel(nf, tile, f_ref, tok, cos, sin, qpos, kpos, *rest):
    blocks, kv_blocks, rest = rest[:nf], rest[nf : 2 * nf], rest[2 * nf :]
    normed_o, kraw_o, kv_o, qraw_o, q_o, att_o, low_o, tot_o, gains, hg, w = rest
    f = f_ref[0]
    share = w.shape[0] // nf
    rows = qpos.shape[0]
    proj = HEADS * HEAD_DIM
    scale = 1.0 / math.sqrt(HEAD_DIM)
    count = tok.shape[0] // tile
    fill(f, blocks, w, 0)
    fill(f, kv_blocks, w, proj)
    extra = ordered(f, [b[share:, :].astype(F32) for b in kv_blocks])
    gains[...] = jnp.concatenate([e[:4, :share] for e in extra], axis=1)
    hg[...] = jnp.concatenate([e[4:6, : HEAD_DIM // nf] for e in extra], axis=1)
    bound = bound_of(hg)

    def keys(t):
        part = tile_rows(t, tile, count)
        u, _ = unit(tok[part, :].astype(F32))
        normed = (u * gains[0:1, :]).astype(BF)
        normed_o[part, :] = normed
        out = dot(normed, w[:, proj:])
        key = out[:, :HEAD_DIM]
        kraw_o[part, :] = key
        u, _ = unit(key)
        kv_o[part, :HEAD_DIM] = rotate(u * hg[1:2, :], cos[part, :], sin[part, :]).astype(BF)
        kv_o[part, HEAD_DIM:] = out[:, HEAD_DIM:].astype(BF)

    tile_loop(count, keys)
    for h in range(HEADS):
        raw = dot(normed_o[:rows, :], w[:, h * HEAD_DIM : (h + 1) * HEAD_DIM])
        k = jnp.bitwise_xor(f, h)
        qraw_o[k] = raw
        u, _ = unit(raw)
        q_o[k] = rotate(u * hg[0:1, :], cos[:rows, :], sin[:rows, :]).astype(BF)
    for k in range(HEADS):

        def step(t, k=k):
            part = tile_rows(t, tile, count)
            raw = dot_nt(q_o[k], kv_o[part, :HEAD_DIM])
            allowed = kpos[:, part] <= qpos[...]
            terms = jnp.where(allowed, jnp.exp(raw * scale - bound), 0.0)
            total = jnp.sum(terms, axis=1, keepdims=True)
            num = dot(terms.astype(BF), kv_o[part, HEAD_DIM:])
            if count == 1:
                tot_o[k], att_o[k] = total, num
            else:
                tot_o[k] += total
                att_o[k] += num

        if count > 1:
            tot_o[k] = jnp.zeros_like(tot_o[k])
            att_o[k] = jnp.zeros_like(att_o[k])
        tile_loop(count, step)
        att = att_o[k] / tot_o[k]
        att_o[k] = att
        low_o[k] = att.astype(BF)


def mid_kernel(nf, tok, gains, att, *rest):
    wo = rest[:nf]
    branch_o, middle_o, ff_o = rest[nf:]
    branch = None
    for k in range(nf):
        term = dot(att[k], wo[k][...])
        branch = term if branch is None else branch + term
    branch_o[...] = branch
    u, _ = unit(branch)
    middle = tok[...].astype(F32) + u * gains[1:2, :]
    middle_o[...] = middle
    u, _ = unit(middle)
    ff_o[...] = (u * gains[2:3, :]).astype(BF)


def gelu_parts(v):
    t = jnp.tanh(0.7978845608028654 * (v + 0.044715 * v * v * v))
    half = 0.5 * (1.0 + t)
    slope = half + 0.5 * v * (1.0 - t * t) * 0.7978845608028654 * (1.0 + 3 * 0.044715 * v * v)
    return v * half, slope


def ff_kernel(mine, other, wg0, wu0, wd0, wg1, wu1, wd1, own_o, send_o, pack_o, hid_o, a_o, b_o):
    rows, d = mine.shape
    pack_o[:rows, :d] = mine[...]
    pack_o[rows:, :d] = other[...]
    x = pack_o[:, :d]
    mixed = None
    for i, (wg, wu, wd) in enumerate(((wg0, wu0, wd0), (wg1, wu1, wd1))):
        gate = dot(x, wg[...])
        up = dot(x, wu[...])
        value, slope = gelu_parts(gate)
        a_o[i] = value
        b_o[i] = up * slope
        hidden = (value * up).astype(BF)
        if i == 0:
            hid_o[...] = hidden
        else:
            pack_o[:, d:] = hidden
        term = dot(hidden, wd[...])
        mixed = term if mixed is None else mixed + term
    own_o[...] = mixed[:rows, :]
    send_o[...] = mixed[rows:, :].astype(BF)


def finish_kernel(own, got, middle, cot, gains, out_o, low_o, gain_o):
    u, r = unit(own[...] + got[...].astype(F32))
    out_o[...] = (middle[...] + u * gains[3:4, :]).astype(BF)
    grad, gain = norm_back(cot[...].astype(F32), u, r, gains[3:4, :])
    low_o[...] = grad.astype(BF)
    gain_o[...] = gain


def ff_back_kernel(
    mine, other, a, b, wg0, wu0, wd0, wg1, wu1, wd1, own_o, send_o, pack_o, gg_o
):
    rows, d = mine.shape
    width = wg0.shape[1]
    pack_o[:rows, :d] = mine[...]
    pack_o[rows:, :d] = other[...]
    c = pack_o[:, :d]
    total = None
    for i, (wg, wu, wd) in enumerate(((wg0, wu0, wd0), (wg1, wu1, wd1))):
        gh = dot_nt(c, wd[...])
        gg = (gh * b[i]).astype(BF)
        gu = (gh * a[i]).astype(BF)
        if i == 0:
            gg_o[:, :width] = gg
            gg_o[:, width:] = gu
        else:
            pack_o[:, d : d + width] = gg
            pack_o[:, d + width :] = gu
        term = dot_nt(gg, wg[...]) + dot_nt(gu, wu[...])
        total = term if total is None else total + term
    own_o[...] = total[:rows, :]
    send_o[...] = total[rows:, :].astype(BF)


def fold(out, at, grad, wide):
    rows = grad.shape[0]
    out[at : at + rows, :] = grad[:, :wide].astype(BF)
    strip = rows // 4
    parts = [grad[i * strip : (i + 1) * strip, wide:] for i in range(4)]
    out[at + rows : at + rows + strip, :] = jnp.concatenate(parts, axis=1).astype(BF)


def unfold(full, at, out):
    rows, wide = out.shape[0], full.shape[1]
    out[:, :wide] = full[at : at + rows]
    strip, piece = rows // 4, wide // 4
    for i in range(4):
        out[i * strip : (i + 1) * strip, wide:] = full[
            at + rows : at + rows + strip, i * piece : (i + 1) * piece
        ]


def ff_grad_kernel(pack1, hid, got1, pack2, gg, got2, gate_o, up_o, x_s, h_s, c_s, g_s):
    rows, width = hid.shape
    d = x_s.shape[1]
    x_s[:rows, :] = pack1[:, :d]
    x_s[rows:, :] = got1[:, :d]
    h_s[:rows, :] = hid[...]
    h_s[rows:, :] = got1[:, d:]
    c_s[:rows, :] = pack2[:, :d]
    c_s[rows:, :] = got2[:, :d]
    g_s[:rows, :] = gg[...]
    g_s[rows:, :] = got2[:, d:]
    gate_o[:d, :] = dot_tn(x_s[...], g_s[:, :width]).astype(BF)
    up_o[...] = dot_tn(x_s[...], g_s[:, width:]).astype(BF)
    fold(gate_o, d, dot_tn(h_s[...], c_s[...]), width)


def post_kernel(own, got, middle, branch, cot, gains, gbl_o, resid_o, gain_o):
    um, rm = unit(middle[...])
    grad, gain2 = norm_back(own[...] + got[...].astype(F32), um, rm, gains[2:3, :])
    grad_middle = cot[...].astype(F32) + grad
    resid_o[...] = grad_middle
    ub, rb = unit(branch[...])
    grad_branch, gain1 = norm_back(grad_middle, ub, rb, gains[1:2, :])
    gbl_o[...] = grad_branch.astype(BF)
    gain_o[...] = jnp.concatenate([gain1, gain2], axis=0)


def back_kernel(
    nf, tile, f_ref, gbl, gain12, gain3, att, tot, q, qraw, kv, normed, kraw, hg, cos, sin, qpos,
    kpos, *rest,
):
    wo = rest[:nf]
    far_o, own_o, next_o, odd_o, even_o, sg_s, tg_s, acc, s_s, e_s, kvw_s, gq_s = rest[nf:]
    f = f_ref[0]
    scale = 1.0 / math.sqrt(HEAD_DIM)
    rows, d = gbl.shape
    bound = bound_of(hg)
    count = kv.shape[0] // tile
    for k in range(HEADS):
        ga = dot_nt(gbl[...], wo[k][...])
        inv = 1.0 / tot[k]
        sg_s[k * rows : (k + 1) * rows, :] = (ga * inv).astype(BF)
        tg_s[k] = -jnp.sum(ga * att[k], axis=1, keepdims=True) * inv

    def step(t):
        part = tile_rows(t, tile, count)
        allowed = kpos[:, part] <= qpos[...]
        for k in range(HEADS):
            mine = slice(k * rows, (k + 1) * rows)
            raw = dot_nt(q[k], kv[part, :HEAD_DIM])
            terms = jnp.where(allowed, jnp.exp(raw * scale - bound), 0.0)
            e_s[mine, :] = terms.astype(BF)
            gp = dot_nt(sg_s[mine, :], kv[part, HEAD_DIM:])
            s = (terms * (gp + tg_s[k]) * scale).astype(BF)
            s_s[mine, :] = s
            term = dot(s, kv[part, :HEAD_DIM])
            if count == 1:
                acc[k] = term
            else:
                acc[k] += term
        queries = q[...].reshape(HEADS * rows, HEAD_DIM)
        c = rotate_back(dot_tn(s_s[...], queries), cos[part, :], sin[part, :])
        u, r = unit(kraw[part, :])
        gk, gain = norm_back(c, u, r, hg[1:2, :])
        gkl = gk.astype(BF)
        gvl = dot_tn(e_s[...], sg_s[...]).astype(BF)
        kk = dot_tn(normed[part, :], gkl)
        vv = dot_tn(normed[part, :], gvl)
        if count == 1:
            kvw_s[:d, :HEAD_DIM] = kk
            kvw_s[:d, HEAD_DIM:] = vv
            kvw_s[d : d + 1, :HEAD_DIM] = gain
        else:
            kvw_s[:d, :HEAD_DIM] += kk
            kvw_s[:d, HEAD_DIM:] += vv
            kvw_s[d : d + 1, :HEAD_DIM] += gain
        for j in range(tile // rows):
            out = even_o if j % 2 == 0 else odd_o
            start = (j // 2) * rows
            if count > 1:
                start = pl.multiple_of(t * (tile // 2) + start, rows)
            out[pl.ds(start, rows), :HEAD_DIM] = gkl[j * rows : (j + 1) * rows, :]
            out[pl.ds(start, rows), HEAD_DIM:] = gvl[j * rows : (j + 1) * rows, :]

    if count > 1:
        acc[...] = jnp.zeros_like(acc)
        kvw_s[...] = jnp.zeros_like(kvw_s)
    tile_loop(count, step)
    share = own_o.shape[0]
    lines = 2 * rows + 16
    for k, out in enumerate((own_o, next_o, None, None)):
        start = pl.multiple_of(jnp.bitwise_xor(f, k) * share, 16)
        chunk = kvw_s[pl.ds(start, share), :]
        if out is not None:
            out[...] = chunk
        else:
            at = lines + (k - 2) * share
            far_o[at : at + share, :] = chunk.astype(BF)
    gain = None
    for k in range(HEADS):
        u, r = unit(qraw[k])
        c = rotate_back(acc[k], cos[:rows, :], sin[:rows, :])
        grad, g = norm_back(c, u, r, hg[0:1, :])
        gain = g if gain is None else gain + g
        h = jnp.bitwise_xor(f, k)
        gq_s[:, pl.ds(pl.multiple_of(h * HEAD_DIM, HEAD_DIM), HEAD_DIM)] = grad.astype(BF)
    wide = 2 * HEAD_DIM
    far_o[:rows, :] = gq_s[:, :wide]
    far_o[rows : 2 * rows, :] = gq_s[:, wide:]
    three = jnp.concatenate([gain12[...], gain3[...]], axis=0)
    tail = jnp.concatenate(
        [three[i : i + 1, wide:] for i in range(3)] + [jnp.zeros((1, 4 * wide - 3 * d), F32)],
        axis=1,
    )
    heads = jnp.concatenate([gain, kvw_s[d : d + 1, :HEAD_DIM]], axis=1)
    pad = jnp.zeros((11, wide), F32)
    far_o[2 * rows : lines, :] = jnp.concatenate(
        [three[:, :wide], tail, heads, pad], axis=0
    ).astype(BF)


def relay_kernel(lines, mine, far, own, nxt, out_o, own_o):
    share = own.shape[0]
    out_o[:lines, :] = mine[:lines, :]
    out_o[lines : 2 * lines, :] = far[:lines, :]
    out_o[2 * lines :, :] = (nxt[...] + far[lines + share :, :].astype(F32)).astype(BF)
    own_o[...] = own[...] + far[lines : lines + share, :].astype(F32)


def query_grad_kernel(lines, mine, far, got, own, *rest):
    cols, (out_o, g_s, n_s) = rest[:4], rest[4:]
    rows, share = cols[0].shape[0], n_s.shape[1]
    wide = mine.shape[1]
    gain = None
    for k, (ref, at) in enumerate(((mine, 0), (got, 0), (far, 0), (got, lines))):
        mine_rows = slice(k * rows, (k + 1) * rows)
        g_s[mine_rows, :wide] = ref[at : at + rows, :]
        g_s[mine_rows, wide:] = ref[at + rows : at + 2 * rows, :]
        n_s[mine_rows, :] = cols[k][:, cols[k].shape[1] - share :]
        part = ref[at + 2 * rows : at + lines, :].astype(F32)
        gain = part if gain is None else gain + part
    qw = dot_tn(n_s[...], g_s[...])
    out_o[:share, :] = qw[:, :wide].astype(BF)
    out_o[share : 2 * share, :] = qw[:, wide:].astype(BF)
    out_o[2 * share : 3 * share, :] = (own[...] + got[2 * lines :, :].astype(F32)).astype(BF)
    out_o[3 * share : 3 * share + 16, :] = gain.astype(BF)
    out_o[3 * share + 16 :, :] = jnp.zeros((out_o.shape[0] - 3 * share - 16, wide), BF)


def out_grad_kernel(nf, up, *refs):
    cols, gbl, (out_o, a_s, b_s) = refs[:nf], refs[nf : 2 * nf], refs[2 * nf :]
    rows = gbl[0].shape[0]
    for k in range(nf):
        a_s[k * rows : (k + 1) * rows, :] = cols[k][:, : a_s.shape[1]]
        b_s[k * rows : (k + 1) * rows, :] = gbl[k][...]
    out_o[: up.shape[0], :] = up[...]
    fold(out_o, up.shape[0], dot_tn(a_s[...], b_s[...]), up.shape[1])


def joined(upper, mine, got):
    a, b = mine[...].astype(F32), got[...].astype(F32)
    return jnp.concatenate([jnp.where(upper, b, a), jnp.where(upper, a, b)], axis=0)


def last_ff_kernel(upper_ref, mine, got, first_o, second_o):
    full = joined(upper_ref[0] != 0, mine, got)
    rows = first_o.shape[0]
    first_o[...] = full[:rows]
    unfold(full, rows, second_o)


def last_kernel(upper_ref, mine, got, wq, wk, wv, q_o, k_o, v_o, p_o, rest_o):
    share = wq.shape[0]
    full = joined(upper_ref[0] != 0, mine, got)
    wide = full.shape[1]
    q_o[:, :wide] = full[:share]
    q_o[:, wide:] = full[share : 2 * share]
    k_o[...] = full[2 * share : 3 * share, :HEAD_DIM]
    v_o[...] = full[2 * share : 3 * share, HEAD_DIM:]
    total = jnp.sum(q_o[...] * wq[...].astype(F32), axis=1, keepdims=True)
    total += jnp.sum(k_o[...] * wk[...].astype(F32), axis=1, keepdims=True)
    p_o[...] = total + jnp.sum(v_o[...] * wv[...].astype(F32), axis=1, keepdims=True)
    rest_o[...] = full[3 * share : 3 * share + 16]


def input_back_kernel(nf, f_ref, tok, gkv, gq, resid, gains, *rest):
    blocks, kv_blocks, (grad_o, w) = rest[:nf], rest[nf : 2 * nf], rest[2 * nf :]
    rows = tok.shape[0]
    proj = HEADS * HEAD_DIM
    fill(f_ref[0], blocks, w, 0)
    fill(f_ref[0], kv_blocks, w, proj)
    low = gkv[...].astype(BF)
    wide = 2 * HEAD_DIM
    gn = dot_nt(gq[:rows, :], w[:, :wide]) + dot_nt(gq[rows : 2 * rows, :], w[:, wide:proj])
    gn = gn + dot_nt(low, w[:, proj:])
    u, r = unit(tok[...].astype(F32))
    gx, _ = norm_back(gn, u, r, gains[0:1, :])
    grad_o[...] = resid[...] + gx


def swap(x, axis, n, bit):
    return lax.ppermute(x, axis, [(i, i ^ bit) for i in range(n)])


class Order:
    def __init__(self):
        self.last = ()

    def arrived(self, *xs):
        out = lax.optimization_barrier(tuple(xs) + self.last)[: len(xs)]
        return out if len(xs) > 1 else out[0]

    def leaves(self, x):
        self.last = (x,)
        return x


def follow(x, *earlier):
    return lax.optimization_barrier((x,) + earlier)[0]


def gather_fsdp(x, n, *earlier):
    far = swap(x, "fsdp", n, 2)
    both = swap(jnp.concatenate([x, follow(far, *earlier)], axis=0), "fsdp", n, 1)
    rows = x.shape[0]
    return [x, both[:rows], far, both[rows:]]


def exchange_fsdp(blocks, n):
    return [b if k == 0 else swap(b, "fsdp", n, k) for k, b in enumerate(blocks)]


def gather_ctx(x, n):
    if n > 8:
        bit = 1
        while bit < n:
            x = jnp.concatenate([x, swap(x, "ctx", n, bit)], axis=0)
            bit *= 2
        return x, x
    far = {k: swap(x, "ctx", n, k) for k in range(n - 2, 0, -2)}
    near = swap(x, "ctx", n, 1)
    rows = x.shape[0]
    first = swap(far[2], "ctx", n, 1)
    ahead = jnp.concatenate([far[k] for k in range(4, n, 2)], axis=0)
    second = swap(ahead, "ctx", n, 1)
    parts = [x, near, far[2], first]
    for i, k in enumerate(range(4, n, 2)):
        parts += [far[k], second[i * rows : (i + 1) * rows]]
    return jnp.concatenate(parts, axis=0), ahead


def scatter_steps(odd, even, n, order, result):
    got = swap(order.leaves(odd), "ctx", n, 1)
    yield
    x = even.astype(F32) + order.arrived(got).astype(F32)
    rows = x.shape[0] * 2 // n
    if n > 8:
        bit = n // 2
        while bit > 1:
            half = x.shape[0] // 2
            got = swap(order.leaves(x[half:].astype(BF)), "ctx", n, bit)
            yield
            x = x[:half] + order.arrived(got).astype(F32)
            bit //= 2
        result.append(x)
        return
    low = order.leaves(x.astype(BF))
    got = [swap(low[k * rows : (k + 1) * rows], "ctx", n, 2 * k) for k in range(n // 2 - 1, 0, -1)]
    yield
    total = x[:rows]
    for g in order.arrived(*got):
        total = total + g.astype(F32)
    result.append(total)


def sum_steps(x, n, c, bits, order, result):
    for bit in bits:
        half = x.shape[0] // 2
        upper = (c & bit) != 0
        keep = jnp.where(upper, x[half:], x[:half])
        send = jnp.where(upper, x[:half], x[half:])
        got = swap(order.leaves(send), "ctx", n, bit)
        yield
        x = (keep.astype(F32) + order.arrived(got).astype(F32)).astype(BF)
    for bit in bits[:0:-1]:
        upper = (c & bit) != 0
        got = swap(order.leaves(x), "ctx", n, bit)
        yield
        got = order.arrived(got)
        x = jnp.concatenate([jnp.where(upper, got, x), jnp.where(upper, x, got)], axis=0)
    got = swap(order.leaves(x), "ctx", n, bits[0])
    yield
    result += [x, order.arrived(got)]


def short_sum_steps(x, n, c, order, result):
    half = x.shape[0] // 2
    upper = (c & 1) != 0
    keep = jnp.where(upper, x[half:], x[:half])
    send = jnp.where(upper, x[:half], x[half:])
    got = swap(order.leaves(send), "ctx", n, 1)
    yield
    x = keep.astype(F32) + order.arrived(got).astype(F32)
    count = n // 2
    rows = half // count
    z = c >> 1
    low = order.leaves(x.astype(BF))
    total = lax.dynamic_slice_in_dim(x, z * rows, rows, 0)
    got = []
    for j in range(count - 1, 0, -1):
        piece = lax.dynamic_slice_in_dim(low, (z ^ j) * rows, rows, 0)
        got.append(swap(piece, "ctx", n, 2 * j))
    yield
    for g in order.arrived(*got):
        total = total + g.astype(F32)
    mine = order.leaves(total.astype(BF))
    parts = [mine] + [swap(mine, "ctx", n, 2 * j) for j in range(1, count)]
    yield
    parts = order.arrived(*parts)
    x = jnp.zeros((half, x.shape[1]), BF)
    for j, p in enumerate(parts):
        x = lax.dynamic_update_slice_in_dim(x, p, (z ^ j) * rows, 0)
    got = swap(order.leaves(x), "ctx", n, 1)
    yield
    result += [x, order.arrived(got)]


def layer(
    nf,
    nc,
    tokens,
    cotangent,
    block_order,
    query_weight,
    key_weight,
    value_weight,
    out_weight,
    gate_weight,
    up_weight,
    down_weight,
    norm_gains,
    head_gains,
):
    rows, d = tokens.shape
    block_len = rows // 2
    f = lax.axis_index("fsdp")
    c = lax.axis_index("ctx")
    f_arr = f.reshape(1).astype(jnp.int32)
    seq = nc * rows
    tile = min(seq, 1024)
    proj = HEADS * HEAD_DIM
    width = gate_weight.shape[1]
    share = d // nf
    qkv = proj + 2 * HEAD_DIM
    hd = (HEADS, rows, HEAD_DIM)

    wq_far = swap(query_weight, "fsdp", nf, 2)
    tok_all, ahead = gather_ctx(tokens, nc)
    (kvpack,) = call(
        pack_kernel, [((share + 16, 2 * HEAD_DIM), BF)],
        key_weight, value_weight, norm_gains, head_gains,
    )

    slots = jnp.take(block_order.reshape(nc, 2), c ^ jnp.arange(nc), axis=0)
    pos = (slots.reshape(-1, 1) * block_len + jnp.arange(block_len)[None, :]).reshape(seq)
    kpos = pos.reshape(1, seq)
    qpos = pos[:rows].reshape(rows, 1)
    inv_freq = ROPE_BASE ** (-2.0 * jnp.arange(HEAD_DIM // 2, dtype=F32) / HEAD_DIM)
    angles = pos.astype(F32)[:, None] * inv_freq[None, :]
    cos, sin = jnp.cos(angles), jnp.sin(angles)

    wkv = gather_fsdp(kvpack, nf, ahead, cos, sin)
    both = swap(jnp.concatenate([query_weight, follow(wq_far, ahead)], axis=0), "fsdp", nf, 1)
    wq = [query_weight, both[:share], wq_far, both[share:]]
    wo = gather_fsdp(out_weight, nf, both, wkv[1])
    own_ff = (gate_weight, up_weight, down_weight)
    next_ff = [swap(w, "fsdp", nf, 1) for w in lax.optimization_barrier(own_ff + (wo[1],))[:3]]

    big = 36 if seq <= 1024 else 60
    normed, kraw, kv, qraw, q, att, att_low, tot, gains, hg = call(
        functools.partial(front_kernel, nf, tile),
        [
            ((seq, d), BF), ((seq, HEAD_DIM), F32), ((seq, 2 * HEAD_DIM), BF),
            (hd, F32), (hd, BF), (hd, F32), (hd, BF), ((HEADS, rows, 1), F32),
            ((4, d), F32), ((2, HEAD_DIM), F32),
        ],
        f_arr, tok_all, cos, sin, qpos, kpos, *wq, *wkv,
        scratch=[pltpu.VMEM((d, qkv), BF)], smem=1, vmem=big, us=6,
    )
    branch, middle, ff_in = call(
        functools.partial(mid_kernel, nf),
        [((rows, d), F32), ((rows, d), F32), ((rows, d), BF)],
        tokens, gains, att_low, *wo, us=0.6,
    )
    cols = exchange_fsdp(
        [
            jnp.concatenate(
                [att_low[k], lax.dynamic_slice_in_dim(normed[:rows], (f ^ k) * share, share, 1)],
                axis=1,
            )
            for k in range(nf)
        ],
        nf,
    )
    two = 2 * rows
    own, send, pack1, hid, act, slope = call(
        ff_kernel,
        [
            ((rows, d), F32), ((rows, d), BF), ((two, d + width), BF), ((two, width), BF),
            ((2, two, width), F32), ((2, two, width), F32),
        ],
        ff_in, swap(ff_in, "fsdp", nf, 2), *own_ff, *next_ff, us=3.6,
    )
    got1 = swap(pack1, "fsdp", nf, 1)
    output, gml, gain3 = call(
        finish_kernel,
        [((rows, d), BF), ((rows, d), BF), ((1, d), F32)],
        own, swap(send, "fsdp", nf, 2), middle, cotangent, gains, after=cols[1:],
    )
    own, send, pack2, gg = call(
        ff_back_kernel,
        [((rows, d), F32), ((rows, d), BF), ((two, d + 2 * width), BF), ((two, 2 * width), BF)],
        gml, swap(gml, "fsdp", nf, 2), act, slope, *own_ff, *next_ff,
        us=3.6, after=[got1],
    )
    got2 = swap(pack2, "fsdp", nf, 1)
    got = swap(send, "fsdp", nf, 2)
    p_part, up_part = call(
        ff_grad_kernel,
        [((d + width + width // 4, width), BF), ((d, width), BF)],
        pack1, hid, got1, pack2, gg, got2,
        scratch=[
            pltpu.VMEM((2 * two, d), BF),
            pltpu.VMEM((2 * two, width), BF),
            pltpu.VMEM((2 * two, d), BF),
            pltpu.VMEM((2 * two, 2 * width), BF),
        ],
        us=2.5,
    )
    order = Order()
    up_bits = [1 << i for i in range(nc.bit_length() - 1)]
    alt_bits = up_bits[1:2] + up_bits[:1] + up_bits[2:]
    p_sum, q_sum, a_sum, kv_sum = [], [], [], []
    p_steps = sum_steps(p_part, nc, c, up_bits, order, p_sum)
    next(p_steps)
    gbl, resid, gain12 = call(
        post_kernel,
        [((rows, d), BF), ((rows, d), F32), ((2, d), F32)],
        own, got, middle, branch, cotangent, gains, after=order.last,
    )
    gbl_far = swap(gbl, "fsdp", nf, 2)
    lines = 2 * rows + 16
    wide = 2 * HEAD_DIM
    ybuf, kvw0, kvw1, odd, even = call(
        functools.partial(back_kernel, nf, tile),
        [
            ((lines + 2 * share, wide), BF),
            ((share, wide), F32),
            ((share, wide), F32),
            ((seq // 2, wide), BF),
            ((seq // 2, wide), BF),
        ],
        f_arr, gbl, gain12, gain3, att, tot, q, qraw, kv, normed, kraw, hg, cos, sin, qpos, kpos,
        *wo,
        scratch=[
            pltpu.VMEM((HEADS * rows, HEAD_DIM), BF),
            pltpu.VMEM((HEADS, rows, 1), F32),
            pltpu.VMEM(hd, F32),
            pltpu.VMEM((HEADS * rows, tile), BF),
            pltpu.VMEM((HEADS * rows, tile), BF),
            pltpu.VMEM((d + 8, wide), F32),
            pltpu.VMEM((rows, proj), BF),
        ],
        smem=1, vmem=big, us=9,
    )
    far = swap(order.leaves(ybuf), "fsdp", nf, 2)
    gbl_both = swap(
        order.leaves(jnp.concatenate([gbl, order.arrived(gbl_far)], axis=0)), "fsdp", nf, 1
    )
    next(p_steps)
    gbl_both = order.arrived(gbl_both)
    (q_part,) = call(
        functools.partial(out_grad_kernel, nf),
        [((d + (proj // nf) * 5 // 4, width), BF)],
        up_part, *cols, gbl, gbl_both[:rows], gbl_far, gbl_both[rows:],
        scratch=[pltpu.VMEM((nf * rows, proj // nf), BF), pltpu.VMEM((nf * rows, d), BF)],
        us=1.3,
    )
    q_steps = sum_steps(q_part, nc, c, alt_bits, order, q_sum)
    next(q_steps)
    kv_steps = scatter_steps(odd, even, nc, order, kv_sum)
    next(kv_steps)

    far = order.arrived(far)
    cbuf, kvw = call(
        functools.partial(relay_kernel, lines),
        [((2 * lines + share, wide), BF), ((share, wide), F32)],
        ybuf, far, kvw0, kvw1,
    )
    near = swap(order.leaves(cbuf), "fsdp", nf, 1)
    next(p_steps)
    near = order.arrived(near)
    (att_part,) = call(
        functools.partial(query_grad_kernel, lines),
        [((-(-(3 * share + 16) // 128) * 128, wide), BF)],
        ybuf, far, near, kvw, *cols,
        scratch=[pltpu.VMEM((nf * rows, proj), BF), pltpu.VMEM((nf * rows, share), BF)],
    )
    if nc > 8:
        a_steps = sum_steps(att_part, nc, c, up_bits, order, a_sum)
    else:
        a_steps = short_sum_steps(att_part, nc, c, order, a_sum)
    next(a_steps)
    turns = [q_steps, kv_steps, p_steps, a_steps, q_steps, kv_steps, p_steps, a_steps, q_steps]
    turns += [p_steps, a_steps, q_steps, a_steps, q_steps, p_steps]
    for steps in turns:
        next(steps, None)
    for steps in (a_steps, q_steps, p_steps, kv_steps):
        for _ in steps:
            pass

    (input_grad,) = call(
        functools.partial(input_back_kernel, nf),
        [((rows, d), F32)],
        f_arr, tokens, kv_sum[0], ybuf, resid, gains, *wq, *wkv,
        scratch=[pltpu.VMEM((d, qkv), BF)], smem=1, us=1.7,
    )
    upper = (c & up_bits[0]).reshape(1).astype(jnp.int32)
    grad_gate, grad_down = call(
        last_ff_kernel, [((d, width), F32), ((width, d), F32)], upper, *p_sum, smem=1
    )
    grad_up, grad_out = call(
        last_ff_kernel, [((d, width), F32), ((proj // nf, d), F32)],
        (c & alt_bits[0]).reshape(1).astype(jnp.int32), *q_sum, smem=1,
    )
    grad_q, grad_k, grad_v, gain0, gain_sum = call(
        last_kernel,
        [
            ((share, proj), F32), ((share, HEAD_DIM), F32), ((share, HEAD_DIM), F32),
            ((share, 1), F32), ((16, wide), F32),
        ],
        upper, *a_sum, query_weight, key_weight, value_weight, smem=1,
    )
    gain0 = gain0.reshape(1, share) / norm_gains[0:1].astype(F32)
    rest = gain_sum[3, : 3 * (d - wide)].reshape(3, d - wide)
    others = jnp.concatenate([gain_sum[:3], rest], axis=1)
    others = lax.dynamic_slice_in_dim(others, f * share, share, 1)
    heads = gain_sum[4].reshape(2, HEAD_DIM)
    return (
        output,
        input_grad,
        grad_q,
        grad_k,
        grad_v,
        grad_out,
        grad_gate,
        grad_up,
        grad_down,
        jnp.concatenate([gain0, others], axis=0),
        lax.dynamic_slice_in_dim(heads, f * (HEAD_DIM // nf), HEAD_DIM // nf, 1),
    )


def solution(mesh):
    row = P(("ctx", "fsdp"), None)
    first, second = P("fsdp", None), P(None, "fsdp")
    body = functools.partial(layer, mesh.shape["fsdp"], mesh.shape["ctx"])
    return jax.shard_map(
        body,
        mesh=mesh,
        in_specs=(row, row, P(), first, first, first, first, second, second, first, second, second),
        out_specs=(row, row, first, first, first, first, second, second, first, second, second),
        check_vma=False,
    )
```

time: 245 us -> 220 us (0.90)
  waiting for transfers between devices: 125 us -> 102 us
  local copies, waits for them, and re-layouts: 23.9 us -> 30.3 us
  Pallas kernels: 28.7 us -> 24.8 us
  other arithmetic: 12.3 us -> 8.45 us
    ppermute x53 -> x52, waiting for transfers between devices: 125 us -> 102 us  [swap(): return lax.ppermute(x, axis, [(i, i ^ bit) for i in range(n)])]
    unnamed x102 -> x200, local copies, waits for them, and re-layouts: 12.1 us -> 25.5 us
    pallas_call x9 -> x16, Pallas kernels: 28.7 us -> 24.8 us  [call(): pl.pallas_call(body, out_shape=[jax.ShapeDtypeStruct(s, d) for s, d in ou...]
    reshape x9 -> x1, local copies, waits for them, and re-layouts: 3.13 us -> 0.08 us  [layer(): slots = jnp.take(block_order.reshape(nc, 2), c ^ jnp.arange(nc), axis=0)]
    ppermute x53 -> x52, starting transfers between devices: 52.8 us -> 52.2 us  [swap(): return lax.ppermute(x, axis, [(i, i ^ bit) for i in range(n)])]
  transfers between devices with their start and end apart: 53 -> 52, of which waited for: 25 -> 19; matrix products, arithmetic and copies ran while one was open for 10% -> 6% of each run, Pallas kernels for 8% -> 7%
where the time goes in v3:
time: 220 us
  waiting for transfers between devices  102 us (46%)
  starting transfers between devices  52.2 us (24%)
  local copies, waits for them, and re-layouts  30.3 us (14%)
  Pallas kernels  24.8 us (11%)
  other arithmetic  8.45 us (4%)
    ppermute x52, waiting for transfers between devices, swap(): return lax.ppermute(x, axis, [(i, i ^ bit) for i in range(n)])  102 us
    ppermute x52, starting transfers between devices, swap(): return lax.ppermute(x, axis, [(i, i ^ bit) for i in range(n)])  52.2 us
    unnamed x200, local copies, waits for them, and re-layouts  25.5 us
    pallas_call x16, Pallas kernels, call(): pl.pallas_call(body, out_shape=[jax.ShapeDtypeStruct(s, d) for s, d in ou...  24.8 us
  transfers between devices with their start and end apart: 52, of which 19 were waited for; matrix products, arithmetic and copies ran while one was open for 6% of the time, Pallas kernels for 7%

profile of v3, /device:TPU:0, one launch (start us, length us, event | category | flops | bytes accessed | tf_op | source)
XLA Modules:
  0.0 219.5 jit_solution(14290140652141622367)
XLA Ops:
  0.7 3.1 %collective-permute-start.1 = (bf16[128,640]{1,0:T(8,128)(2,1)}, bf16[128,640]{1,0:T(8,128)(2,1)S(1)}, u32[]{:S(2)}, u32[]{:S(2)}) collective-permute-start(bf16[128,640]{1,0:T(8,128)(2,1)} %refs_1_.3), channel_id=1, source_target_pairs={{0,8},{4,12},{8,0},{12,4},{16,24},{20,28},{24,16},{28,20},{1,9},{5... | collective-permute-start | bytes 491528 | tf_op jit(solution)/shard_map/ppermute | solution.py:491
  3.7 1.5 collective-permute-start
  5.2 2.6 %collective-permute-start.3 = (bf16[128,640]{1,0:T(8,128)(2,1)}, bf16[128,640]{1,0:T(8,128)(2,1)S(1)}, u32[]{:S(2)}, u32[]{:S(2)}) collective-permute-start(bf16[128,640]{1,0:T(8,128)(2,1)} %refs_1_.3), channel_id=1, source_target_pairs={{0,16},{4,20},{8,24},{12,28},{16,0},{20,4},{24,8},{28,12},{1,17},{... | collective-permute-start | bytes 491528 | tf_op jit(solution)/shard_map/ppermute | solution.py:491
  11.2 1.6 collective-permute-start.8
  13.8 1.9 multiply_sine_fusion
  16.9 4.7 %collective-permute-done.2 = bf16[128,640]{1,0:T(8,128)(2,1)S(1)} collective-permute-done((bf16[128,640]{1,0:T(8,128)(2,1)S(1)}, bf16[128,640]{1,0:T(8,128)(2,1)S(1)}, u32[]{:S(2)}, u32[]{:S(2)}) %collective-permute-start.2) | collective-permute-done | bytes 163872 | tf_op jit(solution)/shard_map/ppermute | solution.py:491
  26.2 1.4 collective-permute-start.10
  28.5 7.3 %collective-permute-done.10.refs_5_.refs_18_ = bf16[256,640]{1,0:T(8,128)(2,1)S(1)} collective-permute-done((bf16[256,640]{1,0:T(8,128)(2,1)S(1)}, bf16[256,640]{1,0:T(8,128)(2,1)S(1)}, u32[]{:S(2)}, u32[]{:S(2)}) %collective-permute-start.10) | collective-permute-done | bytes 327712 | tf_op jit(solution)/shard_map/ppermute | solution.py:491
  35.9 1.5 collective-permute-done.5
  37.6 1.3 fusion.8
  39.7 3.0 %shard_map.204 = (bf16[1024,640]{1,0:T(8,128)(2,1)S(1)}, f32[1024,256]{1,0:T(8,128)S(1)}, bf16[1024,512]{1,0:T(8,128)(2,1)S(1)}, f32[4,128,256]{2,1,0:T(8,128)S(...) custom-call(s32[1]{0:T(128)} %bitcast.refs_0_, ...), custom_call_target="tpu_custom_call" | custom-call | flops 6600000000 | bytes 4395524 | tf_op jit(solution)/shard_map/pallas_call | solution.py:66
  48.3 1.2 collective-permute-start.19
  49.6 4.4 %collective-permute-done.12.refs_1_ = bf16[128,640]{1,0:T(8,128)(2,1)S(1)} collective-permute-done((bf16[128,640]{1,0:T(8,128)(2,1)S(1)}, bf16[128,640]{1,0:T(8,128)(2,1)S(1)}, u32[]{:S(2)}, u32[]{:S(2)}) %collective-permute-start.12) | collective-permute-done | bytes 163872 | tf_op jit(solution)/shard_map/ppermute | solution.py:491
  53.9 1.8 shard_map.206
  56.6 1.4 collective-permute-start.16
  58.1 4.1 %collective-permute-done.18.refs_6_.refs_3_ = bf16[128,416]{1,0:T(8,128)(2,1)S(1)} collective-permute-done((bf16[128,416]{1,0:T(8,128)(2,1)S(1)}, bf16[128,416]{1,0:T(8,128)(2,1)S(1)}, u32[]{:S(2)}, u32[]{:S(2)}) %collective-permute-start.18) | collective-permute-done | bytes 106528 | tf_op jit(solution)/shard_map/ppermute | solution.py:491
  62.2 3.1 %collective-permute-done.16.refs_1_ = bf16[128,640]{1,0:T(8,128)(2,1)S(1)} collective-permute-done((bf16[128,640]{1,0:T(8,128)(2,1)S(1)}, bf16[128,640]{1,0:T(8,128)(2,1)S(1)}, u32[]{:S(2)}, u32[]{:S(2)}) %collective-permute-start.16) | collective-permute-done | bytes 163872 | tf_op jit(solution)/shard_map/ppermute | solution.py:491
  66.9 5.2 %collective-permute-done.20.refs_1_ = bf16[128,640]{1,0:T(8,128)(2,1)S(1)} collective-permute-done((bf16[128,640]{1,0:T(8,128)(2,1)S(1)}, bf16[128,640]{1,0:T(8,128)(2,1)S(1)}, u32[]{:S(2)}, u32[]{:S(2)}) %collective-permute-start.20) | collective-permute-done | bytes 163872 | tf_op jit(solution)/shard_map/ppermute | solution.py:491
  72.1 1.7 shard_map.208
  84.7 1.5 shard_map.209
  90.0 5.0 %shard_map.211 = (bf16[592,512]{1,0:T(8,128)(2,1)}, f32[160,512]{1,0:T(8,128)S(1)}, f32[160,512]{1,0:T(8,128)S(1)}, bf16[512,512]{1,0:T(8,128)(2,1)S(1)}, bf16[512,512]{1,0:T(8,128)(2,1)S(1)}) custom-call(s32[1]{0:T(128)} %bitcast.refs_0_, bf16[128,640]{1,0:T(8,128)(2,1)S(1)} %get-tuple-element.118.refs_1_.refs_5_, f32[2,640]{1,0:T(2,128)S(1)} %get-tuple-element.119.refs_2_, ...), custom_call_target="tpu_custom_call" | custom-call | flops 9900000256 | bytes 7258116 | tf_op jit(solution)/shard_map/pallas_call | solution.py:66
  98.4 1.4 collective-permute-start.25
  100.6 1.6 collective-permute-start.24
  103.1 13.5 %collective-permute-done.25.refs_7_ = bf16[128,640]{1,0:T(8,128)(2,1)S(1)} collective-permute-done((bf16[128,640]{1,0:T(8,128)(2,1)}, bf16[128,640]{1,0:T(8,128)(2,1)S(1)}, u32[]{:S(2)}, u32[]{:S(2)}) %collective-permute-start.25) | collective-permute-done | bytes 163872 | tf_op jit(solution)/shard_map/ppermute | solution.py:491
  118.7 1.2 shard_map.213
  120.4 1.3 add_convert_fusion
  124.6 7.9 %collective-permute-done.31 = bf16[320,512]{1,0:T(8,128)(2,1)S(1)} collective-permute-done((bf16[320,512]{1,0:T(8,128)(2,1)S(1)}, bf16[320,512]{1,0:T(8,128)(2,1)S(1)}, u32[]{:S(2)}, u32[]{:S(2)}) %collective-permute-start.31) | collective-permute-done | bytes 327712 | tf_op jit(solution)/shard_map/ppermute | solution.py:491
  132.7 2.2 collective-permute-start.37
  134.8 1.5 shard_map.214
  137.0 8.7 %collective-permute-done.28 = bf16[480,512]{1,0:T(8,128)(2,1)S(1)} collective-permute-done((bf16[480,512]{1,0:T(8,128)(2,1)S(1)}, bf16[480,512]{1,0:T(8,128)(2,1)S(1)}, u32[]{:S(2)}, u32[]{:S(2)}) %collective-permute-start.28) | collective-permute-done | bytes 491552 | tf_op jit(solution)/shard_map/ppermute | solution.py:491
  146.7 1.8 collective-permute-start.41
  148.5 2.1 collective-permute-start.32
  150.6 1.9 collective-permute-start.33
  153.2 10.2 %collective-permute-done.41 = bf16[160,512]{1,0:T(8,128)(2,1)S(1)} collective-permute-done((bf16[160,512]{1,0:T(8,128)(2,1)S(1)}, bf16[160,512]{1,0:T(8,128)(2,1)S(1)}, u32[]{:S(2)}, u32[]{:S(2)}) %collective-permute-start.41) | collective-permute-done | bytes 163872 | tf_op jit(solution)/shard_map/ppermute | solution.py:491
  163.5 1.4 collective-permute-start.38
  164.8 3.3 %collective-permute-start.40 = (bf16[64,512]{1,0:T(8,128)(2,1)S(1)}, bf16[64,512]{1,0:T(8,128)(2,1)S(1)}, u32[]{:S(2)}, u32[]{:S(2)}) collective-permute-start(bf16[64,512]{1,0:T(8,128)(2,1)S(1)} %get-tuple-element.196), channel_id=1, source_target_pairs={{0,8},{4,12},{8,0},{12,4},{16,24},{20,28},{24,16},{28,20},{1,9},{5... | collective-permute-start | bytes 196616 | tf_op jit(solution)/shard_map/ppermute | solution.py:491
  168.2 3.6 %collective-permute-done.33 = bf16[128,512]{1,0:T(8,128)(2,1)S(1)} collective-permute-done((bf16[128,512]{1,0:T(8,128)(2,1)S(1)}, bf16[128,512]{1,0:T(8,128)(2,1)S(1)}, u32[]{:S(2)}, u32[]{:S(2)}) %collective-permute-start.33) | collective-permute-done | bytes 131104 | tf_op jit(solution)/shard_map/ppermute | solution.py:491
  171.8 3.2 %collective-permute-start.45 = (bf16[320,512]{1,0:T(8,128)(2,1)S(1)}, bf16[320,512]{1,0:T(8,128)(2,1)S(1)}, u32[]{:S(2)}, u32[]{:S(2)}) collective-permute-start(bf16[320,512]{1,0:T(8,128)(2,1)S(1)} %pad_maximum_fusion.5), channel_id=1, source_target_pairs={{0,8},{4,12},{8,0},{12,4},{16,24},{20,28},{24,16},{28,20},{1,9},{5... | collective-permute-start | bytes 983048 | tf_op jit(solution)/shard_map/ppermute | solution.py:491
  175.2 2.5 %collective-permute-start.43 = (bf16[64,512]{1,0:T(8,128)(2,1)S(1)}, bf16[64,512]{1,0:T(8,128)(2,1)S(1)}, u32[]{:S(2)}, u32[]{:S(2)}) collective-permute-start(bf16[64,512]{1,0:T(8,128)(2,1)S(1)} %add_convert_fusion.6), channel_id=1, source_target_pairs={{0,16},{4,20},{8,24},{12,28},{16,0},{20,4},{24,8},{28,12},{1,17},{... | collective-permute-start | bytes 196616 | tf_op jit(solution)/shard_map/ppermute | solution.py:491
  177.7 1.9 collective-permute-start.44
  179.7 9.6 %collective-permute-done.45 = bf16[320,512]{1,0:T(8,128)(2,1)S(1)} collective-permute-done((bf16[320,512]{1,0:T(8,128)(2,1)S(1)}, bf16[320,512]{1,0:T(8,128)(2,1)S(1)}, u32[]{:S(2)}, u32[]{:S(2)}) %collective-permute-start.45) | collective-permute-done | bytes 327712 | tf_op jit(solution)/shard_map/ppermute | solution.py:491
  191.6 2.7 %shard_map.215 = f32[128,640]{1,0:T(8,128)} custom-call(s32[1]{0:T(128)} %bitcast.refs_0_, bf16[128,640]{1,0:T(8,128)(2,1)S(1)} %copy-done.25, f32[128,512]{1,0:T(8,128)S(1)} %fusion.1.refs_2_, bf16[592,512]{1,0:T(8,128)(2,1)} %get-tuple-element.131.refs_0_.refs_3_, f32[128,640]{1,0:T(8,128)S(1)} %copy-done.67, ...), custom_call_target="tpu_custom_call" | custom-call | flops 1870000000 | bytes 3401732 | tf_op jit(solution)/shard_map/pallas_call | solution.py:66
  196.4 2.6 %collective-permute-done.49 = bf16[240,512]{1,0:T(8,128)(2,1)S(1)} collective-permute-done((bf16[240,512]{1,0:T(8,128)(2,1)S(1)}, bf16[240,512]{1,0:T(8,128)(2,1)S(1)}, u32[]{:S(2)}, u32[]{:S(2)}) %collective-permute-start.49) | collective-permute-done | bytes 245792 | tf_op jit(solution)/shard_map/ppermute | solution.py:491
  199.1 1.9 collective-permute-start.50
  201.1 3.5 %collective-permute-done.47.refs_2_ = bf16[256,512]{1,0:T(8,128)(2,1)S(1)} collective-permute-done((bf16[256,512]{1,0:T(8,128)(2,1)S(1)}, bf16[256,512]{1,0:T(8,128)(2,1)S(1)}, u32[]{:S(2)}, u32[]{:S(2)}) %collective-permute-start.47) | collective-permute-done | bytes 262176 | tf_op jit(solution)/shard_map/ppermute | solution.py:491
  207.2 9.2 %collective-permute-done.51.refs_2_ = bf16[640,512]{1,0:T(8,128)(2,1)S(1)} collective-permute-done((bf16[640,512]{1,0:T(8,128)(2,1)S(1)}, bf16[640,512]{1,0:T(8,128)(2,1)S(1)}, u32[]{:S(2)}, u32[]{:S(2)}) %collective-permute-start.51) | collective-permute-done | bytes 655392 | tf_op jit(solution)/shard_map/ppermute | solution.py:491
  216.4 1.7 shard_map.218
  218.1 1.4 shard_map.217
  (344 shorter events, 54.6 us)
Async XLA Ops:
  0.7 15.1 %collective-permute-start.1 = (bf16[128,640]{1,0:T(8,128)(2,1)}, bf16[128,640]{1,0:T(8,128)(2,1)S(1)}, u32[]{:S(2)}, u32[]{:S(2)}) collective-permute-start(bf16[128,640]{1,0:T(8,128)(2,1)} %refs_1_.3), channel_id=1, source_target_pairs={{0,8},{4,12},{8,0},{12,4},{16,24},{20,28},{24,16},{28,20},{1,9},{5... | collective-permute-start | bytes 491528 | tf_op jit(solution)/shard_map/ppermute | solution.py:491
  3.7 12.6 %collective-permute-start = (bf16[128,640]{1,0:T(8,128)(2,1)}, bf16[128,640]{1,0:T(8,128)(2,1)S(1)}, u32[]{:S(2)}, u32[]{:S(2)}) collective-permute-start(bf16[128,640]{1,0:T(8,128)(2,1)} %refs_1_.3), channel_id=1, source_target_pairs={{0,4},{4,0},{8,12},{12,8},{16,20},{20,16},{24,28},{28,24},{1,5},{5... | collective-permute-start | bytes 491528 | tf_op jit(solution)/shard_map/ppermute | solution.py:491
  5.2 16.4 %collective-permute-start.3 = (bf16[128,640]{1,0:T(8,128)(2,1)}, bf16[128,640]{1,0:T(8,128)(2,1)S(1)}, u32[]{:S(2)}, u32[]{:S(2)}) collective-permute-start(bf16[128,640]{1,0:T(8,128)(2,1)} %refs_1_.3), channel_id=1, source_target_pairs={{0,16},{4,20},{8,24},{12,28},{16,0},{20,4},{24,8},{28,12},{1,17},{... | collective-permute-start | bytes 491528 | tf_op jit(solution)/shard_map/ppermute | solution.py:491
  7.8 13.9 %collective-permute-start.4 = (bf16[128,640]{1,0:T(8,128)(2,1)}, bf16[128,640]{1,0:T(8,128)(2,1)S(1)}, u32[]{:S(2)}, u32[]{:S(2)}) collective-permute-start(bf16[128,640]{1,0:T(8,128)(2,1)} %refs_1_.3), channel_id=1, source_target_pairs={{0,24},{4,28},{8,16},{12,20},{16,8},{20,12},{24,0},{28,4},{1,25},{... | collective-permute-start | bytes 491528 | tf_op jit(solution)/shard_map/ppermute | solution.py:491
  11.2 10.6 %collective-permute-start.8 = (bf16[176,512]{1,0:T(8,128)(2,1)S(1)}, bf16[176,512]{1,0:T(8,128)(2,1)S(1)}, u32[]{:S(2)}, u32[]{:S(2)}) collective-permute-start(bf16[176,512]{1,0:T(8,128)(2,1)S(1)} %shard_map.203.refs_10_), channel_id=1, source_target_pairs={{0,2},{1,3},{2,0},{3,1},{4,6},{5,7},{6,4},{7,5},{8,10},{9,11},{10,... | collective-permute-start | bytes 540680 | tf_op jit(solution)/shard_map/ppermute | solution.py:491
  15.7 8.2 %collective-permute-start.6 = (bf16[160,1024]{1,0:T(8,128)(2,1)S(1)}, bf16[160,1024]{1,0:T(8,128)(2,1)S(1)}, u32[]{:S(2)}, u32[]{:S(2)}) collective-permute-start(bf16[160,1024]{1,0:T(8,128)(2,1)S(1)} %copy-done.2), channel_id=1, source_target_pairs={{0,2},{1,3},{2,0},{3,1},{4,6},{5,7},{6,4},{7,5},{8,10},{9,11},{10,... | collective-permute-start | bytes 983048 | tf_op jit(solution)/shard_map/ppermute | solution.py:491
  16.3 5.3 %collective-permute-start.2 = (bf16[128,640]{1,0:T(8,128)(2,1)S(1)}, bf16[128,640]{1,0:T(8,128)(2,1)S(1)}, u32[]{:S(2)}, u32[]{:S(2)}) collective-permute-start(bf16[128,640]{1,0:T(8,128)(2,1)S(1)} %collective-permute-done.1), channel_id=1, source_target_pairs={{0,4},{4,0},{8,12},{12,8},{16,20},{20,16},{24,28},{28,24},{1,5},{5... | collective-permute-start | bytes 491528 | tf_op jit(solution)/shard_map/ppermute | solution.py:491
  24.9 10.9 %collective-permute-start.7 = (bf16[320,1024]{1,0:T(8,128)(2,1)}, bf16[320,1024]{1,0:T(8,128)(2,1)}, u32[]{:S(2)}, u32[]{:S(2)}) collective-permute-start(bf16[320,1024]{1,0:T(8,128)(2,1)} %pad_maximum_fusion), channel_id=1, source_target_pairs={{0,1},{1,0},{2,3},{3,2},{4,5},{5,4},{6,7},{7,6},{8,9},{9,8},{10,11... | collective-permute-start | bytes 1966088 | tf_op jit(solution)/shard_map/ppermute | solution.py:491
  26.2 9.6 %collective-permute-start.10 = (bf16[256,640]{1,0:T(8,128)(2,1)S(1)}, bf16[256,640]{1,0:T(8,128)(2,1)S(1)}, u32[]{:S(2)}, u32[]{:S(2)}) collective-permute-start(bf16[256,640]{1,0:T(8,128)(2,1)S(1)} %copy-done), channel_id=1, source_target_pairs={{0,2},{1,3},{2,0},{3,1},{4,6},{5,7},{6,4},{7,5},{8,10},{9,11},{10,... | collective-permute-start | bytes 983048 | tf_op jit(solution)/shard_map/ppermute | solution.py:491
  27.8 9.6 %collective-permute-start.5 = (bf16[256,640]{1,0:T(8,128)(2,1)}, bf16[256,640]{1,0:T(8,128)(2,1)S(1)}, u32[]{:S(2)}, u32[]{:S(2)}) collective-permute-start(bf16[256,640]{1,0:T(8,128)(2,1)} %copy-done.94), channel_id=1, source_target_pairs={{0,4},{4,0},{8,12},{12,8},{16,20},{20,16},{24,28},{28,24},{1,5},{5... | collective-permute-start | bytes 983048 | tf_op jit(solution)/shard_map/ppermute | solution.py:491
  39.0 15.0 %collective-permute-start.13 = (bf16[640,512]{1,0:T(8,128)(2,1)S(1)}, bf16[640,512]{1,0:T(8,128)(2,1)S(1)}, u32[]{:S(2)}, u32[]{:S(2)}) collective-permute-start(bf16[640,512]{1,0:T(8,128)(2,1)S(1)} %copy-done.40), channel_id=1, source_target_pairs={{0,1},{1,0},{2,3},{3,2},{4,5},{5,4},{6,7},{7,6},{8,9},{9,8},{10,11... | collective-permute-start | bytes 1966088 | tf_op jit(solution)/shard_map/ppermute | solution.py:491
  39.0 14.9 %collective-permute-start.14 = (bf16[640,512]{1,0:T(8,128)(2,1)S(1)}, bf16[640,512]{1,0:T(8,128)(2,1)S(1)}, u32[]{:S(2)}, u32[]{:S(2)}) collective-permute-start(bf16[640,512]{1,0:T(8,128)(2,1)S(1)} %copy-done.41), channel_id=1, source_target_pairs={{0,1},{1,0},{2,3},{3,2},{4,5},{5,4},{6,7},{7,6},{8,9},{9,8},{10,11... | collective-permute-start | bytes 1966088 | tf_op jit(solution)/shard_map/ppermute | solution.py:491
  39.5 14.4 %collective-permute-start.15 = (bf16[512,640]{1,0:T(8,128)(2,1)S(1)}, bf16[512,640]{1,0:T(8,128)(2,1)S(1)}, u32[]{:S(2)}, u32[]{:S(2)}) collective-permute-start(bf16[512,640]{1,0:T(8,128)(2,1)S(1)} %copy-done.42), channel_id=1, source_target_pairs={{0,1},{1,0},{2,3},{3,2},{4,5},{5,4},{6,7},{7,6},{8,9},{9,8},{10,11... | collective-permute-start | bytes 1966088 | tf_op jit(solution)/shard_map/ppermute | solution.py:491
  46.9 7.0 %collective-permute-start.12 = (bf16[128,640]{1,0:T(8,128)(2,1)S(1)}, bf16[128,640]{1,0:T(8,128)(2,1)S(1)}, u32[]{:S(2)}, u32[]{:S(2)}) collective-permute-start(bf16[128,640]{1,0:T(8,128)(2,1)S(1)} %get-tuple-element.98.refs_0_), channel_id=1, source_target_pairs={{0,2},{1,3},{2,0},{3,1},{4,6},{5,7},{6,4},{7,5},{8,10},{9,11},{10,... | collective-permute-start | bytes 491528 | tf_op jit(solution)/shard_map/ppermute | solution.py:491
  48.3 9.7 %collective-permute-start.19 = (bf16[128,416]{1,0:T(8,128)(2,1)S(1)}, bf16[128,416]{1,0:T(8,128)(2,1)S(1)}, u32[]{:S(2)}, u32[]{:S(2)}) collective-permute-start(bf16[128,416]{1,0:T(8,128)(2,1)S(1)} %pad_maximum_fusion.9), channel_id=1, source_target_pairs={{0,3},{1,2},{2,1},{3,0},{4,7},{5,6},{6,5},{7,4},{8,11},{9,10},{10,... | collective-permute-start | bytes 319496 | tf_op jit(solution)/shard_map/ppermute | solution.py:491
  55.8 16.3 %collective-permute-start.21 = (bf16[256,1152]{1,0:T(8,128)(2,1)S(1)}, bf16[256,1152]{1,0:T(8,128)(2,1)S(1)}, u32[]{:S(2)}, u32[]{:S(2)}) collective-permute-start(bf16[256,1152]{1,0:T(8,128)(2,1)S(1)} %get-tuple-element.110.refs_0_), channel_id=1, source_target_pairs={{0,1},{1,0},{2,3},{3,2},{4,5},{5,4},{6,7},{7,6},{8,9},{9,8},{10,11... | collective-permute-start | bytes 1769480 | tf_op jit(solution)/shard_map/ppermute | solution.py:491
  55.9 6.4 %collective-permute-start.18 = (bf16[128,416]{1,0:T(8,128)(2,1)S(1)}, bf16[128,416]{1,0:T(8,128)(2,1)S(1)}, u32[]{:S(2)}, u32[]{:S(2)}) collective-permute-start(bf16[128,416]{1,0:T(8,128)(2,1)S(1)} %pad_maximum_fusion.8), channel_id=1, source_target_pairs={{0,2},{1,3},{2,0},{3,1},{4,6},{5,7},{6,4},{7,5},{8,10},{9,11},{10,... | collective-permute-start | bytes 319496 | tf_op jit(solution)/shard_map/ppermute | solution.py:491
  56.6 8.8 %collective-permute-start.16 = (bf16[128,640]{1,0:T(8,128)(2,1)S(1)}, bf16[128,640]{1,0:T(8,128)(2,1)S(1)}, u32[]{:S(2)}, u32[]{:S(2)}) collective-permute-start(bf16[128,640]{1,0:T(8,128)(2,1)S(1)} %get-tuple-element.103), channel_id=1, source_target_pairs={{0,2},{1,3},{2,0},{3,1},{4,6},{5,7},{6,4},{7,5},{8,10},{9,11},{10,... | collective-permute-start | bytes 491528 | tf_op jit(solution)/shard_map/ppermute | solution.py:491
  66.2 5.9 %collective-permute-start.20 = (bf16[128,640]{1,0:T(8,128)(2,1)S(1)}, bf16[128,640]{1,0:T(8,128)(2,1)S(1)}, u32[]{:S(2)}, u32[]{:S(2)}) collective-permute-start(bf16[128,640]{1,0:T(8,128)(2,1)S(1)} %get-tuple-element.107.refs_0_), channel_id=1, source_target_pairs={{0,2},{1,3},{2,0},{3,1},{4,6},{5,7},{6,4},{7,5},{8,10},{9,11},{10,... | collective-permute-start | bytes 491528 | tf_op jit(solution)/shard_map/ppermute | solution.py:491
  76.9 9.4 %collective-permute-start.22 = (bf16[128,640]{1,0:T(8,128)(2,1)}, bf16[128,640]{1,0:T(8,128)(2,1)S(1)}, u32[]{:S(2)}, u32[]{:S(2)}) collective-permute-start(bf16[128,640]{1,0:T(8,128)(2,1)} %copy-done.48), channel_id=1, source_target_pairs={{0,2},{1,3},{2,0},{3,1},{4,6},{5,7},{6,4},{7,5},{8,10},{9,11},{10,... | collective-permute-start | bytes 491528 | tf_op jit(solution)/shard_map/ppermute | solution.py:491
  97.2 19.6 %collective-permute-start.29 = (bf16[592,512]{1,0:T(8,128)(2,1)}, bf16[592,512]{1,0:T(8,128)(2,1)S(1)}, u32[]{:S(2)}, u32[]{:S(2)}) collective-permute-start(bf16[592,512]{1,0:T(8,128)(2,1)} %get-tuple-element.131.refs_0_.refs_3_), channel_id=1, source_target_pairs={{0,2},{1,3},{2,0},{3,1},{4,6},{5,7},{6,4},{7,5},{8,10},{9,11},{10,... | collective-permute-start | bytes 1818632 | tf_op jit(solution)/shard_map/ppermute | solution.py:491
  97.8 22.6 %collective-permute-start.27 = (bf16[640,512]{1,0:T(8,128)(2,1)S(1)}, bf16[640,512]{1,0:T(8,128)(2,1)}, u32[]{:S(2)}, u32[]{:S(2)}) collective-permute-start(bf16[640,512]{1,0:T(8,128)(2,1)S(1)} %broadcast_select_fusion.refs_6_), channel_id=1, source_target_pairs={{0,4},{4,0},{8,12},{12,8},{16,20},{20,16},{24,28},{28,24},{1,5},{5... | collective-permute-start | bytes 1966088 | tf_op jit(solution)/shard_map/ppermute | solution.py:491
  98.4 18.3 %collective-permute-start.25 = (bf16[128,640]{1,0:T(8,128)(2,1)}, bf16[128,640]{1,0:T(8,128)(2,1)S(1)}, u32[]{:S(2)}, u32[]{:S(2)}) collective-permute-start(bf16[128,640]{1,0:T(8,128)(2,1)} %copy-done.26), channel_id=1, source_target_pairs={{0,2},{1,3},{2,0},{3,1},{4,6},{5,7},{6,4},{7,5},{8,10},{9,11},{10,... | collective-permute-start | bytes 491528 | tf_op jit(solution)/shard_map/ppermute | solution.py:491
  100.6 45.8 %collective-permute-start.24 = (bf16[512,512]{1,0:T(8,128)(2,1)}, bf16[512,512]{1,0:T(8,128)(2,1)S(1)}, u32[]{:S(2)}, u32[]{:S(2)}) collective-permute-start(bf16[512,512]{1,0:T(8,128)(2,1)} %copy-done.45), channel_id=1, source_target_pairs={{0,4},{4,0},{8,12},{12,8},{16,20},{20,16},{24,28},{28,24},{1,5},{5... | collective-permute-start | bytes 1572872 | tf_op jit(solution)/shard_map/ppermute | solution.py:491
  116.7 6.0 %collective-permute-start.26 = (bf16[256,640]{1,0:T(8,128)(2,1)S(1)}, bf16[256,640]{1,0:T(8,128)(2,1)S(1)}, u32[]{:S(2)}, u32[]{:S(2)}) collective-permute-start(bf16[256,640]{1,0:T(8,128)(2,1)S(1)} %constant_dynamic-update-slice_fusion.8), channel_id=1, source_target_pairs={{0,1},{1,0},{2,3},{3,2},{4,5},{5,4},{6,7},{7,6},{8,9},{9,8},{10,11... | collective-permute-start | bytes 983048 | tf_op jit(solution)/shard_map/ppermute | solution.py:491
  119.9 15.0 %collective-permute-start.30 = (bf16[704,512]{1,0:T(8,128)(2,1)S(1)}, bf16[704,512]{1,0:T(8,128)(2,1)S(1)}, u32[]{:S(2)}, u32[]{:S(2)}) collective-permute-start(bf16[704,512]{1,0:T(8,128)(2,1)S(1)} %get-tuple-element.138), channel_id=1, source_target_pairs={{0,1},{1,0},{2,3},{3,2},{4,5},{5,4},{6,7},{7,6},{8,9},{9,8},{10,11... | collective-permute-start | bytes 2162696 | tf_op jit(solution)/shard_map/ppermute | solution.py:491
  121.9 10.6 %collective-permute-start.31 = (bf16[320,512]{1,0:T(8,128)(2,1)S(1)}, bf16[320,512]{1,0:T(8,128)(2,1)S(1)}, u32[]{:S(2)}, u32[]{:S(2)}) collective-permute-start(bf16[320,512]{1,0:T(8,128)(2,1)S(1)} %broadcast_select_fusion.4), channel_id=1, source_target_pairs={{0,8},{4,12},{8,0},{12,4},{16,24},{20,28},{24,16},{28,20},{1,9},{5... | collective-permute-start | bytes 983048 | tf_op jit(solution)/shard_map/ppermute | solution.py:491
  123.6 22.0 %collective-permute-start.28 = (bf16[480,512]{1,0:T(8,128)(2,1)S(1)}, bf16[480,512]{1,0:T(8,128)(2,1)S(1)}, u32[]{:S(2)}, u32[]{:S(2)}) collective-permute-start(bf16[480,512]{1,0:T(8,128)(2,1)S(1)} %broadcast_select_fusion.1), channel_id=1, source_target_pairs={{0,8},{4,12},{8,0},{12,4},{16,24},{20,28},{24,16},{28,20},{1,9},{5... | collective-permute-start | bytes 1474568 | tf_op jit(solution)/shard_map/ppermute | solution.py:491
  132.7 14.0 %collective-permute-start.37 = (bf16[160,512]{1,0:T(8,128)(2,1)S(1)}, bf16[160,512]{1,0:T(8,128)(2,1)S(1)}, u32[]{:S(2)}, u32[]{:S(2)}) collective-permute-start(bf16[160,512]{1,0:T(8,128)(2,1)S(1)} %broadcast_select_fusion.11), channel_id=1, source_target_pairs={{0,16},{4,20},{8,24},{12,28},{16,0},{20,4},{24,8},{28,12},{1,17},{... | collective-permute-start | bytes 491528 | tf_op jit(solution)/shard_map/ppermute | solution.py:491
  136.4 16.1 %collective-permute-start.36 = (bf16[256,512]{1,0:T(8,128)(2,1)S(1)}, bf16[256,512]{1,0:T(8,128)(2,1)S(1)}, u32[]{:S(2)}, u32[]{:S(2)}) collective-permute-start(bf16[256,512]{1,0:T(8,128)(2,1)S(1)} %broadcast_select_fusion.5), channel_id=1, source_target_pairs={{0,4},{4,0},{8,12},{12,8},{16,20},{20,16},{24,28},{28,24},{1,5},{5... | collective-permute-start | bytes 786440 | tf_op jit(solution)/shard_map/ppermute | solution.py:491
  145.8 7.2 %collective-permute-start.35 = (bf16[240,512]{1,0:T(8,128)(2,1)S(1)}, bf16[240,512]{1,0:T(8,128)(2,1)S(1)}, u32[]{:S(2)}, u32[]{:S(2)}) collective-permute-start(bf16[240,512]{1,0:T(8,128)(2,1)S(1)} %broadcast_select_fusion.8), channel_id=1, source_target_pairs={{0,4},{4,0},{8,12},{12,8},{16,20},{20,16},{24,28},{28,24},{1,5},{5... | collective-permute-start | bytes 737288 | tf_op jit(solution)/shard_map/ppermute | solution.py:491
  146.7 16.7 %collective-permute-start.41 = (bf16[160,512]{1,0:T(8,128)(2,1)S(1)}, bf16[160,512]{1,0:T(8,128)(2,1)S(1)}, u32[]{:S(2)}, u32[]{:S(2)}) collective-permute-start(bf16[160,512]{1,0:T(8,128)(2,1)S(1)} %add_convert_fusion.4), channel_id=1, source_target_pairs={{0,16},{4,20},{8,24},{12,28},{16,0},{20,4},{24,8},{28,12},{1,17},{... | collective-permute-start | bytes 491528 | tf_op jit(solution)/shard_map/ppermute | solution.py:491
  148.5 16.3 %collective-permute-start.32 = (bf16[128,512]{1,0:T(8,128)(2,1)S(1)}, bf16[128,512]{1,0:T(8,128)(2,1)S(1)}, u32[]{:S(2)}, u32[]{:S(2)}) collective-permute-start(bf16[128,512]{1,0:T(8,128)(2,1)S(1)} %get-tuple-element.187), channel_id=1, source_target_pairs={{0,24},{4,28},{8,16},{12,20},{16,8},{20,12},{24,0},{28,4},{1,25},{... | collective-permute-start | bytes 393224 | tf_op jit(solution)/shard_map/ppermute | solution.py:491
  150.6 21.2 %collective-permute-start.33 = (bf16[128,512]{1,0:T(8,128)(2,1)S(1)}, bf16[128,512]{1,0:T(8,128)(2,1)S(1)}, u32[]{:S(2)}, u32[]{:S(2)}) collective-permute-start(bf16[128,512]{1,0:T(8,128)(2,1)S(1)} %get-tuple-element.186), channel_id=1, source_target_pairs={{0,16},{4,20},{8,24},{12,28},{16,0},{20,4},{24,8},{28,12},{1,17},{... | collective-permute-start | bytes 393224 | tf_op jit(solution)/shard_map/ppermute | solution.py:491
  152.5 19.3 %collective-permute-start.34 = (bf16[128,512]{1,0:T(8,128)(2,1)S(1)}, bf16[128,512]{1,0:T(8,128)(2,1)S(1)}, u32[]{:S(2)}, u32[]{:S(2)}) collective-permute-start(bf16[128,512]{1,0:T(8,128)(2,1)S(1)} %get-tuple-element.185), channel_id=1, source_target_pairs={{0,8},{4,12},{8,0},{12,4},{16,24},{20,28},{24,16},{28,20},{1,9},{5... | collective-permute-start | bytes 393224 | tf_op jit(solution)/shard_map/ppermute | solution.py:491
  163.5 11.6 %collective-permute-start.38 = (bf16[64,512]{1,0:T(8,128)(2,1)S(1)}, bf16[64,512]{1,0:T(8,128)(2,1)S(1)}, u32[]{:S(2)}, u32[]{:S(2)}) collective-permute-start(bf16[64,512]{1,0:T(8,128)(2,1)S(1)} %get-tuple-element.198), channel_id=1, source_target_pairs={{0,24},{4,28},{8,16},{12,20},{16,8},{20,12},{24,0},{28,4},{1,25},{... | collective-permute-start | bytes 196616 | tf_op jit(solution)/shard_map/ppermute | solution.py:491
  164.8 10.2 %collective-permute-start.39 = (bf16[64,512]{1,0:T(8,128)(2,1)S(1)}, bf16[64,512]{1,0:T(8,128)(2,1)S(1)}, u32[]{:S(2)}, u32[]{:S(2)}) collective-permute-start(bf16[64,512]{1,0:T(8,128)(2,1)S(1)} %get-tuple-element.197), channel_id=1, source_target_pairs={{0,16},{4,20},{8,24},{12,28},{16,0},{20,4},{24,8},{28,12},{1,17},{... | collective-permute-start | bytes 196616 | tf_op jit(solution)/shard_map/ppermute | solution.py:491
  164.8 10.2 %collective-permute-start.40 = (bf16[64,512]{1,0:T(8,128)(2,1)S(1)}, bf16[64,512]{1,0:T(8,128)(2,1)S(1)}, u32[]{:S(2)}, u32[]{:S(2)}) collective-permute-start(bf16[64,512]{1,0:T(8,128)(2,1)S(1)} %get-tuple-element.196), channel_id=1, source_target_pairs={{0,8},{4,12},{8,0},{12,4},{16,24},{20,28},{24,16},{28,20},{1,9},{5... | collective-permute-start | bytes 196616 | tf_op jit(solution)/shard_map/ppermute | solution.py:491
  171.8 7.7 %collective-permute-start.46 = (bf16[120,512]{1,0:T(8,128)(2,1)S(1)}, bf16[120,512]{1,0:T(8,128)(2,1)S(1)}, u32[]{:S(2)}, u32[]{:S(2)}) collective-permute-start(bf16[120,512]{1,0:T(8,128)(2,1)S(1)} %broadcast_select_fusion.14), channel_id=1, source_target_pairs={{0,16},{4,20},{8,24},{12,28},{16,0},{20,4},{24,8},{28,12},{1,17},{... | collective-permute-start | bytes 368648 | tf_op jit(solution)/shard_map/ppermute | solution.py:491
  171.8 17.4 %collective-permute-start.45 = (bf16[320,512]{1,0:T(8,128)(2,1)S(1)}, bf16[320,512]{1,0:T(8,128)(2,1)S(1)}, u32[]{:S(2)}, u32[]{:S(2)}) collective-permute-start(bf16[320,512]{1,0:T(8,128)(2,1)S(1)} %pad_maximum_fusion.5), channel_id=1, source_target_pairs={{0,8},{4,12},{8,0},{12,4},{16,24},{20,28},{24,16},{28,20},{1,9},{5... | collective-permute-start | bytes 983048 | tf_op jit(solution)/shard_map/ppermute | solution.py:491
  175.1 15.2 %collective-permute-start.42 = (bf16[64,512]{1,0:T(8,128)(2,1)S(1)}, bf16[64,512]{1,0:T(8,128)(2,1)S(1)}, u32[]{:S(2)}, u32[]{:S(2)}) collective-permute-start(bf16[64,512]{1,0:T(8,128)(2,1)S(1)} %add_convert_fusion.6), channel_id=1, source_target_pairs={{0,8},{4,12},{8,0},{12,4},{16,24},{20,28},{24,16},{28,20},{1,9},{5... | collective-permute-start | bytes 196616 | tf_op jit(solution)/shard_map/ppermute | solution.py:491
  175.2 15.1 %collective-permute-start.43 = (bf16[64,512]{1,0:T(8,128)(2,1)S(1)}, bf16[64,512]{1,0:T(8,128)(2,1)S(1)}, u32[]{:S(2)}, u32[]{:S(2)}) collective-permute-start(bf16[64,512]{1,0:T(8,128)(2,1)S(1)} %add_convert_fusion.6), channel_id=1, source_target_pairs={{0,16},{4,20},{8,24},{12,28},{16,0},{20,4},{24,8},{28,12},{1,17},{... | collective-permute-start | bytes 196616 | tf_op jit(solution)/shard_map/ppermute | solution.py:491
  177.7 12.6 %collective-permute-start.44 = (bf16[64,512]{1,0:T(8,128)(2,1)S(1)}, bf16[64,512]{1,0:T(8,128)(2,1)S(1)}, u32[]{:S(2)}, u32[]{:S(2)}) collective-permute-start(bf16[64,512]{1,0:T(8,128)(2,1)S(1)} %add_convert_fusion.6), channel_id=1, source_target_pairs={{0,24},{4,28},{8,16},{12,20},{16,8},{20,12},{24,0},{28,4},{1,25},{... | collective-permute-start | bytes 196616 | tf_op jit(solution)/shard_map/ppermute | solution.py:491
  179.6 10.8 %collective-permute-start.48 = (bf16[120,512]{1,0:T(8,128)(2,1)S(1)}, bf16[120,512]{1,0:T(8,128)(2,1)S(1)}, u32[]{:S(2)}, u32[]{:S(2)}) collective-permute-start(bf16[120,512]{1,0:T(8,128)(2,1)S(1)} %add_convert_fusion.5), channel_id=1, source_target_pairs={{0,16},{4,20},{8,24},{12,28},{16,0},{20,4},{24,8},{28,12},{1,17},{... | collective-permute-start | bytes 368648 | tf_op jit(solution)/shard_map/ppermute | solution.py:491
  190.4 8.5 %collective-permute-start.49 = (bf16[240,512]{1,0:T(8,128)(2,1)S(1)}, bf16[240,512]{1,0:T(8,128)(2,1)S(1)}, u32[]{:S(2)}, u32[]{:S(2)}) collective-permute-start(bf16[240,512]{1,0:T(8,128)(2,1)S(1)} %pad_maximum_fusion.6), channel_id=1, source_target_pairs={{0,4},{4,0},{8,12},{12,8},{16,20},{20,16},{24,28},{28,24},{1,5},{5... | collective-permute-start | bytes 737288 | tf_op jit(solution)/shard_map/ppermute | solution.py:491
  194.4 10.2 %collective-permute-start.47 = (bf16[256,512]{1,0:T(8,128)(2,1)S(1)}, bf16[256,512]{1,0:T(8,128)(2,1)S(1)}, u32[]{:S(2)}, u32[]{:S(2)}) collective-permute-start(bf16[256,512]{1,0:T(8,128)(2,1)S(1)} %constant_dynamic-update-slice_fusion.10.refs_1_), channel_id=1, source_target_pairs={{0,4},{4,0},{8,12},{12,8},{16,20},{20,16},{24,28},{28,24},{1,5},{5... | collective-permute-start | bytes 786440 | tf_op jit(solution)/shard_map/ppermute | solution.py:491
  195.4 20.9 %collective-permute-start.51 = (bf16[640,512]{1,0:T(8,128)(2,1)S(1)}, bf16[640,512]{1,0:T(8,128)(2,1)S(1)}, u32[]{:S(2)}, u32[]{:S(2)}) collective-permute-start(bf16[640,512]{1,0:T(8,128)(2,1)S(1)} %pad_maximum_fusion.2.refs_1_), channel_id=1, source_target_pairs={{0,4},{4,0},{8,12},{12,8},{16,20},{20,16},{24,28},{28,24},{1,5},{5... | collective-permute-start | bytes 1966088 | tf_op jit(solution)/shard_map/ppermute | solution.py:491
  199.1 18.9 %collective-permute-start.50 = (bf16[480,512]{1,0:T(8,128)(2,1)S(1)}, bf16[480,512]{1,0:T(8,128)(2,1)S(1)}, u32[]{:S(2)}, u32[]{:S(2)}) collective-permute-start(bf16[480,512]{1,0:T(8,128)(2,1)S(1)} %pad_maximum_fusion.3.refs_1_), channel_id=1, source_target_pairs={{0,8},{4,12},{8,0},{12,4},{16,24},{20,28},{24,16},{28,20},{1,9},{5... | collective-permute-start | bytes 1474568 | tf_op jit(solution)/shard_map/ppermute | solution.py:491
  (100 other events, 380.3 us)

commit v4 on v3

--- a/solution.py
+++ b/solution.py
@@ -52,7 +52,7 @@
     return jnp.concatenate([a * cos + b * sin, b * cos - a * sin], axis=-1)
 
 
-def call(kernel, outs, *args, scratch=(), vmem=20, us=1.0, smem=0, after=()):
+def call(kernel, outs, *args, scratch=(), vmem=16, us=1.0, smem=0, after=()):
     specs = [pl.BlockSpec(memory_space=pltpu.VMEM)] * len(args)
     for i in range(smem):
         specs[i] = pl.BlockSpec(memory_space=pltpu.SMEM)
@@ -527,12 +527,11 @@
             bit *= 2
         return x, x
     far = {k: swap(x, "ctx", n, k) for k in range(n - 2, 0, -2)}
-    near = swap(x, "ctx", n, 1)
     rows = x.shape[0]
-    first = swap(far[2], "ctx", n, 1)
+    first = swap(jnp.concatenate([x, far[2]], axis=0), "ctx", n, 1)
     ahead = jnp.concatenate([far[k] for k in range(4, n, 2)], axis=0)
     second = swap(ahead, "ctx", n, 1)
-    parts = [x, near, far[2], first]
+    parts = [x, first[:rows], far[2], first[rows:]]
     for i, k in enumerate(range(4, n, 2)):
         parts += [far[k], second[i * rows : (i + 1) * rows]]
     return jnp.concatenate(parts, axis=0), ahead
@@ -665,7 +664,7 @@
     own_ff = (gate_weight, up_weight, down_weight)
     next_ff = [swap(w, "fsdp", nf, 1) for w in lax.optimization_barrier(own_ff + (wo[1],))[:3]]
 
-    big = 36 if seq <= 1024 else 60
+    big = 16 if seq <= 1024 else 60
     normed, kraw, kv, qraw, q, att, att_low, tot, gains, hg = call(
         functools.partial(front_kernel, nf, tile),
         [
@@ -730,7 +729,7 @@
     up_bits = [1 << i for i in range(nc.bit_length() - 1)]
     alt_bits = up_bits[1:2] + up_bits[:1] + up_bits[2:]
     p_sum, q_sum, a_sum, kv_sum = [], [], [], []
-    p_steps = sum_steps(p_part, nc, c, up_bits, order, p_sum)
+    p_steps = sum_steps(p_part, nc, c, alt_bits, order, p_sum)
     next(p_steps)
     gbl, resid, gain12 = call(
         post_kernel,
@@ -760,7 +759,7 @@
             pltpu.VMEM((d + 8, wide), F32),
             pltpu.VMEM((rows, proj), BF),
         ],
-        smem=1, vmem=big, us=9,
+        smem=1, vmem=big, us=9, after=[gbl_far],
     )
     far = swap(order.leaves(ybuf), "fsdp", nf, 2)
     gbl_both = swap(
@@ -775,7 +774,7 @@
         scratch=[pltpu.VMEM((nf * rows, proj // nf), BF), pltpu.VMEM((nf * rows, d), BF)],
         us=1.3,
     )
-    q_steps = sum_steps(q_part, nc, c, alt_bits, order, q_sum)
+    q_steps = sum_steps(q_part, nc, c, up_bits, order, q_sum)
     next(q_steps)
     kv_steps = scatter_steps(odd, even, nc, order, kv_sum)
     next(kv_steps)
@@ -815,12 +814,13 @@
         scratch=[pltpu.VMEM((d, qkv), BF)], smem=1, us=1.7,
     )
     upper = (c & up_bits[0]).reshape(1).astype(jnp.int32)
+    alt = (c & alt_bits[0]).reshape(1).astype(jnp.int32)
     grad_gate, grad_down = call(
-        last_ff_kernel, [((d, width), F32), ((width, d), F32)], upper, *p_sum, smem=1
+        last_ff_kernel, [((d, width), F32), ((width, d), F32)], alt, *p_sum, smem=1
     )
     grad_up, grad_out = call(
         last_ff_kernel, [((d, width), F32), ((proj // nf, d), F32)],
-        (c & alt_bits[0]).reshape(1).astype(jnp.int32), *q_sum, smem=1,
+        upper, *q_sum, smem=1,
     )
     grad_q, grad_k, grad_v, gain0, gain_sum = call(
         last_kernel,

time: 220 us -> 200 us (0.909)
  local copies, waits for them, and re-layouts: 30.3 us -> 20.9 us
  waiting for transfers between devices: 102 us -> 93.8 us
    unnamed x200 -> x148, local copies, waits for them, and re-layouts: 25.5 us -> 15.5 us
    ppermute x52 -> x51, waiting for transfers between devices: 102 us -> 93.8 us  [swap(): return lax.ppermute(x, axis, [(i, i ^ bit) for i in range(n)])]
    ppermute x52 -> x51, starting transfers between devices: 52.2 us -> 54.2 us  [swap(): return lax.ppermute(x, axis, [(i, i ^ bit) for i in range(n)])]
  transfers between devices with their start and end apart: 52 -> 51, of which waited for: 19 -> 23; matrix products, arithmetic and copies ran while one was open for 6% -> 6% of each run, Pallas kernels for 7% -> 9%
where the time goes in v4:
time: 200 us
  waiting for transfers between devices  93.8 us (47%)
  starting transfers between devices  54.2 us (27%)
  Pallas kernels  22.9 us (11%)
  local copies, waits for them, and re-layouts  20.9 us (10%)
  other arithmetic  6.42 us (3%)
    ppermute x51, waiting for transfers between devices, swap(): return lax.ppermute(x, axis, [(i, i ^ bit) for i in range(n)])  93.8 us
    ppermute x51, starting transfers between devices, swap(): return lax.ppermute(x, axis, [(i, i ^ bit) for i in range(n)])  54.2 us
    pallas_call x16, Pallas kernels, call(): pl.pallas_call(body, out_shape=[jax.ShapeDtypeStruct(s, d) for s, d in ou...  22.9 us
    unnamed x148, local copies, waits for them, and re-layouts  15.5 us
  transfers between devices with their start and end apart: 51, of which 23 were waited for; matrix products, arithmetic and copies ran while one was open for 6% of the time, Pallas kernels for 9%

profile of v4, /device:TPU:0, one launch (start us, length us, event | category | flops | bytes accessed | tf_op | source)
XLA Modules:
  0.0 199.9 jit_solution(17524474949806877769)
XLA Ops:
  0.7 3.1 %collective-permute-start = (bf16[128,640]{1,0:T(8,128)(2,1)}, bf16[128,640]{1,0:T(8,128)(2,1)S(1)}, u32[]{:S(2)}, u32[]{:S(2)}) collective-permute-start(bf16[128,640]{1,0:T(8,128)(2,1)} %refs_1_.3), channel_id=1, source_target_pairs={{0,8},{4,12},{8,0},{12,4},{16,24},{20,28},{24,16},{28,20},{1,9},{5... | collective-permute-start | bytes 491528 | tf_op jit(solution)/shard_map/ppermute | solution.py:491
  3.8 2.6 %collective-permute-start.2 = (bf16[128,640]{1,0:T(8,128)(2,1)}, bf16[128,640]{1,0:T(8,128)(2,1)S(1)}, u32[]{:S(2)}, u32[]{:S(2)}) collective-permute-start(bf16[128,640]{1,0:T(8,128)(2,1)} %refs_1_.3), channel_id=1, source_target_pairs={{0,16},{4,20},{8,24},{12,28},{16,0},{20,4},{24,8},{28,12},{1,17},{... | collective-permute-start | bytes 491528 | tf_op jit(solution)/shard_map/ppermute | solution.py:491
  9.5 1.8 collective-permute-start.7
  12.6 1.8 collective-permute-start.1
  14.4 1.9 multiply_sine_fusion
  16.3 4.7 %collective-permute-done.1 = bf16[256,640]{1,0:T(8,128)(2,1)S(1)} collective-permute-done((bf16[256,640]{1,0:T(8,128)(2,1)S(1)}, bf16[256,640]{1,0:T(8,128)(2,1)S(1)}, u32[]{:S(2)}, u32[]{:S(2)}) %collective-permute-start.1) | collective-permute-done | bytes 327712 | tf_op jit(solution)/shard_map/ppermute | solution.py:491
  24.5 1.5 collective-permute-start.9
  28.4 5.7 %collective-permute-done.9.refs_5_.refs_18_ = bf16[256,640]{1,0:T(8,128)(2,1)S(1)} collective-permute-done((bf16[256,640]{1,0:T(8,128)(2,1)S(1)}, bf16[256,640]{1,0:T(8,128)(2,1)S(1)}, u32[]{:S(2)}, u32[]{:S(2)}) %collective-permute-start.9) | collective-permute-done | bytes 327712 | tf_op jit(solution)/shard_map/ppermute | solution.py:491
  34.3 2.1 %collective-permute-done.4 = bf16[256,640]{1,0:T(8,128)(2,1)S(1)} collective-permute-done((bf16[256,640]{1,0:T(8,128)(2,1)}, bf16[256,640]{1,0:T(8,128)(2,1)S(1)}, u32[]{:S(2)}, u32[]{:S(2)}) %collective-permute-start.4) | collective-permute-done | bytes 327712 | tf_op jit(solution)/shard_map/ppermute | solution.py:491
  38.6 3.1 %shard_map.204 = (bf16[1024,640]{1,0:T(8,128)(2,1)S(1)}, f32[1024,256]{1,0:T(8,128)S(1)}, bf16[1024,512]{1,0:T(8,128)(2,1)S(1)}, f32[4,128,256]{2,1,0:T(8,128)S(...) custom-call(s32[1]{0:T(128)} %bitcast.refs_0_, ...), custom_call_target="tpu_custom_call" | custom-call | flops 6600000000 | bytes 4395524 | tf_op jit(solution)/shard_map/pallas_call | solution.py:66
  48.5 4.4 %collective-permute-done.11.refs_1_ = bf16[128,640]{1,0:T(8,128)(2,1)S(1)} collective-permute-done((bf16[128,640]{1,0:T(8,128)(2,1)S(1)}, bf16[128,640]{1,0:T(8,128)(2,1)S(1)}, u32[]{:S(2)}, u32[]{:S(2)}) %collective-permute-start.11) | collective-permute-done | bytes 163872 | tf_op jit(solution)/shard_map/ppermute | solution.py:491
  52.9 1.9 shard_map.206
  56.1 1.5 collective-permute-start.15
  57.8 4.1 %collective-permute-done.17.refs_6_.refs_3_ = bf16[128,416]{1,0:T(8,128)(2,1)S(1)} collective-permute-done((bf16[128,416]{1,0:T(8,128)(2,1)S(1)}, bf16[128,416]{1,0:T(8,128)(2,1)S(1)}, u32[]{:S(2)}, u32[]{:S(2)}) %collective-permute-start.17) | collective-permute-done | bytes 106528 | tf_op jit(solution)/shard_map/ppermute | solution.py:491
  61.9 3.1 %collective-permute-done.15.refs_1_ = bf16[128,640]{1,0:T(8,128)(2,1)S(1)} collective-permute-done((bf16[128,640]{1,0:T(8,128)(2,1)S(1)}, bf16[128,640]{1,0:T(8,128)(2,1)S(1)}, u32[]{:S(2)}, u32[]{:S(2)}) %collective-permute-start.15) | collective-permute-done | bytes 163872 | tf_op jit(solution)/shard_map/ppermute | solution.py:491
  66.5 5.3 %collective-permute-done.19.refs_1_ = bf16[128,640]{1,0:T(8,128)(2,1)S(1)} collective-permute-done((bf16[128,640]{1,0:T(8,128)(2,1)S(1)}, bf16[128,640]{1,0:T(8,128)(2,1)S(1)}, u32[]{:S(2)}, u32[]{:S(2)}) %collective-permute-start.19) | collective-permute-done | bytes 163872 | tf_op jit(solution)/shard_map/ppermute | solution.py:491
  71.8 2.1 %shard_map.208 = (f32[128,640]{1,0:T(8,128)S(1)}, bf16[128,640]{1,0:T(8,128)(2,1)S(1)}, bf16[256,1664]{1,0:T(8,128)(2,1)}, bf16[256,1024]{1,0:T(8,128)(2,1)S(1)}) custom-call(bf16[128,640]{1,0:T(8,128)(2,1)S(1)} %get-tuple-element.107.refs_0_, bf16[128,640]{1,0:T(8,128)(2,1)S(1)} %collective-permute-done.19.refs_1_, ...), custom_call_target="tpu_custom_call" | custom-call | flops 3960000000 | bytes 6356992 | tf_op jit(solution)/shard_map/pallas_call | solution.py:66
  76.6 2.2 %collective-permute-done.22.refs_5_ = bf16[256,1664]{1,0:T(8,128)(2,1)} collective-permute-done((bf16[256,1664]{1,0:T(8,128)(2,1)}, bf16[256,1664]{1,0:T(8,128)(2,1)}, u32[]{:S(2)}, u32[]{:S(2)}) %collective-permute-start.22) | collective-permute-done | bytes 852000 | tf_op jit(solution)/shard_map/ppermute | solution.py:491
  82.9 2.9 %shard_map.209 = (bf16[1280,512]{1,0:T(8,128)(2,1)S(1)}, bf16[640,512]{1,0:T(8,128)(2,1)S(1)}) custom-call(bf16[256,1152]{1,0:T(8,128)(2,1)S(1)} %copy-done.27, bf16[256,512]{1,0:T(8,128)(2,1)S(1)} %copy-done.53, bf16[256,1152]{1,0:T(8,128)(2,1)S(1)} %copy-done.29, bf16[256,1664]{1,0:T(8,128)(2,1)} %get-tuple-element.115.refs_3_, ...), custom_call_target="tpu_custom_call" | custom-call | flops 2750000128 | bytes 3670016 | tf_op jit(solution)/shard_map/pallas_call | solution.py:66
  88.9 5.0 %collective-permute-done.23.refs_20_.refs_7_ = bf16[128,640]{1,0:T(8,128)(2,1)S(1)} collective-permute-done((bf16[128,640]{1,0:T(8,128)(2,1)S(1)}, bf16[128,640]{1,0:T(8,128)(2,1)S(1)}, u32[]{:S(2)}, u32[]{:S(2)}) %collective-permute-start.23) | collective-permute-done | bytes 163872 | tf_op jit(solution)/shard_map/ppermute | solution.py:491
  94.0 4.3 %shard_map.211 = (bf16[592,512]{1,0:T(8,128)(2,1)S(1)}, f32[160,512]{1,0:T(8,128)S(1)}, f32[160,512]{1,0:T(8,128)S(1)}, bf16[512,512]{1,0:T(8,128)(2,1)S(1)}, bf16[512,512]{1,0:T(8,128)(2,1)S(1)}) custom-call(s32[1]{0:T(128)} %bitcast.refs_0_, bf16[128,640]{1,0:T(8,128)(2,1)S(1)} %get-tuple-element.118.refs_1_.refs_5_, ...), custom_call_target="tpu_custom_call" | custom-call | flops 9900000256 | bytes 7258116 | tf_op jit(solution)/shard_map/pallas_call | solution.py:66
  98.9 1.6 collective-permute-start.24
  100.5 4.2 %collective-permute-done.26 = bf16[640,512]{1,0:T(8,128)(2,1)S(1)} collective-permute-done((bf16[640,512]{1,0:T(8,128)(2,1)S(1)}, bf16[640,512]{1,0:T(8,128)(2,1)S(1)}, u32[]{:S(2)}, u32[]{:S(2)}) %collective-permute-start.26) | collective-permute-done | bytes 655392 | tf_op jit(solution)/shard_map/ppermute | solution.py:491
  105.1 1.6 collective-permute-start.30
  107.1 6.1 %collective-permute-done.28.refs_1_ = bf16[592,512]{1,0:T(8,128)(2,1)S(1)} collective-permute-done((bf16[592,512]{1,0:T(8,128)(2,1)S(1)}, bf16[592,512]{1,0:T(8,128)(2,1)S(1)}, u32[]{:S(2)}, u32[]{:S(2)}) %collective-permute-start.28) | collective-permute-done | bytes 606240 | tf_op jit(solution)/shard_map/ppermute | solution.py:491
  113.5 1.5 collective-permute-start.27
  115.0 5.7 %collective-permute-done.30 = bf16[320,512]{1,0:T(8,128)(2,1)S(1)} collective-permute-done((bf16[320,512]{1,0:T(8,128)(2,1)S(1)}, bf16[320,512]{1,0:T(8,128)(2,1)S(1)}, u32[]{:S(2)}, u32[]{:S(2)}) %collective-permute-start.30) | collective-permute-done | bytes 327712 | tf_op jit(solution)/shard_map/ppermute | solution.py:491
  120.9 1.7 collective-permute-start.36
  123.1 1.5 collective-permute-start.35
  124.6 6.7 %collective-permute-done.27 = bf16[480,512]{1,0:T(8,128)(2,1)S(1)} collective-permute-done((bf16[480,512]{1,0:T(8,128)(2,1)S(1)}, bf16[480,512]{1,0:T(8,128)(2,1)S(1)}, u32[]{:S(2)}, u32[]{:S(2)}) %collective-permute-start.27) | collective-permute-done | bytes 491552 | tf_op jit(solution)/shard_map/ppermute | solution.py:491
  132.5 3.5 %collective-permute-start.40 = (bf16[160,512]{1,0:T(8,128)(2,1)S(1)}, bf16[160,512]{1,0:T(8,128)(2,1)S(1)}, u32[]{:S(2)}, u32[]{:S(2)}) collective-permute-start(bf16[160,512]{1,0:T(8,128)(2,1)S(1)} %add_convert_fusion.4), channel_id=1, source_target_pairs={{0,16},{4,20},{8,24},{12,28},{16,0},{20,4},{24,8},{28,12},{1,17},{... | collective-permute-start | bytes 491528 | tf_op jit(solution)/shard_map/ppermute | solution.py:491
  137.6 2.9 %collective-permute-start.33 = (bf16[128,512]{1,0:T(8,128)(2,1)S(1)}, bf16[128,512]{1,0:T(8,128)(2,1)S(1)}, u32[]{:S(2)}, u32[]{:S(2)}) collective-permute-start(bf16[128,512]{1,0:T(8,128)(2,1)S(1)} %get-tuple-element.185), channel_id=1, source_target_pairs={{0,8},{4,12},{8,0},{12,4},{16,24},{20,28},{24,16},{28,20},{1,9},{5... | collective-permute-start | bytes 393224 | tf_op jit(solution)/shard_map/ppermute | solution.py:491
  140.6 3.6 %collective-permute-done.34 = bf16[240,512]{1,0:T(8,128)(2,1)S(1)} collective-permute-done((bf16[240,512]{1,0:T(8,128)(2,1)S(1)}, bf16[240,512]{1,0:T(8,128)(2,1)S(1)}, u32[]{:S(2)}, u32[]{:S(2)}) %collective-permute-start.34) | collective-permute-done | bytes 245792 | tf_op jit(solution)/shard_map/ppermute | solution.py:491
  144.3 5.1 %collective-permute-done.40 = bf16[160,512]{1,0:T(8,128)(2,1)S(1)} collective-permute-done((bf16[160,512]{1,0:T(8,128)(2,1)S(1)}, bf16[160,512]{1,0:T(8,128)(2,1)S(1)}, u32[]{:S(2)}, u32[]{:S(2)}) %collective-permute-start.40) | collective-permute-done | bytes 163872 | tf_op jit(solution)/shard_map/ppermute | solution.py:491
  149.4 4.1 %collective-permute-start.37 = (bf16[64,512]{1,0:T(8,128)(2,1)S(1)}, bf16[64,512]{1,0:T(8,128)(2,1)S(1)}, u32[]{:S(2)}, u32[]{:S(2)}) collective-permute-start(bf16[64,512]{1,0:T(8,128)(2,1)S(1)} %get-tuple-element.198), channel_id=1, source_target_pairs={{0,24},{4,28},{8,16},{12,20},{16,8},{20,12},{24,0},{28,4},{1,25},{... | collective-permute-start | bytes 196616 | tf_op jit(solution)/shard_map/ppermute | solution.py:491
  153.5 1.5 collective-permute-start.39
  155.1 4.9 %collective-permute-done.32 = bf16[128,512]{1,0:T(8,128)(2,1)S(1)} collective-permute-done((bf16[128,512]{1,0:T(8,128)(2,1)S(1)}, bf16[128,512]{1,0:T(8,128)(2,1)S(1)}, u32[]{:S(2)}, u32[]{:S(2)}) %collective-permute-start.32) | collective-permute-done | bytes 131104 | tf_op jit(solution)/shard_map/ppermute | solution.py:491
  160.0 1.5 collective-permute-start.44
  162.4 1.9 collective-permute-start.41
  166.9 5.0 %collective-permute-done.45 = bf16[120,512]{1,0:T(8,128)(2,1)S(1)} collective-permute-done((bf16[120,512]{1,0:T(8,128)(2,1)S(1)}, bf16[120,512]{1,0:T(8,128)(2,1)S(1)}, u32[]{:S(2)}, u32[]{:S(2)}) %collective-permute-start.45) | collective-permute-done | bytes 122912 | tf_op jit(solution)/shard_map/ppermute | solution.py:491
  173.4 4.6 %collective-permute-done.47 = bf16[120,512]{1,0:T(8,128)(2,1)S(1)} collective-permute-done((bf16[120,512]{1,0:T(8,128)(2,1)S(1)}, bf16[120,512]{1,0:T(8,128)(2,1)S(1)}, u32[]{:S(2)}, u32[]{:S(2)}) %collective-permute-start.47) | collective-permute-done | bytes 122912 | tf_op jit(solution)/shard_map/ppermute | solution.py:491
  178.2 1.7 shard_map.215
  179.9 1.5 collective-permute-start.46
  181.4 2.0 %collective-permute-start.50 = (bf16[640,512]{1,0:T(8,128)(2,1)S(1)}, bf16[640,512]{1,0:T(8,128)(2,1)S(1)}, u32[]{:S(2)}, u32[]{:S(2)}) collective-permute-start(bf16[640,512]{1,0:T(8,128)(2,1)S(1)} %pad_maximum_fusion.2.refs_1_), channel_id=1, source_target_pairs={{0,8},{4,12},{8,0},{12,4},{16,24},{20,28},{24,16},{28,20},{1,9},{5... | collective-permute-start | bytes 1966088 | tf_op jit(solution)/shard_map/ppermute | solution.py:491
  183.4 3.6 %collective-permute-done.48 = bf16[240,512]{1,0:T(8,128)(2,1)S(1)} collective-permute-done((bf16[240,512]{1,0:T(8,128)(2,1)S(1)}, bf16[240,512]{1,0:T(8,128)(2,1)S(1)}, u32[]{:S(2)}, u32[]{:S(2)}) %collective-permute-start.48) | collective-permute-done | bytes 245792 | tf_op jit(solution)/shard_map/ppermute | solution.py:491
  187.1 1.6 collective-permute-start.49
  191.6 5.2 %collective-permute-done.50.refs_2_ = bf16[640,512]{1,0:T(8,128)(2,1)S(1)} collective-permute-done((bf16[640,512]{1,0:T(8,128)(2,1)S(1)}, bf16[640,512]{1,0:T(8,128)(2,1)S(1)}, u32[]{:S(2)}, u32[]{:S(2)}) %collective-permute-start.50) | collective-permute-done | bytes 655392 | tf_op jit(solution)/shard_map/ppermute | solution.py:491
  196.8 1.7 shard_map.218
  (291 shorter events, 46.4 us)
Async XLA Ops:
  0.7 11.9 %collective-permute-start = (bf16[128,640]{1,0:T(8,128)(2,1)}, bf16[128,640]{1,0:T(8,128)(2,1)S(1)}, u32[]{:S(2)}, u32[]{:S(2)}) collective-permute-start(bf16[128,640]{1,0:T(8,128)(2,1)} %refs_1_.3), channel_id=1, source_target_pairs={{0,8},{4,12},{8,0},{12,4},{16,24},{20,28},{24,16},{28,20},{1,9},{5... | collective-permute-start | bytes 491528 | tf_op jit(solution)/shard_map/ppermute | solution.py:491
  3.8 17.4 %collective-permute-start.2 = (bf16[128,640]{1,0:T(8,128)(2,1)}, bf16[128,640]{1,0:T(8,128)(2,1)S(1)}, u32[]{:S(2)}, u32[]{:S(2)}) collective-permute-start(bf16[128,640]{1,0:T(8,128)(2,1)} %refs_1_.3), channel_id=1, source_target_pairs={{0,16},{4,20},{8,24},{12,28},{16,0},{20,4},{24,8},{28,12},{1,17},{... | collective-permute-start | bytes 491528 | tf_op jit(solution)/shard_map/ppermute | solution.py:491
  6.3 14.9 %collective-permute-start.3 = (bf16[128,640]{1,0:T(8,128)(2,1)}, bf16[128,640]{1,0:T(8,128)(2,1)S(1)}, u32[]{:S(2)}, u32[]{:S(2)}) collective-permute-start(bf16[128,640]{1,0:T(8,128)(2,1)} %refs_1_.3), channel_id=1, source_target_pairs={{0,24},{4,28},{8,16},{12,20},{16,8},{20,12},{24,0},{28,4},{1,25},{... | collective-permute-start | bytes 491528 | tf_op jit(solution)/shard_map/ppermute | solution.py:491
  9.5 11.8 %collective-permute-start.7 = (bf16[176,512]{1,0:T(8,128)(2,1)S(1)}, bf16[176,512]{1,0:T(8,128)(2,1)S(1)}, u32[]{:S(2)}, u32[]{:S(2)}) collective-permute-start(bf16[176,512]{1,0:T(8,128)(2,1)S(1)} %shard_map.203.refs_10_), channel_id=1, source_target_pairs={{0,2},{1,3},{2,0},{3,1},{4,6},{5,7},{6,4},{7,5},{8,10},{9,11},{10,... | collective-permute-start | bytes 540680 | tf_op jit(solution)/shard_map/ppermute | solution.py:491
  11.3 11.1 %collective-permute-start.5 = (bf16[160,1024]{1,0:T(8,128)(2,1)S(1)}, bf16[160,1024]{1,0:T(8,128)(2,1)S(1)}, u32[]{:S(2)}, u32[]{:S(2)}) collective-permute-start(bf16[160,1024]{1,0:T(8,128)(2,1)S(1)} %copy-done.2), channel_id=1, source_target_pairs={{0,2},{1,3},{2,0},{3,1},{4,6},{5,7},{6,4},{7,5},{8,10},{9,11},{10,... | collective-permute-start | bytes 983048 | tf_op jit(solution)/shard_map/ppermute | solution.py:491
  12.6 8.4 %collective-permute-start.1 = (bf16[256,640]{1,0:T(8,128)(2,1)S(1)}, bf16[256,640]{1,0:T(8,128)(2,1)S(1)}, u32[]{:S(2)}, u32[]{:S(2)}) collective-permute-start(bf16[256,640]{1,0:T(8,128)(2,1)S(1)} %pad_maximum_fusion.5), channel_id=1, source_target_pairs={{0,4},{4,0},{8,12},{12,8},{16,20},{20,16},{24,28},{28,24},{1,5},{5... | collective-permute-start | bytes 983048 | tf_op jit(solution)/shard_map/ppermute | solution.py:491
  23.2 10.9 %collective-permute-start.6 = (bf16[320,1024]{1,0:T(8,128)(2,1)}, bf16[320,1024]{1,0:T(8,128)(2,1)}, u32[]{:S(2)}, u32[]{:S(2)}) collective-permute-start(bf16[320,1024]{1,0:T(8,128)(2,1)} %pad_maximum_fusion), channel_id=1, source_target_pairs={{0,1},{1,0},{2,3},{3,2},{4,5},{5,4},{6,7},{7,6},{8,9},{9,8},{10,11... | collective-permute-start | bytes 1966088 | tf_op jit(solution)/shard_map/ppermute | solution.py:491
  24.0 4.4 %collective-permute-start.8 = (bf16[352,512]{1,0:T(8,128)(2,1)}, bf16[352,512]{1,0:T(8,128)(2,1)S(1)}, u32[]{:S(2)}, u32[]{:S(2)}) collective-permute-start(bf16[352,512]{1,0:T(8,128)(2,1)} %pad_maximum_fusion.4), channel_id=1, source_target_pairs={{0,1},{1,0},{2,3},{3,2},{4,5},{5,4},{6,7},{7,6},{8,9},{9,8},{10,11... | collective-permute-start | bytes 1081352 | tf_op jit(solution)/shard_map/ppermute | solution.py:491
  24.5 9.6 %collective-permute-start.9 = (bf16[256,640]{1,0:T(8,128)(2,1)S(1)}, bf16[256,640]{1,0:T(8,128)(2,1)S(1)}, u32[]{:S(2)}, u32[]{:S(2)}) collective-permute-start(bf16[256,640]{1,0:T(8,128)(2,1)S(1)} %copy-done.1), channel_id=1, source_target_pairs={{0,2},{1,3},{2,0},{3,1},{4,6},{5,7},{6,4},{7,5},{8,10},{9,11},{10,... | collective-permute-start | bytes 983048 | tf_op jit(solution)/shard_map/ppermute | solution.py:491
  26.9 9.5 %collective-permute-start.4 = (bf16[256,640]{1,0:T(8,128)(2,1)}, bf16[256,640]{1,0:T(8,128)(2,1)S(1)}, u32[]{:S(2)}, u32[]{:S(2)}) collective-permute-start(bf16[256,640]{1,0:T(8,128)(2,1)} %copy-done.68), channel_id=1, source_target_pairs={{0,4},{4,0},{8,12},{12,8},{16,20},{20,16},{24,28},{28,24},{1,5},{5... | collective-permute-start | bytes 983048 | tf_op jit(solution)/shard_map/ppermute | solution.py:491
  37.9 15.0 %collective-permute-start.12 = (bf16[640,512]{1,0:T(8,128)(2,1)S(1)}, bf16[640,512]{1,0:T(8,128)(2,1)S(1)}, u32[]{:S(2)}, u32[]{:S(2)}) collective-permute-start(bf16[640,512]{1,0:T(8,128)(2,1)S(1)} %copy-done.23), channel_id=1, source_target_pairs={{0,1},{1,0},{2,3},{3,2},{4,5},{5,4},{6,7},{7,6},{8,9},{9,8},{10,11... | collective-permute-start | bytes 1966088 | tf_op jit(solution)/shard_map/ppermute | solution.py:491
  38.0 14.9 %collective-permute-start.13 = (bf16[640,512]{1,0:T(8,128)(2,1)S(1)}, bf16[640,512]{1,0:T(8,128)(2,1)S(1)}, u32[]{:S(2)}, u32[]{:S(2)}) collective-permute-start(bf16[640,512]{1,0:T(8,128)(2,1)S(1)} %copy-done.24), channel_id=1, source_target_pairs={{0,1},{1,0},{2,3},{3,2},{4,5},{5,4},{6,7},{7,6},{8,9},{9,8},{10,11... | collective-permute-start | bytes 1966088 | tf_op jit(solution)/shard_map/ppermute | solution.py:491
  38.5 14.4 %collective-permute-start.14 = (bf16[512,640]{1,0:T(8,128)(2,1)S(1)}, bf16[512,640]{1,0:T(8,128)(2,1)S(1)}, u32[]{:S(2)}, u32[]{:S(2)}) collective-permute-start(bf16[512,640]{1,0:T(8,128)(2,1)S(1)} %copy-done.25), channel_id=1, source_target_pairs={{0,1},{1,0},{2,3},{3,2},{4,5},{5,4},{6,7},{7,6},{8,9},{9,8},{10,11... | collective-permute-start | bytes 1966088 | tf_op jit(solution)/shard_map/ppermute | solution.py:491
  45.9 7.0 %collective-permute-start.11 = (bf16[128,640]{1,0:T(8,128)(2,1)S(1)}, bf16[128,640]{1,0:T(8,128)(2,1)S(1)}, u32[]{:S(2)}, u32[]{:S(2)}) collective-permute-start(bf16[128,640]{1,0:T(8,128)(2,1)S(1)} %get-tuple-element.98.refs_0_), channel_id=1, source_target_pairs={{0,2},{1,3},{2,0},{3,1},{4,6},{5,7},{6,4},{7,5},{8,10},{9,11},{10,... | collective-permute-start | bytes 491528 | tf_op jit(solution)/shard_map/ppermute | solution.py:491
  47.2 10.5 %collective-permute-start.18 = (bf16[128,416]{1,0:T(8,128)(2,1)S(1)}, bf16[128,416]{1,0:T(8,128)(2,1)S(1)}, u32[]{:S(2)}, u32[]{:S(2)}) collective-permute-start(bf16[128,416]{1,0:T(8,128)(2,1)S(1)} %pad_maximum_fusion.10), channel_id=1, source_target_pairs={{0,3},{1,2},{2,1},{3,0},{4,7},{5,6},{6,5},{7,4},{8,11},{9,10},{10,... | collective-permute-start | bytes 319496 | tf_op jit(solution)/shard_map/ppermute | solution.py:491
  55.5 16.3 %collective-permute-start.20 = (bf16[256,1152]{1,0:T(8,128)(2,1)S(1)}, bf16[256,1152]{1,0:T(8,128)(2,1)S(1)}, u32[]{:S(2)}, u32[]{:S(2)}) collective-permute-start(bf16[256,1152]{1,0:T(8,128)(2,1)S(1)} %get-tuple-element.110.refs_0_), channel_id=1, source_target_pairs={{0,1},{1,0},{2,3},{3,2},{4,5},{5,4},{6,7},{7,6},{8,9},{9,8},{10,11... | collective-permute-start | bytes 1769480 | tf_op jit(solution)/shard_map/ppermute | solution.py:491
  55.5 6.4 %collective-permute-start.17 = (bf16[128,416]{1,0:T(8,128)(2,1)S(1)}, bf16[128,416]{1,0:T(8,128)(2,1)S(1)}, u32[]{:S(2)}, u32[]{:S(2)}) collective-permute-start(bf16[128,416]{1,0:T(8,128)(2,1)S(1)} %pad_maximum_fusion.9), channel_id=1, source_target_pairs={{0,2},{1,3},{2,0},{3,1},{4,6},{5,7},{6,4},{7,5},{8,10},{9,11},{10,... | collective-permute-start | bytes 319496 | tf_op jit(solution)/shard_map/ppermute | solution.py:491
  56.1 8.9 %collective-permute-start.15 = (bf16[128,640]{1,0:T(8,128)(2,1)S(1)}, bf16[128,640]{1,0:T(8,128)(2,1)S(1)}, u32[]{:S(2)}, u32[]{:S(2)}) collective-permute-start(bf16[128,640]{1,0:T(8,128)(2,1)S(1)} %get-tuple-element.103), channel_id=1, source_target_pairs={{0,2},{1,3},{2,0},{3,1},{4,6},{5,7},{6,4},{7,5},{8,10},{9,11},{10,... | collective-permute-start | bytes 491528 | tf_op jit(solution)/shard_map/ppermute | solution.py:491
  65.9 5.9 %collective-permute-start.19 = (bf16[128,640]{1,0:T(8,128)(2,1)S(1)}, bf16[128,640]{1,0:T(8,128)(2,1)S(1)}, u32[]{:S(2)}, u32[]{:S(2)}) collective-permute-start(bf16[128,640]{1,0:T(8,128)(2,1)S(1)} %get-tuple-element.107.refs_0_), channel_id=1, source_target_pairs={{0,2},{1,3},{2,0},{3,1},{4,6},{5,7},{6,4},{7,5},{8,10},{9,11},{10,... | collective-permute-start | bytes 491528 | tf_op jit(solution)/shard_map/ppermute | solution.py:491
  76.1 9.9 %collective-permute-start.21 = (bf16[128,640]{1,0:T(8,128)(2,1)}, bf16[128,640]{1,0:T(8,128)(2,1)S(1)}, u32[]{:S(2)}, u32[]{:S(2)}) collective-permute-start(bf16[128,640]{1,0:T(8,128)(2,1)} %copy-done.32), channel_id=1, source_target_pairs={{0,2},{1,3},{2,0},{3,1},{4,6},{5,7},{6,4},{7,5},{8,10},{9,11},{10,... | collective-permute-start | bytes 491528 | tf_op jit(solution)/shard_map/ppermute | solution.py:491
  87.6 6.3 %collective-permute-start.23 = (bf16[128,640]{1,0:T(8,128)(2,1)S(1)}, bf16[128,640]{1,0:T(8,128)(2,1)S(1)}, u32[]{:S(2)}, u32[]{:S(2)}) collective-permute-start(bf16[128,640]{1,0:T(8,128)(2,1)S(1)} %get-tuple-element.118.refs_1_.refs_5_), channel_id=1, source_target_pairs={{0,2},{1,3},{2,0},{3,1},{4,6},{5,7},{6,4},{7,5},{8,10},{9,11},{10,... | collective-permute-start | bytes 491528 | tf_op jit(solution)/shard_map/ppermute | solution.py:491
  88.2 16.6 %collective-permute-start.26 = (bf16[640,512]{1,0:T(8,128)(2,1)S(1)}, bf16[640,512]{1,0:T(8,128)(2,1)S(1)}, u32[]{:S(2)}, u32[]{:S(2)}) collective-permute-start(bf16[640,512]{1,0:T(8,128)(2,1)S(1)} %broadcast_select_fusion.refs_6_), channel_id=1, source_target_pairs={{0,8},{4,12},{8,0},{12,4},{16,24},{20,28},{24,16},{28,20},{1,9},{5... | collective-permute-start | bytes 1966088 | tf_op jit(solution)/shard_map/ppermute | solution.py:491
  98.3 15.0 %collective-permute-start.28 = (bf16[592,512]{1,0:T(8,128)(2,1)S(1)}, bf16[592,512]{1,0:T(8,128)(2,1)S(1)}, u32[]{:S(2)}, u32[]{:S(2)}) collective-permute-start(bf16[592,512]{1,0:T(8,128)(2,1)S(1)} %get-tuple-element.131.refs_0_.refs_3_), channel_id=1, source_target_pairs={{0,2},{1,3},{2,0},{3,1},{4,6},{5,7},{6,4},{7,5},{8,10},{9,11},{10,... | collective-permute-start | bytes 1818632 | tf_op jit(solution)/shard_map/ppermute | solution.py:491
  98.9 7.8 %collective-permute-start.25 = (bf16[256,640]{1,0:T(8,128)(2,1)S(1)}, bf16[256,640]{1,0:T(8,128)(2,1)S(1)}, u32[]{:S(2)}, u32[]{:S(2)}) collective-permute-start(bf16[256,640]{1,0:T(8,128)(2,1)S(1)} %constant_dynamic-update-slice_fusion.6), channel_id=1, source_target_pairs={{0,1},{1,0},{2,3},{3,2},{4,5},{5,4},{6,7},{7,6},{8,9},{9,8},{10,11... | collective-permute-start | bytes 983048 | tf_op jit(solution)/shard_map/ppermute | solution.py:491
  98.9 33.3 %collective-permute-start.24 = (bf16[512,512]{1,0:T(8,128)(2,1)S(1)}, bf16[512,512]{1,0:T(8,128)(2,1)S(1)}, u32[]{:S(2)}, u32[]{:S(2)}) collective-permute-start(bf16[512,512]{1,0:T(8,128)(2,1)S(1)} %get-tuple-element.129), channel_id=1, source_target_pairs={{0,4},{4,0},{8,12},{12,8},{16,20},{20,16},{24,28},{28,24},{1,5},{5... | collective-permute-start | bytes 1572872 | tf_op jit(solution)/shard_map/ppermute | solution.py:491
  105.1 15.7 %collective-permute-start.30 = (bf16[320,512]{1,0:T(8,128)(2,1)S(1)}, bf16[320,512]{1,0:T(8,128)(2,1)S(1)}, u32[]{:S(2)}, u32[]{:S(2)}) collective-permute-start(bf16[320,512]{1,0:T(8,128)(2,1)S(1)} %broadcast_select_fusion.4), channel_id=1, source_target_pairs={{0,4},{4,0},{8,12},{12,8},{16,20},{20,16},{24,28},{28,24},{1,5},{5... | collective-permute-start | bytes 983048 | tf_op jit(solution)/shard_map/ppermute | solution.py:491
  113.3 9.3 %collective-permute-start.29 = (bf16[704,512]{1,0:T(8,128)(2,1)S(1)}, bf16[704,512]{1,0:T(8,128)(2,1)S(1)}, u32[]{:S(2)}, u32[]{:S(2)}) collective-permute-start(bf16[704,512]{1,0:T(8,128)(2,1)S(1)} %get-tuple-element.138), channel_id=1, source_target_pairs={{0,1},{1,0},{2,3},{3,2},{4,5},{5,4},{6,7},{7,6},{8,9},{9,8},{10,11... | collective-permute-start | bytes 2162696 | tf_op jit(solution)/shard_map/ppermute | solution.py:491
  113.5 17.8 %collective-permute-start.27 = (bf16[480,512]{1,0:T(8,128)(2,1)S(1)}, bf16[480,512]{1,0:T(8,128)(2,1)S(1)}, u32[]{:S(2)}, u32[]{:S(2)}) collective-permute-start(bf16[480,512]{1,0:T(8,128)(2,1)S(1)} %broadcast_select_fusion.1), channel_id=1, source_target_pairs={{0,4},{4,0},{8,12},{12,8},{16,20},{20,16},{24,28},{28,24},{1,5},{5... | collective-permute-start | bytes 1474568 | tf_op jit(solution)/shard_map/ppermute | solution.py:491
  120.9 11.5 %collective-permute-start.36 = (bf16[160,512]{1,0:T(8,128)(2,1)S(1)}, bf16[160,512]{1,0:T(8,128)(2,1)S(1)}, u32[]{:S(2)}, u32[]{:S(2)}) collective-permute-start(bf16[160,512]{1,0:T(8,128)(2,1)S(1)} %broadcast_select_fusion.11), channel_id=1, source_target_pairs={{0,16},{4,20},{8,24},{12,28},{16,0},{20,4},{24,8},{28,12},{1,17},{... | collective-permute-start | bytes 491528 | tf_op jit(solution)/shard_map/ppermute | solution.py:491
  123.1 14.6 %collective-permute-start.35 = (bf16[256,512]{1,0:T(8,128)(2,1)S(1)}, bf16[256,512]{1,0:T(8,128)(2,1)S(1)}, u32[]{:S(2)}, u32[]{:S(2)}) collective-permute-start(bf16[256,512]{1,0:T(8,128)(2,1)S(1)} %broadcast_select_fusion.5), channel_id=1, source_target_pairs={{0,4},{4,0},{8,12},{12,8},{16,20},{20,16},{24,28},{28,24},{1,5},{5... | collective-permute-start | bytes 786440 | tf_op jit(solution)/shard_map/ppermute | solution.py:491
  131.5 12.7 %collective-permute-start.34 = (bf16[240,512]{1,0:T(8,128)(2,1)S(1)}, bf16[240,512]{1,0:T(8,128)(2,1)S(1)}, u32[]{:S(2)}, u32[]{:S(2)}) collective-permute-start(bf16[240,512]{1,0:T(8,128)(2,1)S(1)} %broadcast_select_fusion.8), channel_id=1, source_target_pairs={{0,8},{4,12},{8,0},{12,4},{16,24},{20,28},{24,16},{28,20},{1,9},{5... | collective-permute-start | bytes 737288 | tf_op jit(solution)/shard_map/ppermute | solution.py:491
  132.5 16.9 %collective-permute-start.40 = (bf16[160,512]{1,0:T(8,128)(2,1)S(1)}, bf16[160,512]{1,0:T(8,128)(2,1)S(1)}, u32[]{:S(2)}, u32[]{:S(2)}) collective-permute-start(bf16[160,512]{1,0:T(8,128)(2,1)S(1)} %add_convert_fusion.4), channel_id=1, source_target_pairs={{0,16},{4,20},{8,24},{12,28},{16,0},{20,4},{24,8},{28,12},{1,17},{... | collective-permute-start | bytes 491528 | tf_op jit(solution)/shard_map/ppermute | solution.py:491
  136.1 17.4 %collective-permute-start.31 = (bf16[128,512]{1,0:T(8,128)(2,1)S(1)}, bf16[128,512]{1,0:T(8,128)(2,1)S(1)}, u32[]{:S(2)}, u32[]{:S(2)}) collective-permute-start(bf16[128,512]{1,0:T(8,128)(2,1)S(1)} %get-tuple-element.187), channel_id=1, source_target_pairs={{0,24},{4,28},{8,16},{12,20},{16,8},{20,12},{24,0},{28,4},{1,25},{... | collective-permute-start | bytes 393224 | tf_op jit(solution)/shard_map/ppermute | solution.py:491
  136.4 23.6 %collective-permute-start.32 = (bf16[128,512]{1,0:T(8,128)(2,1)S(1)}, bf16[128,512]{1,0:T(8,128)(2,1)S(1)}, u32[]{:S(2)}, u32[]{:S(2)}) collective-permute-start(bf16[128,512]{1,0:T(8,128)(2,1)S(1)} %get-tuple-element.186), channel_id=1, source_target_pairs={{0,16},{4,20},{8,24},{12,28},{16,0},{20,4},{24,8},{28,12},{1,17},{... | collective-permute-start | bytes 393224 | tf_op jit(solution)/shard_map/ppermute | solution.py:491
  137.6 22.4 %collective-permute-start.33 = (bf16[128,512]{1,0:T(8,128)(2,1)S(1)}, bf16[128,512]{1,0:T(8,128)(2,1)S(1)}, u32[]{:S(2)}, u32[]{:S(2)}) collective-permute-start(bf16[128,512]{1,0:T(8,128)(2,1)S(1)} %get-tuple-element.185), channel_id=1, source_target_pairs={{0,8},{4,12},{8,0},{12,4},{16,24},{20,28},{24,16},{28,20},{1,9},{5... | collective-permute-start | bytes 393224 | tf_op jit(solution)/shard_map/ppermute | solution.py:491
  149.4 12.1 %collective-permute-start.37 = (bf16[64,512]{1,0:T(8,128)(2,1)S(1)}, bf16[64,512]{1,0:T(8,128)(2,1)S(1)}, u32[]{:S(2)}, u32[]{:S(2)}) collective-permute-start(bf16[64,512]{1,0:T(8,128)(2,1)S(1)} %get-tuple-element.198), channel_id=1, source_target_pairs={{0,24},{4,28},{8,16},{12,20},{16,8},{20,12},{24,0},{28,4},{1,25},{... | collective-permute-start | bytes 196616 | tf_op jit(solution)/shard_map/ppermute | solution.py:491
  153.5 8.9 %collective-permute-start.38 = (bf16[64,512]{1,0:T(8,128)(2,1)S(1)}, bf16[64,512]{1,0:T(8,128)(2,1)S(1)}, u32[]{:S(2)}, u32[]{:S(2)}) collective-permute-start(bf16[64,512]{1,0:T(8,128)(2,1)S(1)} %get-tuple-element.197), channel_id=1, source_target_pairs={{0,16},{4,20},{8,24},{12,28},{16,0},{20,4},{24,8},{28,12},{1,17},{... | collective-permute-start | bytes 196616 | tf_op jit(solution)/shard_map/ppermute | solution.py:491
  153.5 8.9 %collective-permute-start.39 = (bf16[64,512]{1,0:T(8,128)(2,1)S(1)}, bf16[64,512]{1,0:T(8,128)(2,1)S(1)}, u32[]{:S(2)}, u32[]{:S(2)}) collective-permute-start(bf16[64,512]{1,0:T(8,128)(2,1)S(1)} %get-tuple-element.196), channel_id=1, source_target_pairs={{0,8},{4,12},{8,0},{12,4},{16,24},{20,28},{24,16},{28,20},{1,9},{5... | collective-permute-start | bytes 196616 | tf_op jit(solution)/shard_map/ppermute | solution.py:491
  160.0 11.9 %collective-permute-start.45 = (bf16[120,512]{1,0:T(8,128)(2,1)S(1)}, bf16[120,512]{1,0:T(8,128)(2,1)S(1)}, u32[]{:S(2)}, u32[]{:S(2)}) collective-permute-start(bf16[120,512]{1,0:T(8,128)(2,1)S(1)} %broadcast_select_fusion.14), channel_id=1, source_target_pairs={{0,16},{4,20},{8,24},{12,28},{16,0},{20,4},{24,8},{28,12},{1,17},{... | collective-permute-start | bytes 368648 | tf_op jit(solution)/shard_map/ppermute | solution.py:491
  160.0 12.0 %collective-permute-start.44 = (bf16[320,512]{1,0:T(8,128)(2,1)S(1)}, bf16[320,512]{1,0:T(8,128)(2,1)S(1)}, u32[]{:S(2)}, u32[]{:S(2)}) collective-permute-start(bf16[320,512]{1,0:T(8,128)(2,1)S(1)} %pad_maximum_fusion.6), channel_id=1, source_target_pairs={{0,4},{4,0},{8,12},{12,8},{16,20},{20,16},{24,28},{28,24},{1,5},{5... | collective-permute-start | bytes 983048 | tf_op jit(solution)/shard_map/ppermute | solution.py:491
  162.4 9.8 %collective-permute-start.41 = (bf16[64,512]{1,0:T(8,128)(2,1)S(1)}, bf16[64,512]{1,0:T(8,128)(2,1)S(1)}, u32[]{:S(2)}, u32[]{:S(2)}) collective-permute-start(bf16[64,512]{1,0:T(8,128)(2,1)S(1)} %add_convert_fusion.6), channel_id=1, source_target_pairs={{0,8},{4,12},{8,0},{12,4},{16,24},{20,28},{24,16},{28,20},{1,9},{5... | collective-permute-start | bytes 196616 | tf_op jit(solution)/shard_map/ppermute | solution.py:491
  164.3 9.0 %collective-permute-start.42 = (bf16[64,512]{1,0:T(8,128)(2,1)S(1)}, bf16[64,512]{1,0:T(8,128)(2,1)S(1)}, u32[]{:S(2)}, u32[]{:S(2)}) collective-permute-start(bf16[64,512]{1,0:T(8,128)(2,1)S(1)} %add_convert_fusion.6), channel_id=1, source_target_pairs={{0,16},{4,20},{8,24},{12,28},{16,0},{20,4},{24,8},{28,12},{1,17},{... | collective-permute-start | bytes 196616 | tf_op jit(solution)/shard_map/ppermute | solution.py:491
  165.4 7.9 %collective-permute-start.43 = (bf16[64,512]{1,0:T(8,128)(2,1)S(1)}, bf16[64,512]{1,0:T(8,128)(2,1)S(1)}, u32[]{:S(2)}, u32[]{:S(2)}) collective-permute-start(bf16[64,512]{1,0:T(8,128)(2,1)S(1)} %add_convert_fusion.6), channel_id=1, source_target_pairs={{0,24},{4,28},{8,16},{12,20},{16,8},{20,12},{24,0},{28,4},{1,25},{... | collective-permute-start | bytes 196616 | tf_op jit(solution)/shard_map/ppermute | solution.py:491
  171.9 6.0 %collective-permute-start.47 = (bf16[120,512]{1,0:T(8,128)(2,1)S(1)}, bf16[120,512]{1,0:T(8,128)(2,1)S(1)}, u32[]{:S(2)}, u32[]{:S(2)}) collective-permute-start(bf16[120,512]{1,0:T(8,128)(2,1)S(1)} %add_convert_fusion.5), channel_id=1, source_target_pairs={{0,16},{4,20},{8,24},{12,28},{16,0},{20,4},{24,8},{28,12},{1,17},{... | collective-permute-start | bytes 368648 | tf_op jit(solution)/shard_map/ppermute | solution.py:491
  178.0 9.0 %collective-permute-start.48 = (bf16[240,512]{1,0:T(8,128)(2,1)S(1)}, bf16[240,512]{1,0:T(8,128)(2,1)S(1)}, u32[]{:S(2)}, u32[]{:S(2)}) collective-permute-start(bf16[240,512]{1,0:T(8,128)(2,1)S(1)} %pad_maximum_fusion.7), channel_id=1, source_target_pairs={{0,8},{4,12},{8,0},{12,4},{16,24},{20,28},{24,16},{28,20},{1,9},{5... | collective-permute-start | bytes 737288 | tf_op jit(solution)/shard_map/ppermute | solution.py:491
  179.9 9.1 %collective-permute-start.46 = (bf16[256,512]{1,0:T(8,128)(2,1)S(1)}, bf16[256,512]{1,0:T(8,128)(2,1)S(1)}, u32[]{:S(2)}, u32[]{:S(2)}) collective-permute-start(bf16[256,512]{1,0:T(8,128)(2,1)S(1)} %constant_dynamic-update-slice_fusion.8.refs_1_), channel_id=1, source_target_pairs={{0,4},{4,0},{8,12},{12,8},{16,20},{20,16},{24,28},{28,24},{1,5},{5... | collective-permute-start | bytes 786440 | tf_op jit(solution)/shard_map/ppermute | solution.py:491
  181.4 15.4 %collective-permute-start.50 = (bf16[640,512]{1,0:T(8,128)(2,1)S(1)}, bf16[640,512]{1,0:T(8,128)(2,1)S(1)}, u32[]{:S(2)}, u32[]{:S(2)}) collective-permute-start(bf16[640,512]{1,0:T(8,128)(2,1)S(1)} %pad_maximum_fusion.2.refs_1_), channel_id=1, source_target_pairs={{0,8},{4,12},{8,0},{12,4},{16,24},{20,28},{24,16},{28,20},{1,9},{5... | collective-permute-start | bytes 1966088 | tf_op jit(solution)/shard_map/ppermute | solution.py:491
  187.1 11.4 %collective-permute-start.49 = (bf16[480,512]{1,0:T(8,128)(2,1)S(1)}, bf16[480,512]{1,0:T(8,128)(2,1)S(1)}, u32[]{:S(2)}, u32[]{:S(2)}) collective-permute-start(bf16[480,512]{1,0:T(8,128)(2,1)S(1)} %pad_maximum_fusion.3.refs_1_), channel_id=1, source_target_pairs={{0,4},{4,0},{8,12},{12,8},{16,20},{20,16},{24,28},{28,24},{1,5},{5... | collective-permute-start | bytes 1474568 | tf_op jit(solution)/shard_map/ppermute | solution.py:491
  (73 other events, 322.5 us)

commit v5 on v4

--- a/solution.py
+++ b/solution.py
@@ -223,8 +223,8 @@
         gate = dot(x, wg[...])
         up = dot(x, wu[...])
         value, slope = gelu_parts(gate)
-        a_o[i] = value
-        b_o[i] = up * slope
+        a_o[i] = value.astype(BF)
+        b_o[i] = (up * slope).astype(BF)
         hidden = (value * up).astype(BF)
         if i == 0:
             hid_o[...] = hidden
@@ -255,8 +255,8 @@
     total = None
     for i, (wg, wu, wd) in enumerate(((wg0, wu0, wd0), (wg1, wu1, wd1))):
         gh = dot_nt(c, wd[...])
-        gg = (gh * b[i]).astype(BF)
-        gu = (gh * a[i]).astype(BF)
+        gg = (gh * b[i].astype(F32)).astype(BF)
+        gu = (gh * a[i].astype(F32)).astype(BF)
         if i == 0:
             gg_o[:, :width] = gg
             gg_o[:, width:] = gu
@@ -695,7 +695,7 @@
         ff_kernel,
         [
             ((rows, d), F32), ((rows, d), BF), ((two, d + width), BF), ((two, width), BF),
-            ((2, two, width), F32), ((2, two, width), F32),
+            ((2, two, width), BF), ((2, two, width), BF),
         ],
         ff_in, swap(ff_in, "fsdp", nf, 2), *own_ff, *next_ff, us=3.6,
     )

time: 200 us -> 200 us (level)
  transfers between devices with their start and end apart: 51 -> 51, of which waited for: 23 -> 23; matrix products, arithmetic and copies ran while one was open for 6% -> 6% of each run, Pallas kernels for 9% -> 10%
where the time goes in v5:
time: 200 us
  waiting for transfers between devices  93.8 us (47%)
  starting transfers between devices  54.2 us (27%)
  Pallas kernels  23 us (12%)
  local copies, waits for them, and re-layouts  20.9 us (10%)
  other arithmetic  6.42 us (3%)
    ppermute x51, waiting for transfers between devices, swap(): return lax.ppermute(x, axis, [(i, i ^ bit) for i in range(n)])  93.8 us
    ppermute x51, starting transfers between devices, swap(): return lax.ppermute(x, axis, [(i, i ^ bit) for i in range(n)])  54.2 us
    pallas_call x16, Pallas kernels, call(): pl.pallas_call(body, out_shape=[jax.ShapeDtypeStruct(s, d) for s, d in ou...  23 us
    unnamed x148, local copies, waits for them, and re-layouts  15.5 us
  transfers between devices with their start and end apart: 51, of which 23 were waited for; matrix products, arithmetic and copies ran while one was open for 6% of the time, Pallas kernels for 10%

profile of v5, /device:TPU:0, one launch (start us, length us, event | category | flops | bytes accessed | tf_op | source)
XLA Modules:
  0.0 200.0 jit_solution(11182342920009932732)
XLA Ops:
  0.7 3.1 %collective-permute-start = (bf16[128,640]{1,0:T(8,128)(2,1)}, bf16[128,640]{1,0:T(8,128)(2,1)S(1)}, u32[]{:S(2)}, u32[]{:S(2)}) collective-permute-start(bf16[128,640]{1,0:T(8,128)(2,1)} %refs_1_.3), channel_id=1, source_target_pairs={{0,8},{4,12},{8,0},{12,4},{16,24},{20,28},{24,16},{28,20},{1,9},{5... | collective-permute-start | bytes 491528 | tf_op jit(solution)/shard_map/ppermute | solution.py:491
  3.8 2.6 %collective-permute-start.2 = (bf16[128,640]{1,0:T(8,128)(2,1)}, bf16[128,640]{1,0:T(8,128)(2,1)S(1)}, u32[]{:S(2)}, u32[]{:S(2)}) collective-permute-start(bf16[128,640]{1,0:T(8,128)(2,1)} %refs_1_.3), channel_id=1, source_target_pairs={{0,16},{4,20},{8,24},{12,28},{16,0},{20,4},{24,8},{28,12},{1,17},{... | collective-permute-start | bytes 491528 | tf_op jit(solution)/shard_map/ppermute | solution.py:491
  9.5 1.8 collective-permute-start.7
  12.6 1.8 collective-permute-start.1
  14.4 1.9 multiply_sine_fusion
  16.3 4.7 %collective-permute-done.1 = bf16[256,640]{1,0:T(8,128)(2,1)S(1)} collective-permute-done((bf16[256,640]{1,0:T(8,128)(2,1)S(1)}, bf16[256,640]{1,0:T(8,128)(2,1)S(1)}, u32[]{:S(2)}, u32[]{:S(2)}) %collective-permute-start.1) | collective-permute-done | bytes 327712 | tf_op jit(solution)/shard_map/ppermute | solution.py:491
  24.5 1.5 collective-permute-start.9
  26.9 1.5 collective-permute-start.4
  28.4 5.7 %collective-permute-done.9.refs_5_.refs_18_ = bf16[256,640]{1,0:T(8,128)(2,1)S(1)} collective-permute-done((bf16[256,640]{1,0:T(8,128)(2,1)S(1)}, bf16[256,640]{1,0:T(8,128)(2,1)S(1)}, u32[]{:S(2)}, u32[]{:S(2)}) %collective-permute-start.9) | collective-permute-done | bytes 327712 | tf_op jit(solution)/shard_map/ppermute | solution.py:491
  34.3 2.1 %collective-permute-done.4 = bf16[256,640]{1,0:T(8,128)(2,1)S(1)} collective-permute-done((bf16[256,640]{1,0:T(8,128)(2,1)}, bf16[256,640]{1,0:T(8,128)(2,1)S(1)}, u32[]{:S(2)}, u32[]{:S(2)}) %collective-permute-start.4) | collective-permute-done | bytes 327712 | tf_op jit(solution)/shard_map/ppermute | solution.py:491
  38.6 3.1 %shard_map.204 = (bf16[1024,640]{1,0:T(8,128)(2,1)S(1)}, f32[1024,256]{1,0:T(8,128)S(1)}, bf16[1024,512]{1,0:T(8,128)(2,1)S(1)}, f32[4,128,256]{2,1,0:T(8,128)S(...) custom-call(s32[1]{0:T(128)} %bitcast.refs_0_, ...), custom_call_target="tpu_custom_call" | custom-call | flops 6600000000 | bytes 4395524 | tf_op jit(solution)/shard_map/pallas_call | solution.py:66
  48.5 4.4 %collective-permute-done.11.refs_1_ = bf16[128,640]{1,0:T(8,128)(2,1)S(1)} collective-permute-done((bf16[128,640]{1,0:T(8,128)(2,1)S(1)}, bf16[128,640]{1,0:T(8,128)(2,1)S(1)}, u32[]{:S(2)}, u32[]{:S(2)}) %collective-permute-start.11) | collective-permute-done | bytes 163872 | tf_op jit(solution)/shard_map/ppermute | solution.py:491
  52.9 1.9 shard_map.206
  56.1 1.5 collective-permute-start.15
  57.8 4.1 %collective-permute-done.17.refs_6_.refs_3_ = bf16[128,416]{1,0:T(8,128)(2,1)S(1)} collective-permute-done((bf16[128,416]{1,0:T(8,128)(2,1)S(1)}, bf16[128,416]{1,0:T(8,128)(2,1)S(1)}, u32[]{:S(2)}, u32[]{:S(2)}) %collective-permute-start.17) | collective-permute-done | bytes 106528 | tf_op jit(solution)/shard_map/ppermute | solution.py:491
  61.9 3.1 %collective-permute-done.15.refs_1_ = bf16[128,640]{1,0:T(8,128)(2,1)S(1)} collective-permute-done((bf16[128,640]{1,0:T(8,128)(2,1)S(1)}, bf16[128,640]{1,0:T(8,128)(2,1)S(1)}, u32[]{:S(2)}, u32[]{:S(2)}) %collective-permute-start.15) | collective-permute-done | bytes 163872 | tf_op jit(solution)/shard_map/ppermute | solution.py:491
  66.5 5.3 %collective-permute-done.19.refs_1_ = bf16[128,640]{1,0:T(8,128)(2,1)S(1)} collective-permute-done((bf16[128,640]{1,0:T(8,128)(2,1)S(1)}, bf16[128,640]{1,0:T(8,128)(2,1)S(1)}, u32[]{:S(2)}, u32[]{:S(2)}) %collective-permute-start.19) | collective-permute-done | bytes 163872 | tf_op jit(solution)/shard_map/ppermute | solution.py:491
  71.8 2.1 %shard_map.208 = (f32[128,640]{1,0:T(8,128)S(1)}, bf16[128,640]{1,0:T(8,128)(2,1)S(1)}, bf16[256,1664]{1,0:T(8,128)(2,1)}, bf16[256,1024]{1,0:T(8,128)(2,1)S(1)}) custom-call(bf16[128,640]{1,0:T(8,128)(2,1)S(1)} %get-tuple-element.107.refs_0_, bf16[128,640]{1,0:T(8,128)(2,1)S(1)} %collective-permute-done.19.refs_1_, ...), custom_call_target="tpu_custom_call" | custom-call | flops 3960000000 | bytes 5308416 | tf_op jit(solution)/shard_map/pallas_call | solution.py:66
  76.6 2.2 %collective-permute-done.22.refs_5_ = bf16[256,1664]{1,0:T(8,128)(2,1)} collective-permute-done((bf16[256,1664]{1,0:T(8,128)(2,1)}, bf16[256,1664]{1,0:T(8,128)(2,1)}, u32[]{:S(2)}, u32[]{:S(2)}) %collective-permute-start.22) | collective-permute-done | bytes 852000 | tf_op jit(solution)/shard_map/ppermute | solution.py:491
  83.0 2.9 %shard_map.209 = (bf16[1280,512]{1,0:T(8,128)(2,1)S(1)}, bf16[640,512]{1,0:T(8,128)(2,1)S(1)}) custom-call(bf16[256,1152]{1,0:T(8,128)(2,1)S(1)} %copy-done.27, bf16[256,512]{1,0:T(8,128)(2,1)S(1)} %copy-done.53, bf16[256,1152]{1,0:T(8,128)(2,1)S(1)} %copy-done.29, bf16[256,1664]{1,0:T(8,128)(2,1)} %get-tuple-element.115.refs_3_, ...), custom_call_target="tpu_custom_call" | custom-call | flops 2750000128 | bytes 3670016 | tf_op jit(solution)/shard_map/pallas_call | solution.py:66
  88.9 5.0 %collective-permute-done.23.refs_20_.refs_7_ = bf16[128,640]{1,0:T(8,128)(2,1)S(1)} collective-permute-done((bf16[128,640]{1,0:T(8,128)(2,1)S(1)}, bf16[128,640]{1,0:T(8,128)(2,1)S(1)}, u32[]{:S(2)}, u32[]{:S(2)}) %collective-permute-start.23) | collective-permute-done | bytes 163872 | tf_op jit(solution)/shard_map/ppermute | solution.py:491
  94.0 4.3 %shard_map.211 = (bf16[592,512]{1,0:T(8,128)(2,1)S(1)}, f32[160,512]{1,0:T(8,128)S(1)}, f32[160,512]{1,0:T(8,128)S(1)}, bf16[512,512]{1,0:T(8,128)(2,1)S(1)}, bf16[512,512]{1,0:T(8,128)(2,1)S(1)}) custom-call(s32[1]{0:T(128)} %bitcast.refs_0_, bf16[128,640]{1,0:T(8,128)(2,1)S(1)} %get-tuple-element.118.refs_1_.refs_5_, ...), custom_call_target="tpu_custom_call" | custom-call | flops 9900000256 | bytes 7258116 | tf_op jit(solution)/shard_map/pallas_call | solution.py:66
  99.0 1.6 collective-permute-start.24
  100.5 4.2 %collective-permute-done.26 = bf16[640,512]{1,0:T(8,128)(2,1)S(1)} collective-permute-done((bf16[640,512]{1,0:T(8,128)(2,1)S(1)}, bf16[640,512]{1,0:T(8,128)(2,1)S(1)}, u32[]{:S(2)}, u32[]{:S(2)}) %collective-permute-start.26) | collective-permute-done | bytes 655392 | tf_op jit(solution)/shard_map/ppermute | solution.py:491
  105.1 1.6 collective-permute-start.30
  107.1 6.1 %collective-permute-done.28.refs_1_ = bf16[592,512]{1,0:T(8,128)(2,1)S(1)} collective-permute-done((bf16[592,512]{1,0:T(8,128)(2,1)S(1)}, bf16[592,512]{1,0:T(8,128)(2,1)S(1)}, u32[]{:S(2)}, u32[]{:S(2)}) %collective-permute-start.28) | collective-permute-done | bytes 606240 | tf_op jit(solution)/shard_map/ppermute | solution.py:491
  113.5 1.6 collective-permute-start.27
  115.1 5.7 %collective-permute-done.30 = bf16[320,512]{1,0:T(8,128)(2,1)S(1)} collective-permute-done((bf16[320,512]{1,0:T(8,128)(2,1)S(1)}, bf16[320,512]{1,0:T(8,128)(2,1)S(1)}, u32[]{:S(2)}, u32[]{:S(2)}) %collective-permute-start.30) | collective-permute-done | bytes 327712 | tf_op jit(solution)/shard_map/ppermute | solution.py:491
  120.9 1.7 collective-permute-start.36
  123.1 1.6 collective-permute-start.35
  124.6 6.7 %collective-permute-done.27 = bf16[480,512]{1,0:T(8,128)(2,1)S(1)} collective-permute-done((bf16[480,512]{1,0:T(8,128)(2,1)S(1)}, bf16[480,512]{1,0:T(8,128)(2,1)S(1)}, u32[]{:S(2)}, u32[]{:S(2)}) %collective-permute-start.27) | collective-permute-done | bytes 491552 | tf_op jit(solution)/shard_map/ppermute | solution.py:491
  132.5 3.5 %collective-permute-start.40 = (bf16[160,512]{1,0:T(8,128)(2,1)S(1)}, bf16[160,512]{1,0:T(8,128)(2,1)S(1)}, u32[]{:S(2)}, u32[]{:S(2)}) collective-permute-start(bf16[160,512]{1,0:T(8,128)(2,1)S(1)} %add_convert_fusion.4), channel_id=1, source_target_pairs={{0,16},{4,20},{8,24},{12,28},{16,0},{20,4},{24,8},{28,12},{1,17},{... | collective-permute-start | bytes 491528 | tf_op jit(solution)/shard_map/ppermute | solution.py:491
  137.6 2.9 %collective-permute-start.33 = (bf16[128,512]{1,0:T(8,128)(2,1)S(1)}, bf16[128,512]{1,0:T(8,128)(2,1)S(1)}, u32[]{:S(2)}, u32[]{:S(2)}) collective-permute-start(bf16[128,512]{1,0:T(8,128)(2,1)S(1)} %get-tuple-element.185), channel_id=1, source_target_pairs={{0,8},{4,12},{8,0},{12,4},{16,24},{20,28},{24,16},{28,20},{1,9},{5... | collective-permute-start | bytes 393224 | tf_op jit(solution)/shard_map/ppermute | solution.py:491
  140.7 3.6 %collective-permute-done.34 = bf16[240,512]{1,0:T(8,128)(2,1)S(1)} collective-permute-done((bf16[240,512]{1,0:T(8,128)(2,1)S(1)}, bf16[240,512]{1,0:T(8,128)(2,1)S(1)}, u32[]{:S(2)}, u32[]{:S(2)}) %collective-permute-start.34) | collective-permute-done | bytes 245792 | tf_op jit(solution)/shard_map/ppermute | solution.py:491
  144.3 5.1 %collective-permute-done.40 = bf16[160,512]{1,0:T(8,128)(2,1)S(1)} collective-permute-done((bf16[160,512]{1,0:T(8,128)(2,1)S(1)}, bf16[160,512]{1,0:T(8,128)(2,1)S(1)}, u32[]{:S(2)}, u32[]{:S(2)}) %collective-permute-start.40) | collective-permute-done | bytes 163872 | tf_op jit(solution)/shard_map/ppermute | solution.py:491
  149.5 4.1 %collective-permute-start.37 = (bf16[64,512]{1,0:T(8,128)(2,1)S(1)}, bf16[64,512]{1,0:T(8,128)(2,1)S(1)}, u32[]{:S(2)}, u32[]{:S(2)}) collective-permute-start(bf16[64,512]{1,0:T(8,128)(2,1)S(1)} %get-tuple-element.198), channel_id=1, source_target_pairs={{0,24},{4,28},{8,16},{12,20},{16,8},{20,12},{24,0},{28,4},{1,25},{... | collective-permute-start | bytes 196616 | tf_op jit(solution)/shard_map/ppermute | solution.py:491
  153.5 1.6 collective-permute-start.39
  155.1 4.9 %collective-permute-done.32 = bf16[128,512]{1,0:T(8,128)(2,1)S(1)} collective-permute-done((bf16[128,512]{1,0:T(8,128)(2,1)S(1)}, bf16[128,512]{1,0:T(8,128)(2,1)S(1)}, u32[]{:S(2)}, u32[]{:S(2)}) %collective-permute-start.32) | collective-permute-done | bytes 131104 | tf_op jit(solution)/shard_map/ppermute | solution.py:491
  160.1 1.5 collective-permute-start.44
  162.5 1.9 collective-permute-start.41
  166.9 5.0 %collective-permute-done.45 = bf16[120,512]{1,0:T(8,128)(2,1)S(1)} collective-permute-done((bf16[120,512]{1,0:T(8,128)(2,1)S(1)}, bf16[120,512]{1,0:T(8,128)(2,1)S(1)}, u32[]{:S(2)}, u32[]{:S(2)}) %collective-permute-start.45) | collective-permute-done | bytes 122912 | tf_op jit(solution)/shard_map/ppermute | solution.py:491
  173.4 4.6 %collective-permute-done.47 = bf16[120,512]{1,0:T(8,128)(2,1)S(1)} collective-permute-done((bf16[120,512]{1,0:T(8,128)(2,1)S(1)}, bf16[120,512]{1,0:T(8,128)(2,1)S(1)}, u32[]{:S(2)}, u32[]{:S(2)}) %collective-permute-start.47) | collective-permute-done | bytes 122912 | tf_op jit(solution)/shard_map/ppermute | solution.py:491
  178.2 1.7 shard_map.215
  181.4 2.0 %collective-permute-start.50 = (bf16[640,512]{1,0:T(8,128)(2,1)S(1)}, bf16[640,512]{1,0:T(8,128)(2,1)S(1)}, u32[]{:S(2)}, u32[]{:S(2)}) collective-permute-start(bf16[640,512]{1,0:T(8,128)(2,1)S(1)} %pad_maximum_fusion.2.refs_1_), channel_id=1, source_target_pairs={{0,8},{4,12},{8,0},{12,4},{16,24},{20,28},{24,16},{28,20},{1,9},{5... | collective-permute-start | bytes 1966088 | tf_op jit(solution)/shard_map/ppermute | solution.py:491
  183.4 3.6 %collective-permute-done.48 = bf16[240,512]{1,0:T(8,128)(2,1)S(1)} collective-permute-done((bf16[240,512]{1,0:T(8,128)(2,1)S(1)}, bf16[240,512]{1,0:T(8,128)(2,1)S(1)}, u32[]{:S(2)}, u32[]{:S(2)}) %collective-permute-start.48) | collective-permute-done | bytes 245792 | tf_op jit(solution)/shard_map/ppermute | solution.py:491
  187.1 1.5 collective-permute-start.49
  191.6 5.2 %collective-permute-done.50.refs_2_ = bf16[640,512]{1,0:T(8,128)(2,1)S(1)} collective-permute-done((bf16[640,512]{1,0:T(8,128)(2,1)S(1)}, bf16[640,512]{1,0:T(8,128)(2,1)S(1)}, u32[]{:S(2)}, u32[]{:S(2)}) %collective-permute-start.50) | collective-permute-done | bytes 655392 | tf_op jit(solution)/shard_map/ppermute | solution.py:491
  196.8 1.7 shard_map.218
  (291 shorter events, 46.5 us)
Async XLA Ops:
  0.7 11.9 %collective-permute-start = (bf16[128,640]{1,0:T(8,128)(2,1)}, bf16[128,640]{1,0:T(8,128)(2,1)S(1)}, u32[]{:S(2)}, u32[]{:S(2)}) collective-permute-start(bf16[128,640]{1,0:T(8,128)(2,1)} %refs_1_.3), channel_id=1, source_target_pairs={{0,8},{4,12},{8,0},{12,4},{16,24},{20,28},{24,16},{28,20},{1,9},{5... | collective-permute-start | bytes 491528 | tf_op jit(solution)/shard_map/ppermute | solution.py:491
  3.8 17.4 %collective-permute-start.2 = (bf16[128,640]{1,0:T(8,128)(2,1)}, bf16[128,640]{1,0:T(8,128)(2,1)S(1)}, u32[]{:S(2)}, u32[]{:S(2)}) collective-permute-start(bf16[128,640]{1,0:T(8,128)(2,1)} %refs_1_.3), channel_id=1, source_target_pairs={{0,16},{4,20},{8,24},{12,28},{16,0},{20,4},{24,8},{28,12},{1,17},{... | collective-permute-start | bytes 491528 | tf_op jit(solution)/shard_map/ppermute | solution.py:491
  6.3 14.9 %collective-permute-start.3 = (bf16[128,640]{1,0:T(8,128)(2,1)}, bf16[128,640]{1,0:T(8,128)(2,1)S(1)}, u32[]{:S(2)}, u32[]{:S(2)}) collective-permute-start(bf16[128,640]{1,0:T(8,128)(2,1)} %refs_1_.3), channel_id=1, source_target_pairs={{0,24},{4,28},{8,16},{12,20},{16,8},{20,12},{24,0},{28,4},{1,25},{... | collective-permute-start | bytes 491528 | tf_op jit(solution)/shard_map/ppermute | solution.py:491
  9.5 11.8 %collective-permute-start.7 = (bf16[176,512]{1,0:T(8,128)(2,1)S(1)}, bf16[176,512]{1,0:T(8,128)(2,1)S(1)}, u32[]{:S(2)}, u32[]{:S(2)}) collective-permute-start(bf16[176,512]{1,0:T(8,128)(2,1)S(1)} %shard_map.203.refs_10_), channel_id=1, source_target_pairs={{0,2},{1,3},{2,0},{3,1},{4,6},{5,7},{6,4},{7,5},{8,10},{9,11},{10,... | collective-permute-start | bytes 540680 | tf_op jit(solution)/shard_map/ppermute | solution.py:491
  11.3 11.1 %collective-permute-start.5 = (bf16[160,1024]{1,0:T(8,128)(2,1)S(1)}, bf16[160,1024]{1,0:T(8,128)(2,1)S(1)}, u32[]{:S(2)}, u32[]{:S(2)}) collective-permute-start(bf16[160,1024]{1,0:T(8,128)(2,1)S(1)} %copy-done.2), channel_id=1, source_target_pairs={{0,2},{1,3},{2,0},{3,1},{4,6},{5,7},{6,4},{7,5},{8,10},{9,11},{10,... | collective-permute-start | bytes 983048 | tf_op jit(solution)/shard_map/ppermute | solution.py:491
  12.6 8.4 %collective-permute-start.1 = (bf16[256,640]{1,0:T(8,128)(2,1)S(1)}, bf16[256,640]{1,0:T(8,128)(2,1)S(1)}, u32[]{:S(2)}, u32[]{:S(2)}) collective-permute-start(bf16[256,640]{1,0:T(8,128)(2,1)S(1)} %pad_maximum_fusion.5), channel_id=1, source_target_pairs={{0,4},{4,0},{8,12},{12,8},{16,20},{20,16},{24,28},{28,24},{1,5},{5... | collective-permute-start | bytes 983048 | tf_op jit(solution)/shard_map/ppermute | solution.py:491
  23.2 10.9 %collective-permute-start.6 = (bf16[320,1024]{1,0:T(8,128)(2,1)}, bf16[320,1024]{1,0:T(8,128)(2,1)}, u32[]{:S(2)}, u32[]{:S(2)}) collective-permute-start(bf16[320,1024]{1,0:T(8,128)(2,1)} %pad_maximum_fusion), channel_id=1, source_target_pairs={{0,1},{1,0},{2,3},{3,2},{4,5},{5,4},{6,7},{7,6},{8,9},{9,8},{10,11... | collective-permute-start | bytes 1966088 | tf_op jit(solution)/shard_map/ppermute | solution.py:491
  24.0 4.4 %collective-permute-start.8 = (bf16[352,512]{1,0:T(8,128)(2,1)}, bf16[352,512]{1,0:T(8,128)(2,1)S(1)}, u32[]{:S(2)}, u32[]{:S(2)}) collective-permute-start(bf16[352,512]{1,0:T(8,128)(2,1)} %pad_maximum_fusion.4), channel_id=1, source_target_pairs={{0,1},{1,0},{2,3},{3,2},{4,5},{5,4},{6,7},{7,6},{8,9},{9,8},{10,11... | collective-permute-start | bytes 1081352 | tf_op jit(solution)/shard_map/ppermute | solution.py:491
  24.5 9.6 %collective-permute-start.9 = (bf16[256,640]{1,0:T(8,128)(2,1)S(1)}, bf16[256,640]{1,0:T(8,128)(2,1)S(1)}, u32[]{:S(2)}, u32[]{:S(2)}) collective-permute-start(bf16[256,640]{1,0:T(8,128)(2,1)S(1)} %copy-done.1), channel_id=1, source_target_pairs={{0,2},{1,3},{2,0},{3,1},{4,6},{5,7},{6,4},{7,5},{8,10},{9,11},{10,... | collective-permute-start | bytes 983048 | tf_op jit(solution)/shard_map/ppermute | solution.py:491
  26.9 9.5 %collective-permute-start.4 = (bf16[256,640]{1,0:T(8,128)(2,1)}, bf16[256,640]{1,0:T(8,128)(2,1)S(1)}, u32[]{:S(2)}, u32[]{:S(2)}) collective-permute-start(bf16[256,640]{1,0:T(8,128)(2,1)} %copy-done.68), channel_id=1, source_target_pairs={{0,4},{4,0},{8,12},{12,8},{16,20},{20,16},{24,28},{28,24},{1,5},{5... | collective-permute-start | bytes 983048 | tf_op jit(solution)/shard_map/ppermute | solution.py:491
  37.9 15.0 %collective-permute-start.12 = (bf16[640,512]{1,0:T(8,128)(2,1)S(1)}, bf16[640,512]{1,0:T(8,128)(2,1)S(1)}, u32[]{:S(2)}, u32[]{:S(2)}) collective-permute-start(bf16[640,512]{1,0:T(8,128)(2,1)S(1)} %copy-done.23), channel_id=1, source_target_pairs={{0,1},{1,0},{2,3},{3,2},{4,5},{5,4},{6,7},{7,6},{8,9},{9,8},{10,11... | collective-permute-start | bytes 1966088 | tf_op jit(solution)/shard_map/ppermute | solution.py:491
  38.0 14.9 %collective-permute-start.13 = (bf16[640,512]{1,0:T(8,128)(2,1)S(1)}, bf16[640,512]{1,0:T(8,128)(2,1)S(1)}, u32[]{:S(2)}, u32[]{:S(2)}) collective-permute-start(bf16[640,512]{1,0:T(8,128)(2,1)S(1)} %copy-done.24), channel_id=1, source_target_pairs={{0,1},{1,0},{2,3},{3,2},{4,5},{5,4},{6,7},{7,6},{8,9},{9,8},{10,11... | collective-permute-start | bytes 1966088 | tf_op jit(solution)/shard_map/ppermute | solution.py:491
  38.5 14.4 %collective-permute-start.14 = (bf16[512,640]{1,0:T(8,128)(2,1)S(1)}, bf16[512,640]{1,0:T(8,128)(2,1)S(1)}, u32[]{:S(2)}, u32[]{:S(2)}) collective-permute-start(bf16[512,640]{1,0:T(8,128)(2,1)S(1)} %copy-done.25), channel_id=1, source_target_pairs={{0,1},{1,0},{2,3},{3,2},{4,5},{5,4},{6,7},{7,6},{8,9},{9,8},{10,11... | collective-permute-start | bytes 1966088 | tf_op jit(solution)/shard_map/ppermute | solution.py:491
  45.9 7.0 %collective-permute-start.11 = (bf16[128,640]{1,0:T(8,128)(2,1)S(1)}, bf16[128,640]{1,0:T(8,128)(2,1)S(1)}, u32[]{:S(2)}, u32[]{:S(2)}) collective-permute-start(bf16[128,640]{1,0:T(8,128)(2,1)S(1)} %get-tuple-element.98.refs_0_), channel_id=1, source_target_pairs={{0,2},{1,3},{2,0},{3,1},{4,6},{5,7},{6,4},{7,5},{8,10},{9,11},{10,... | collective-permute-start | bytes 491528 | tf_op jit(solution)/shard_map/ppermute | solution.py:491
  47.2 10.6 %collective-permute-start.18 = (bf16[128,416]{1,0:T(8,128)(2,1)S(1)}, bf16[128,416]{1,0:T(8,128)(2,1)S(1)}, u32[]{:S(2)}, u32[]{:S(2)}) collective-permute-start(bf16[128,416]{1,0:T(8,128)(2,1)S(1)} %pad_maximum_fusion.10), channel_id=1, source_target_pairs={{0,3},{1,2},{2,1},{3,0},{4,7},{5,6},{6,5},{7,4},{8,11},{9,10},{10,... | collective-permute-start | bytes 319496 | tf_op jit(solution)/shard_map/ppermute | solution.py:491
  55.5 16.3 %collective-permute-start.20 = (bf16[256,1152]{1,0:T(8,128)(2,1)S(1)}, bf16[256,1152]{1,0:T(8,128)(2,1)S(1)}, u32[]{:S(2)}, u32[]{:S(2)}) collective-permute-start(bf16[256,1152]{1,0:T(8,128)(2,1)S(1)} %get-tuple-element.110.refs_0_), channel_id=1, source_target_pairs={{0,1},{1,0},{2,3},{3,2},{4,5},{5,4},{6,7},{7,6},{8,9},{9,8},{10,11... | collective-permute-start | bytes 1769480 | tf_op jit(solution)/shard_map/ppermute | solution.py:491
  55.6 6.4 %collective-permute-start.17 = (bf16[128,416]{1,0:T(8,128)(2,1)S(1)}, bf16[128,416]{1,0:T(8,128)(2,1)S(1)}, u32[]{:S(2)}, u32[]{:S(2)}) collective-permute-start(bf16[128,416]{1,0:T(8,128)(2,1)S(1)} %pad_maximum_fusion.9), channel_id=1, source_target_pairs={{0,2},{1,3},{2,0},{3,1},{4,6},{5,7},{6,4},{7,5},{8,10},{9,11},{10,... | collective-permute-start | bytes 319496 | tf_op jit(solution)/shard_map/ppermute | solution.py:491
  56.1 8.9 %collective-permute-start.15 = (bf16[128,640]{1,0:T(8,128)(2,1)S(1)}, bf16[128,640]{1,0:T(8,128)(2,1)S(1)}, u32[]{:S(2)}, u32[]{:S(2)}) collective-permute-start(bf16[128,640]{1,0:T(8,128)(2,1)S(1)} %get-tuple-element.103), channel_id=1, source_target_pairs={{0,2},{1,3},{2,0},{3,1},{4,6},{5,7},{6,4},{7,5},{8,10},{9,11},{10,... | collective-permute-start | bytes 491528 | tf_op jit(solution)/shard_map/ppermute | solution.py:491
  65.9 5.9 %collective-permute-start.19 = (bf16[128,640]{1,0:T(8,128)(2,1)S(1)}, bf16[128,640]{1,0:T(8,128)(2,1)S(1)}, u32[]{:S(2)}, u32[]{:S(2)}) collective-permute-start(bf16[128,640]{1,0:T(8,128)(2,1)S(1)} %get-tuple-element.107.refs_0_), channel_id=1, source_target_pairs={{0,2},{1,3},{2,0},{3,1},{4,6},{5,7},{6,4},{7,5},{8,10},{9,11},{10,... | collective-permute-start | bytes 491528 | tf_op jit(solution)/shard_map/ppermute | solution.py:491
  76.1 9.9 %collective-permute-start.21 = (bf16[128,640]{1,0:T(8,128)(2,1)}, bf16[128,640]{1,0:T(8,128)(2,1)S(1)}, u32[]{:S(2)}, u32[]{:S(2)}) collective-permute-start(bf16[128,640]{1,0:T(8,128)(2,1)} %copy-done.32), channel_id=1, source_target_pairs={{0,2},{1,3},{2,0},{3,1},{4,6},{5,7},{6,4},{7,5},{8,10},{9,11},{10,... | collective-permute-start | bytes 491528 | tf_op jit(solution)/shard_map/ppermute | solution.py:491
  87.6 6.3 %collective-permute-start.23 = (bf16[128,640]{1,0:T(8,128)(2,1)S(1)}, bf16[128,640]{1,0:T(8,128)(2,1)S(1)}, u32[]{:S(2)}, u32[]{:S(2)}) collective-permute-start(bf16[128,640]{1,0:T(8,128)(2,1)S(1)} %get-tuple-element.118.refs_1_.refs_5_), channel_id=1, source_target_pairs={{0,2},{1,3},{2,0},{3,1},{4,6},{5,7},{6,4},{7,5},{8,10},{9,11},{10,... | collective-permute-start | bytes 491528 | tf_op jit(solution)/shard_map/ppermute | solution.py:491
  88.2 16.6 %collective-permute-start.26 = (bf16[640,512]{1,0:T(8,128)(2,1)S(1)}, bf16[640,512]{1,0:T(8,128)(2,1)S(1)}, u32[]{:S(2)}, u32[]{:S(2)}) collective-permute-start(bf16[640,512]{1,0:T(8,128)(2,1)S(1)} %broadcast_select_fusion.refs_6_), channel_id=1, source_target_pairs={{0,8},{4,12},{8,0},{12,4},{16,24},{20,28},{24,16},{28,20},{1,9},{5... | collective-permute-start | bytes 1966088 | tf_op jit(solution)/shard_map/ppermute | solution.py:491
  98.3 14.9 %collective-permute-start.28 = (bf16[592,512]{1,0:T(8,128)(2,1)S(1)}, bf16[592,512]{1,0:T(8,128)(2,1)S(1)}, u32[]{:S(2)}, u32[]{:S(2)}) collective-permute-start(bf16[592,512]{1,0:T(8,128)(2,1)S(1)} %get-tuple-element.131.refs_0_.refs_3_), channel_id=1, source_target_pairs={{0,2},{1,3},{2,0},{3,1},{4,6},{5,7},{6,4},{7,5},{8,10},{9,11},{10,... | collective-permute-start | bytes 1818632 | tf_op jit(solution)/shard_map/ppermute | solution.py:491
  98.9 7.8 %collective-permute-start.25 = (bf16[256,640]{1,0:T(8,128)(2,1)S(1)}, bf16[256,640]{1,0:T(8,128)(2,1)S(1)}, u32[]{:S(2)}, u32[]{:S(2)}) collective-permute-start(bf16[256,640]{1,0:T(8,128)(2,1)S(1)} %constant_dynamic-update-slice_fusion.6), channel_id=1, source_target_pairs={{0,1},{1,0},{2,3},{3,2},{4,5},{5,4},{6,7},{7,6},{8,9},{9,8},{10,11... | collective-permute-start | bytes 983048 | tf_op jit(solution)/shard_map/ppermute | solution.py:491
  99.0 33.3 %collective-permute-start.24 = (bf16[512,512]{1,0:T(8,128)(2,1)S(1)}, bf16[512,512]{1,0:T(8,128)(2,1)S(1)}, u32[]{:S(2)}, u32[]{:S(2)}) collective-permute-start(bf16[512,512]{1,0:T(8,128)(2,1)S(1)} %get-tuple-element.129), channel_id=1, source_target_pairs={{0,4},{4,0},{8,12},{12,8},{16,20},{20,16},{24,28},{28,24},{1,5},{5... | collective-permute-start | bytes 1572872 | tf_op jit(solution)/shard_map/ppermute | solution.py:491
  105.1 15.7 %collective-permute-start.30 = (bf16[320,512]{1,0:T(8,128)(2,1)S(1)}, bf16[320,512]{1,0:T(8,128)(2,1)S(1)}, u32[]{:S(2)}, u32[]{:S(2)}) collective-permute-start(bf16[320,512]{1,0:T(8,128)(2,1)S(1)} %broadcast_select_fusion.4), channel_id=1, source_target_pairs={{0,4},{4,0},{8,12},{12,8},{16,20},{20,16},{24,28},{28,24},{1,5},{5... | collective-permute-start | bytes 983048 | tf_op jit(solution)/shard_map/ppermute | solution.py:491
  113.3 9.3 %collective-permute-start.29 = (bf16[704,512]{1,0:T(8,128)(2,1)S(1)}, bf16[704,512]{1,0:T(8,128)(2,1)S(1)}, u32[]{:S(2)}, u32[]{:S(2)}) collective-permute-start(bf16[704,512]{1,0:T(8,128)(2,1)S(1)} %get-tuple-element.138), channel_id=1, source_target_pairs={{0,1},{1,0},{2,3},{3,2},{4,5},{5,4},{6,7},{7,6},{8,9},{9,8},{10,11... | collective-permute-start | bytes 2162696 | tf_op jit(solution)/shard_map/ppermute | solution.py:491
  113.5 17.8 %collective-permute-start.27 = (bf16[480,512]{1,0:T(8,128)(2,1)S(1)}, bf16[480,512]{1,0:T(8,128)(2,1)S(1)}, u32[]{:S(2)}, u32[]{:S(2)}) collective-permute-start(bf16[480,512]{1,0:T(8,128)(2,1)S(1)} %broadcast_select_fusion.1), channel_id=1, source_target_pairs={{0,4},{4,0},{8,12},{12,8},{16,20},{20,16},{24,28},{28,24},{1,5},{5... | collective-permute-start | bytes 1474568 | tf_op jit(solution)/shard_map/ppermute | solution.py:491
  120.9 11.5 %collective-permute-start.36 = (bf16[160,512]{1,0:T(8,128)(2,1)S(1)}, bf16[160,512]{1,0:T(8,128)(2,1)S(1)}, u32[]{:S(2)}, u32[]{:S(2)}) collective-permute-start(bf16[160,512]{1,0:T(8,128)(2,1)S(1)} %broadcast_select_fusion.11), channel_id=1, source_target_pairs={{0,16},{4,20},{8,24},{12,28},{16,0},{20,4},{24,8},{28,12},{1,17},{... | collective-permute-start | bytes 491528 | tf_op jit(solution)/shard_map/ppermute | solution.py:491
  123.1 14.6 %collective-permute-start.35 = (bf16[256,512]{1,0:T(8,128)(2,1)S(1)}, bf16[256,512]{1,0:T(8,128)(2,1)S(1)}, u32[]{:S(2)}, u32[]{:S(2)}) collective-permute-start(bf16[256,512]{1,0:T(8,128)(2,1)S(1)} %broadcast_select_fusion.5), channel_id=1, source_target_pairs={{0,4},{4,0},{8,12},{12,8},{16,20},{20,16},{24,28},{28,24},{1,5},{5... | collective-permute-start | bytes 786440 | tf_op jit(solution)/shard_map/ppermute | solution.py:491
  131.5 12.7 %collective-permute-start.34 = (bf16[240,512]{1,0:T(8,128)(2,1)S(1)}, bf16[240,512]{1,0:T(8,128)(2,1)S(1)}, u32[]{:S(2)}, u32[]{:S(2)}) collective-permute-start(bf16[240,512]{1,0:T(8,128)(2,1)S(1)} %broadcast_select_fusion.8), channel_id=1, source_target_pairs={{0,8},{4,12},{8,0},{12,4},{16,24},{20,28},{24,16},{28,20},{1,9},{5... | collective-permute-start | bytes 737288 | tf_op jit(solution)/shard_map/ppermute | solution.py:491
  132.5 16.9 %collective-permute-start.40 = (bf16[160,512]{1,0:T(8,128)(2,1)S(1)}, bf16[160,512]{1,0:T(8,128)(2,1)S(1)}, u32[]{:S(2)}, u32[]{:S(2)}) collective-permute-start(bf16[160,512]{1,0:T(8,128)(2,1)S(1)} %add_convert_fusion.4), channel_id=1, source_target_pairs={{0,16},{4,20},{8,24},{12,28},{16,0},{20,4},{24,8},{28,12},{1,17},{... | collective-permute-start | bytes 491528 | tf_op jit(solution)/shard_map/ppermute | solution.py:491
  136.1 17.4 %collective-permute-start.31 = (bf16[128,512]{1,0:T(8,128)(2,1)S(1)}, bf16[128,512]{1,0:T(8,128)(2,1)S(1)}, u32[]{:S(2)}, u32[]{:S(2)}) collective-permute-start(bf16[128,512]{1,0:T(8,128)(2,1)S(1)} %get-tuple-element.187), channel_id=1, source_target_pairs={{0,24},{4,28},{8,16},{12,20},{16,8},{20,12},{24,0},{28,4},{1,25},{... | collective-permute-start | bytes 393224 | tf_op jit(solution)/shard_map/ppermute | solution.py:491
  136.4 23.6 %collective-permute-start.32 = (bf16[128,512]{1,0:T(8,128)(2,1)S(1)}, bf16[128,512]{1,0:T(8,128)(2,1)S(1)}, u32[]{:S(2)}, u32[]{:S(2)}) collective-permute-start(bf16[128,512]{1,0:T(8,128)(2,1)S(1)} %get-tuple-element.186), channel_id=1, source_target_pairs={{0,16},{4,20},{8,24},{12,28},{16,0},{20,4},{24,8},{28,12},{1,17},{... | collective-permute-start | bytes 393224 | tf_op jit(solution)/shard_map/ppermute | solution.py:491
  137.6 22.4 %collective-permute-start.33 = (bf16[128,512]{1,0:T(8,128)(2,1)S(1)}, bf16[128,512]{1,0:T(8,128)(2,1)S(1)}, u32[]{:S(2)}, u32[]{:S(2)}) collective-permute-start(bf16[128,512]{1,0:T(8,128)(2,1)S(1)} %get-tuple-element.185), channel_id=1, source_target_pairs={{0,8},{4,12},{8,0},{12,4},{16,24},{20,28},{24,16},{28,20},{1,9},{5... | collective-permute-start | bytes 393224 | tf_op jit(solution)/shard_map/ppermute | solution.py:491
  149.5 12.1 %collective-permute-start.37 = (bf16[64,512]{1,0:T(8,128)(2,1)S(1)}, bf16[64,512]{1,0:T(8,128)(2,1)S(1)}, u32[]{:S(2)}, u32[]{:S(2)}) collective-permute-start(bf16[64,512]{1,0:T(8,128)(2,1)S(1)} %get-tuple-element.198), channel_id=1, source_target_pairs={{0,24},{4,28},{8,16},{12,20},{16,8},{20,12},{24,0},{28,4},{1,25},{... | collective-permute-start | bytes 196616 | tf_op jit(solution)/shard_map/ppermute | solution.py:491
  153.5 8.9 %collective-permute-start.38 = (bf16[64,512]{1,0:T(8,128)(2,1)S(1)}, bf16[64,512]{1,0:T(8,128)(2,1)S(1)}, u32[]{:S(2)}, u32[]{:S(2)}) collective-permute-start(bf16[64,512]{1,0:T(8,128)(2,1)S(1)} %get-tuple-element.197), channel_id=1, source_target_pairs={{0,16},{4,20},{8,24},{12,28},{16,0},{20,4},{24,8},{28,12},{1,17},{... | collective-permute-start | bytes 196616 | tf_op jit(solution)/shard_map/ppermute | solution.py:491
  153.5 8.9 %collective-permute-start.39 = (bf16[64,512]{1,0:T(8,128)(2,1)S(1)}, bf16[64,512]{1,0:T(8,128)(2,1)S(1)}, u32[]{:S(2)}, u32[]{:S(2)}) collective-permute-start(bf16[64,512]{1,0:T(8,128)(2,1)S(1)} %get-tuple-element.196), channel_id=1, source_target_pairs={{0,8},{4,12},{8,0},{12,4},{16,24},{20,28},{24,16},{28,20},{1,9},{5... | collective-permute-start | bytes 196616 | tf_op jit(solution)/shard_map/ppermute | solution.py:491
  160.0 11.8 %collective-permute-start.45 = (bf16[120,512]{1,0:T(8,128)(2,1)S(1)}, bf16[120,512]{1,0:T(8,128)(2,1)S(1)}, u32[]{:S(2)}, u32[]{:S(2)}) collective-permute-start(bf16[120,512]{1,0:T(8,128)(2,1)S(1)} %broadcast_select_fusion.14), channel_id=1, source_target_pairs={{0,16},{4,20},{8,24},{12,28},{16,0},{20,4},{24,8},{28,12},{1,17},{... | collective-permute-start | bytes 368648 | tf_op jit(solution)/shard_map/ppermute | solution.py:491
  160.1 12.0 %collective-permute-start.44 = (bf16[320,512]{1,0:T(8,128)(2,1)S(1)}, bf16[320,512]{1,0:T(8,128)(2,1)S(1)}, u32[]{:S(2)}, u32[]{:S(2)}) collective-permute-start(bf16[320,512]{1,0:T(8,128)(2,1)S(1)} %pad_maximum_fusion.6), channel_id=1, source_target_pairs={{0,4},{4,0},{8,12},{12,8},{16,20},{20,16},{24,28},{28,24},{1,5},{5... | collective-permute-start | bytes 983048 | tf_op jit(solution)/shard_map/ppermute | solution.py:491
  162.5 9.8 %collective-permute-start.41 = (bf16[64,512]{1,0:T(8,128)(2,1)S(1)}, bf16[64,512]{1,0:T(8,128)(2,1)S(1)}, u32[]{:S(2)}, u32[]{:S(2)}) collective-permute-start(bf16[64,512]{1,0:T(8,128)(2,1)S(1)} %add_convert_fusion.6), channel_id=1, source_target_pairs={{0,8},{4,12},{8,0},{12,4},{16,24},{20,28},{24,16},{28,20},{1,9},{5... | collective-permute-start | bytes 196616 | tf_op jit(solution)/shard_map/ppermute | solution.py:491
  164.3 9.0 %collective-permute-start.42 = (bf16[64,512]{1,0:T(8,128)(2,1)S(1)}, bf16[64,512]{1,0:T(8,128)(2,1)S(1)}, u32[]{:S(2)}, u32[]{:S(2)}) collective-permute-start(bf16[64,512]{1,0:T(8,128)(2,1)S(1)} %add_convert_fusion.6), channel_id=1, source_target_pairs={{0,16},{4,20},{8,24},{12,28},{16,0},{20,4},{24,8},{28,12},{1,17},{... | collective-permute-start | bytes 196616 | tf_op jit(solution)/shard_map/ppermute | solution.py:491
  165.4 7.9 %collective-permute-start.43 = (bf16[64,512]{1,0:T(8,128)(2,1)S(1)}, bf16[64,512]{1,0:T(8,128)(2,1)S(1)}, u32[]{:S(2)}, u32[]{:S(2)}) collective-permute-start(bf16[64,512]{1,0:T(8,128)(2,1)S(1)} %add_convert_fusion.6), channel_id=1, source_target_pairs={{0,24},{4,28},{8,16},{12,20},{16,8},{20,12},{24,0},{28,4},{1,25},{... | collective-permute-start | bytes 196616 | tf_op jit(solution)/shard_map/ppermute | solution.py:491
  171.9 6.0 %collective-permute-start.47 = (bf16[120,512]{1,0:T(8,128)(2,1)S(1)}, bf16[120,512]{1,0:T(8,128)(2,1)S(1)}, u32[]{:S(2)}, u32[]{:S(2)}) collective-permute-start(bf16[120,512]{1,0:T(8,128)(2,1)S(1)} %add_convert_fusion.5), channel_id=1, source_target_pairs={{0,16},{4,20},{8,24},{12,28},{16,0},{20,4},{24,8},{28,12},{1,17},{... | collective-permute-start | bytes 368648 | tf_op jit(solution)/shard_map/ppermute | solution.py:491
  178.0 9.0 %collective-permute-start.48 = (bf16[240,512]{1,0:T(8,128)(2,1)S(1)}, bf16[240,512]{1,0:T(8,128)(2,1)S(1)}, u32[]{:S(2)}, u32[]{:S(2)}) collective-permute-start(bf16[240,512]{1,0:T(8,128)(2,1)S(1)} %pad_maximum_fusion.7), channel_id=1, source_target_pairs={{0,8},{4,12},{8,0},{12,4},{16,24},{20,28},{24,16},{28,20},{1,9},{5... | collective-permute-start | bytes 737288 | tf_op jit(solution)/shard_map/ppermute | solution.py:491
  179.9 9.1 %collective-permute-start.46 = (bf16[256,512]{1,0:T(8,128)(2,1)S(1)}, bf16[256,512]{1,0:T(8,128)(2,1)S(1)}, u32[]{:S(2)}, u32[]{:S(2)}) collective-permute-start(bf16[256,512]{1,0:T(8,128)(2,1)S(1)} %constant_dynamic-update-slice_fusion.8.refs_1_), channel_id=1, source_target_pairs={{0,4},{4,0},{8,12},{12,8},{16,20},{20,16},{24,28},{28,24},{1,5},{5... | collective-permute-start | bytes 786440 | tf_op jit(solution)/shard_map/ppermute | solution.py:491
  181.4 15.5 %collective-permute-start.50 = (bf16[640,512]{1,0:T(8,128)(2,1)S(1)}, bf16[640,512]{1,0:T(8,128)(2,1)S(1)}, u32[]{:S(2)}, u32[]{:S(2)}) collective-permute-start(bf16[640,512]{1,0:T(8,128)(2,1)S(1)} %pad_maximum_fusion.2.refs_1_), channel_id=1, source_target_pairs={{0,8},{4,12},{8,0},{12,4},{16,24},{20,28},{24,16},{28,20},{1,9},{5... | collective-permute-start | bytes 1966088 | tf_op jit(solution)/shard_map/ppermute | solution.py:491
  187.1 11.4 %collective-permute-start.49 = (bf16[480,512]{1,0:T(8,128)(2,1)S(1)}, bf16[480,512]{1,0:T(8,128)(2,1)S(1)}, u32[]{:S(2)}, u32[]{:S(2)}) collective-permute-start(bf16[480,512]{1,0:T(8,128)(2,1)S(1)} %pad_maximum_fusion.3.refs_1_), channel_id=1, source_target_pairs={{0,4},{4,0},{8,12},{12,8},{16,20},{20,16},{24,28},{28,24},{1,5},{5... | collective-permute-start | bytes 1474568 | tf_op jit(solution)/shard_map/ppermute | solution.py:491
  (73 other events, 322.5 us)
